TPU v7x, 32 devices: a whole 2x2x4 slice. The times are simulated.
32 devices in a mesh: groups: 2 (over x), row: 16 (over z, y, core).
Axes of the slice: x: 2, y: 2, z: 4, core: 2. Of those that a mesh axis runs over, the one named last changes fastest.
Arguments:
- tokens: bfloat16 [32, 64, 1024], P(('groups', 'row')), parts along dimension 0, may hold values from -6 to 6
- gate_weight: bfloat16 [16, 1024, 2048], P('row'), may hold values from -0.09375 to 0.09375
- up_weight: bfloat16 [16, 1024, 2048], P('row'), may hold values from -0.09375 to 0.09375
- down_weight: bfloat16 [16, 2048, 1024], P('row'), may hold values from -0.0625 to 0.0625
- cotangent: bfloat16 [32, 64, 1024], P(('groups', 'row')), parts along dimension 0, may hold values from -6 to 6
Outputs:
- mixed: bfloat16 [32, 64, 1024], P(('groups', 'row')), parts along dimension 0
- input_grad: bfloat16 [32, 64, 1024], P(('groups', 'row')), parts along dimension 0
- gate_grad: float32 [32, 1024, 2048], P(('groups', 'row')), parts along dimension 0
- up_grad: float32 [32, 1024, 2048], P(('groups', 'row')), parts along dimension 0
- down_grad: float32 [32, 2048, 1024], P(('groups', 'row')), parts along dimension 0
There are 2 independent parts, one for each index of `groups`. A program takes and returns all parts, laid end to end along the dimension named above; an argument that names none is the same for every part. Nothing has to cross between parts.
All inputs are finite; a program needn't handle non-finite values.
Results may differ from a plain program's by a relative error of at most 0.005.
Values may be sent and summed in bfloat16 or wider, within the bound.
No kernel may reach another device: no remote copies, remote signals or barrier semaphores. Data moves between devices by JAX's collectives and lax.ppermute only.
A program may use at most 128 MiB of HBM per device.

v0:
```python
import math

import jax
import jax.numpy as jnp
from jax import lax
from jax.sharding import PartitionSpec as P


def partner_2(block, axis, apart):
    count = lax.axis_size(axis)
    route = []
    for low in range(count):
        high = low | 1 << apart
        if high != low and high < count:
            route += [(low, high), (high, low)]
    return lax.ppermute(block, axis, route)


def contract_rows(left, right):
    return lax.dot_general(
        left, right, (((0,), (0,)), ((), ())), preferred_element_type=jnp.float32
    )


def contract_cols(left, right):
    return lax.dot_general(
        left, right, (((1,), (1,)), ((), ())), preferred_element_type=jnp.float32
    )


def halves(values, dim):
    size = values.shape[dim] // 2
    return (
        lax.slice_in_dim(values, 0, size, axis=dim),
        lax.slice_in_dim(values, size, 2 * size, axis=dim),
    )


def bit_set(position, level):
    return position // 2**level % 2 == 1


def gather_across(values, dim, position, levels):
    for level in range(levels):
        partner = partner_2(values, "row", level)
        values = jnp.where(
            bit_set(position, level),
            jnp.concatenate([partner, values], dim),
            jnp.concatenate([values, partner], dim),
        )
    return values


def sum_across(values, dim, position, levels):
    for level in reversed(range(levels)):
        lower, upper = halves(values, dim)
        is_upper = bit_set(position, level)
        outgoing = jnp.where(is_upper, lower, upper)
        kept = jnp.where(is_upper, upper, lower)
        values = kept + partner_2(outgoing, "row", level)
    return values


def total_down(values, levels):
    for level in range(levels):
        values = values + partner_2(values, "row", levels + level)
    return values


def body(tokens, gate_weight, up_weight, down_weight, cotangent):
    side = math.isqrt(lax.axis_size("row"))
    levels = side.bit_length() - 1
    place = lax.axis_index("row")
    across = place % side
    w_gate = gate_weight[0]
    w_up = up_weight[0]
    w_down = down_weight[0]
    gathered = gather_across(jnp.stack([tokens[0], cotangent[0]]), 1, across, levels)
    inputs = gathered[0]
    outgrad = gathered[1]
    partial_value = jnp.stack(
        [
            jnp.dot(inputs, w_gate, preferred_element_type=jnp.float32),
            jnp.dot(inputs, w_up, preferred_element_type=jnp.float32),
        ]
    )
    grad_partial = contract_cols(outgrad, w_down)
    summed = total_down(partial_value, levels)
    gate = summed[0]
    up = summed[1]
    sigma = jax.nn.sigmoid(gate)
    activated = gate * sigma
    hidden_all = (activated * up).astype(jnp.bfloat16)
    hidden_grad = total_down(grad_partial, levels)
    gate_delta = (hidden_grad * up * sigma * (1.0 + gate * (1.0 - sigma))).astype(jnp.bfloat16)
    up_delta = (hidden_grad * activated).astype(jnp.bfloat16)
    deltas_all = jnp.stack([gate_delta, up_delta])
    out_partial = jnp.dot(hidden_all, w_down, preferred_element_type=jnp.float32)
    mixed = sum_across(out_partial, 0, across, levels).astype(jnp.bfloat16)
    down_grad = contract_rows(hidden_all, outgrad)
    gate_grad = contract_rows(inputs, deltas_all[0])
    up_grad = contract_rows(inputs, deltas_all[1])
    in_partial = contract_cols(deltas_all[0], w_gate) + contract_cols(deltas_all[1], w_up)
    input_grad = sum_across(in_partial, 0, across, levels).astype(jnp.bfloat16)
    return (mixed[None], input_grad[None], gate_grad[None], up_grad[None], down_grad[None])


def solution(mesh):
    in_specs = (
        P(("groups", "row"), None, None),
        P("row", None, None),
        P("row", None, None),
        P("row", None, None),
        P(("groups", "row"), None, None),
    )
    out_specs = (
        P(("groups", "row"), None, None),
        P(("groups", "row"), None, None),
        P(("groups", "row"), None, None),
        P(("groups", "row"), None, None),
        P(("groups", "row"), None, None),
    )
    return jax.shard_map(body, mesh=mesh, in_specs=in_specs, out_specs=out_specs, check_vma=False)
```

profile of v0, /device:TPU:0, one launch (start us, length us, event | category | flops | bytes accessed | tf_op | source)
XLA Modules:
  0.0 426.0 jit_solution(14457903455920228299)
XLA Ops:
  3.0 1.2 collective-permute-done
  4.3 3.0 collective-permute-start.1
  7.2 12.2 %collective-permute-done.1 = bf16[2,128,1024]{2,1,0:T(8,128)(2,1)S(1)} collective-permute-done((bf16[2,128,1024]{2,1,0:T(8,128)(2,1)S(1)}, bf16[2,128,1024]{2,1,0:T(8,128)(2,1)S(1)}, u32[]{:S(2)}, u32[]{:S(2)}) %collective-permute-start.1) | collective-permute-done | bytes 524320 | tf_op jit(solution)/shard_map/ppermute | solution.py:16
  19.9 3.5 fusion.12
  23.4 1.3 fusion.15
  25.2 1.9 collective-permute-start.2
  27.1 90.3 %collective-permute-done.2 = f32[2,256,2048]{2,1,0:T(8,128)S(1)} collective-permute-done((f32[2,256,2048]{2,1,0:T(8,128)S(1)}, f32[2,256,2048]{2,1,0:T(8,128)S(1)}, u32[]{:S(2)}, u32[]{:S(2)}) %collective-permute-start.2) | collective-permute-done | bytes 4194336 | tf_op jit(solution)/shard_map/ppermute | solution.py:16
  118.1 2.6 collective-permute-start.3
  120.7 1.3 fusion
  122.0 1.6 collective-permute-start.6
  123.6 130.4 %collective-permute-done.6 = f32[256,2048]{1,0:T(8,128)S(1)} collective-permute-done((f32[256,2048]{1,0:T(8,128)S(1)}, f32[256,2048]{1,0:T(8,128)S(1)}, u32[]{:S(2)}, u32[]{:S(2)}) %collective-permute-start.6) | collective-permute-done | bytes 2097184 | tf_op jit(solution)/shard_map/ppermute | solution.py:16
  254.3 2.4 collective-permute-start.7
  256.8 89.1 %collective-permute-done.3 = f32[2,256,2048]{2,1,0:T(8,128)S(1)} collective-permute-done((f32[2,256,2048]{2,1,0:T(8,128)S(1)}, f32[2,256,2048]{2,1,0:T(8,128)S(1)}, u32[]{:S(2)}, u32[]{:S(2)}) %collective-permute-start.3) | collective-permute-done | bytes 4194336 | tf_op jit(solution)/shard_map/ppermute | solution.py:16
  345.9 1.7 fusion.37
  348.2 41.8 %collective-permute-done.7 = f32[256,2048]{1,0:T(8,128)S(1)} collective-permute-done((f32[256,2048]{1,0:T(8,128)S(1)}, f32[256,2048]{1,0:T(8,128)S(1)}, u32[]{:S(2)}, u32[]{:S(2)}) %collective-permute-start.7) | collective-permute-done | bytes 2097184 | tf_op jit(solution)/shard_map/ppermute | solution.py:16
  390.1 1.5 fusion.25
  391.6 1.3 fusion.4
  393.8 1.3 fusion.32
  396.3 1.5 fusion.2
  398.8 4.7 %convolution_bitcast_fusion.1 = f32[1,1024,2048]{2,1,0:T(8,128)} fusion(bf16[256,2048]{1,0:T(8,128)(2,1)S(1)} %get-tuple-element.5, bf16[2,256,1024]{2,1,0:T(8,128)(2,1)S(1)} %maximum_select_fusion), kind=kOutput, calls=%fused_computation.1 | convolution fusion | flops 1073741824 | bytes 9961472 | tf_op jit(solution)/shard_map/dot_general | solution.py:20
  403.5 4.7 %convolution_bitcast_fusion.2 = f32[1,1024,2048]{2,1,0:T(8,128)} fusion(bf16[256,2048]{1,0:T(8,128)(2,1)S(1)} %get-tuple-element.6, bf16[2,256,1024]{2,1,0:T(8,128)(2,1)S(1)} %maximum_select_fusion), kind=kOutput, calls=%fused_computation.2 | convolution fusion | flops 1073741824 | bytes 9961472 | tf_op jit(solution)/shard_map/dot_general | solution.py:20
  408.2 1.8 collective-permute-done.8
  410.3 9.4 %collective-permute-done.4 = f32[128,1024]{1,0:T(8,128)S(1)} collective-permute-done((f32[128,1024]{1,0:T(8,128)S(1)}, f32[128,1024]{1,0:T(8,128)S(1)}, u32[]{:S(2)}, u32[]{:S(2)}) %collective-permute-start.4) | collective-permute-done | bytes 524320 | tf_op jit(solution)/shard_map/ppermute | solution.py:16
  419.9 4.7 %convolution_bitcast_fusion = f32[1,2048,1024]{2,1,0:T(8,128)} fusion(bf16[1,256,2048]{2,1,0:T(8,128)(2,1)S(1)} %multiply_convert_fusion, bf16[2,256,1024]{2,1,0:T(8,128)(2,1)S(1)} %maximum_select_fusion), kind=kOutput, calls=%fused_computation | convolution fusion | flops 1073741824 | bytes 9961472 | tf_op jit(solution)/shard_map/dot_general | solution.py:20
  (33 shorter events, 10.1 us)
Async XLA Ops:
  2.5 1.7 collective-permute-start
  4.3 15.2 %collective-permute-start.1 = (bf16[2,128,1024]{2,1,0:T(8,128)(2,1)S(1)}, bf16[2,128,1024]{2,1,0:T(8,128)(2,1)S(1)}, u32[]{:S(2)}, u32[]{:S(2)}) collective-permute-start(bf16[2,128,1024]{2,1,0:T(8,128)(2,1)S(1)} %maximum_select_fusion.1), channel_id=1, source_target_pairs={{0,2},{2,0},{1,3},{3,1},{4,6},{6,4},{5,7},{7,5},{8,10},{10,8},{9,1... | collective-permute-start | bytes 1572872 | tf_op jit(solution)/shard_map/ppermute | solution.py:16
  7.2 16.2 %copy-start = (bf16[1,1024,2048]{2,1,0:T(8,128)(2,1)S(1)}, bf16[1,1024,2048]{2,1,0:T(8,128)(2,1)}, u32[]{:S(2)}) copy-start(bf16[1,1024,2048]{2,1,0:T(8,128)(2,1)} %param.7) | copy-start | bytes 12582916
  25.2 95.5 %copy-start.3 = (bf16[1,2048,1024]{2,1,0:T(8,128)(2,1)S(1)}, bf16[1,2048,1024]{2,1,0:T(8,128)(2,1)}, u32[]{:S(2)}) copy-start(bf16[1,2048,1024]{2,1,0:T(8,128)(2,1)} %param.8) | copy-start | bytes 12582916
  25.2 92.2 %collective-permute-start.2 = (f32[2,256,2048]{2,1,0:T(8,128)S(1)}, f32[2,256,2048]{2,1,0:T(8,128)S(1)}, u32[]{:S(2)}, u32[]{:S(2)}) collective-permute-start(f32[2,256,2048]{2,1,0:T(8,128)S(1)} %pad_maximum_fusion), channel_id=1, source_target_pairs={{0,4},{4,0},{1,5},{5,1},{2,6},{6,2},{3,7},{7,3},{8,12},{12,8},{9,1... | collective-permute-start | bytes 12582920 | tf_op jit(solution)/shard_map/ppermute | solution.py:16
  118.1 227.7 %collective-permute-start.3 = (f32[2,256,2048]{2,1,0:T(8,128)S(1)}, f32[2,256,2048]{2,1,0:T(8,128)S(1)}, u32[]{:S(2)}, u32[]{:S(2)}) collective-permute-start(f32[2,256,2048]{2,1,0:T(8,128)S(1)} %fusion.31), channel_id=1, source_target_pairs={{0,8},{8,0},{1,9},{9,1},{2,10},{10,2},{3,11},{11,3},{4,12},{12,4},... | collective-permute-start | bytes 12582920 | tf_op jit(solution)/shard_map/ppermute | solution.py:16
  122.0 132.1 %collective-permute-start.6 = (f32[256,2048]{1,0:T(8,128)S(1)}, f32[256,2048]{1,0:T(8,128)S(1)}, u32[]{:S(2)}, u32[]{:S(2)}) collective-permute-start(f32[256,2048]{1,0:T(8,128)S(1)} %fusion), channel_id=1, source_target_pairs={{0,4},{4,0},{1,5},{5,1},{2,6},{6,2},{3,7},{7,3},{8,12},{12,8},{9,1... | collective-permute-start | bytes 6291464 | tf_op jit(solution)/shard_map/ppermute | solution.py:16
  254.3 135.8 %collective-permute-start.7 = (f32[256,2048]{1,0:T(8,128)S(1)}, f32[256,2048]{1,0:T(8,128)S(1)}, u32[]{:S(2)}, u32[]{:S(2)}) collective-permute-start(f32[256,2048]{1,0:T(8,128)S(1)} %add.61), channel_id=1, source_target_pairs={{0,8},{8,0},{1,9},{9,1},{2,10},{10,2},{3,11},{11,3},{4,12},{12,4},... | collective-permute-start | bytes 6291464 | tf_op jit(solution)/shard_map/ppermute | solution.py:16
  348.2 43.4 %copy-start.1 = (bf16[1,1024,2048]{2,1,0:T(8,128)(2,1)S(1)}, bf16[1,1024,2048]{2,1,0:T(8,128)(2,1)}, u32[]{:S(2)}) copy-start(bf16[1,1024,2048]{2,1,0:T(8,128)(2,1)} %param.7) | copy-start | bytes 12582916
  391.6 2.2 copy-start.2
  393.8 2.5 copy-start.4
  395.1 14.9 %collective-permute-start.8 = (f32[128,1024]{1,0:T(8,128)S(1)}, f32[128,1024]{1,0:T(8,128)S(1)}, u32[]{:S(2)}, u32[]{:S(2)}) collective-permute-start(f32[128,1024]{1,0:T(8,128)S(1)} %slice_select_fusion), channel_id=1, source_target_pairs={{0,2},{2,0},{1,3},{3,1},{4,6},{6,4},{5,7},{7,5},{8,10},{10,8},{9,1... | collective-permute-start | bytes 1572872 | tf_op jit(solution)/shard_map/ppermute | solution.py:16
  397.8 21.8 %collective-permute-start.4 = (f32[128,1024]{1,0:T(8,128)S(1)}, f32[128,1024]{1,0:T(8,128)S(1)}, u32[]{:S(2)}, u32[]{:S(2)}) collective-permute-start(f32[128,1024]{1,0:T(8,128)S(1)} %slice_select_fusion.1), channel_id=1, source_target_pairs={{0,2},{2,0},{1,3},{3,1},{4,6},{6,4},{5,7},{7,5},{8,10},{10,8},{9,1... | collective-permute-start | bytes 1572872 | tf_op jit(solution)/shard_map/ppermute | solution.py:16
  410.2 14.4 %collective-permute-start.9 = (f32[64,1024]{1,0:T(8,128)S(1)}, f32[64,1024]{1,0:T(8,128)S(1)}, u32[]{:S(2)}, u32[]{:S(2)}) collective-permute-start(f32[64,1024]{1,0:T(8,128)S(1)} %slice_select_fusion.2), channel_id=1, source_target_pairs={{0,1},{1,0},{2,3},{3,2},{4,5},{5,4},{6,7},{7,6},{8,9},{9,8},{10,11... | collective-permute-start | bytes 786440 | tf_op jit(solution)/shard_map/ppermute | solution.py:16
  419.8 5.5 %collective-permute-start.5 = (f32[64,1024]{1,0:T(8,128)S(1)}, f32[64,1024]{1,0:T(8,128)S(1)}, u32[]{:S(2)}, u32[]{:S(2)}) collective-permute-start(f32[64,1024]{1,0:T(8,128)S(1)} %slice_select_fusion.3), channel_id=1, source_target_pairs={{0,1},{1,0},{2,3},{3,2},{4,5},{5,4},{6,7},{7,6},{8,9},{9,8},{10,11... | collective-permute-start | bytes 786440 | tf_op jit(solution)/shard_map/ppermute | solution.py:16
where the time goes:
time: 426 us
  waiting for transfers between devices  376 us (88%)
  matrix products  24.1 us (6%)
  starting transfers between devices  14.3 us (3%)
  other arithmetic  7.73 us (2%)
    ppermute x10, waiting for transfers between devices, partner_2(): return lax.ppermute(block, axis, route)  376 us
    ppermute x10, starting transfers between devices, partner_2(): return lax.ppermute(block, axis, route)  14.3 us
    dot_general x3, matrix products, contract_rows(): lax.dot_general(left, right, (((0,), (0,)), ((), ())), preferred_element_...  14.1 us
  transfers between devices with their start and end apart: 10, of which 8 were waited for; matrix products, arithmetic and copies ran while one was open for 5% of the time, Pallas kernels for 0%

commit v1 on v0

v1 whole, which is shorter than its diff:
```python
import math

import jax
import jax.numpy as jnp
from jax import lax
from jax.experimental import pallas as pl
from jax.experimental.pallas import tpu as pltpu
from jax.sharding import PartitionSpec as P

BF = jnp.bfloat16
F32 = jnp.float32
SLABS = 4
LAG = 3
VMEM = 16 * 2**20


def mm(left, right, ldim, rdim):
    return lax.dot_general(
        left, right, (((ldim,), (rdim,)), ((), ())), preferred_element_type=F32
    )


def params():
    return pltpu.CompilerParams(vmem_limit_bytes=VMEM)


def partial_kernel(x_ref, c_ref, wg_ref, wu_ref, wd_ref, *refs):
    p_ref, s_ref = refs[-2:]
    x = x_ref[...]
    for i, part in enumerate(
        (
            mm(x, wg_ref[...], 1, 0),
            mm(x, wu_ref[...], 1, 0),
            mm(c_ref[...], wd_ref[...], 1, 1),
        )
    ):
        p_ref[i] = part
        s_ref[i] = part.astype(s_ref.dtype)


def partials(x, c, w_gate, w_up, w_down, h, slab, wire, behind):
    m, feat = x.shape
    bn = min(256, slab)
    nb = slab // bn
    cols = pl.BlockSpec((feat, bn), lambda j: (0, h * nb + j))
    whole = pl.BlockSpec((m, feat), lambda j: (0, 0))
    out = pl.BlockSpec((3, m, bn), lambda j: (0, 0, j))
    return pl.pallas_call(
        partial_kernel,
        grid=(nb,),
        in_specs=[
            whole,
            whole,
            cols,
            cols,
            pl.BlockSpec((bn, feat), lambda j: (h * nb + j, 0)),
        ]
        + [pl.BlockSpec(memory_space=pl.ANY)] * len(behind),
        out_specs=[out, out],
        out_shape=[
            jax.ShapeDtypeStruct((3, m, slab), F32),
            jax.ShapeDtypeStruct((3, m, slab), wire),
        ],
        compiler_params=params(),
        cost_estimate=pl.CostEstimate(
            flops=6 * m * feat * slab,
            bytes_accessed=6 * feat * slab + 18 * m * slab,
            transcendentals=0,
        ),
        name="partials",
    )(x, c, w_gate, w_up, w_down, *behind)


def grads_kernel(n, xt_ref, c_ref, *refs):
    fulls = refs[:n]
    gate_ref, up_ref, down_ref, mark_ref = refs[-4:]
    mark_ref[...] = jnp.zeros_like(mark_ref)
    hidden, gate_delta, up_delta = [
        jnp.concatenate([f[i] for f in fulls], 0) for i in range(3)
    ]
    gate_ref[...] = mm(xt_ref[...], gate_delta, 1, 0)
    up_ref[...] = mm(xt_ref[...], up_delta, 1, 0)
    down_ref[...] = mm(hidden, c_ref[...], 0, 0)


def weight_grads(xt, c, fulls, h, hid, before):
    feat, tok = xt.shape
    slab = fulls[0].shape[2]
    rows = fulls[0].shape[1]
    bn = min(256, slab)
    nb = slab // bn
    n = len(fulls)
    cols = pl.BlockSpec((feat, bn), lambda j: (0, h * nb + j))
    return pl.pallas_call(
        lambda *refs: grads_kernel(n, *refs),
        grid=(nb,),
        in_specs=[
            pl.BlockSpec((feat, tok), lambda j: (0, 0)),
            pl.BlockSpec((tok, feat), lambda j: (0, 0)),
        ]
        + [pl.BlockSpec((3, rows, bn), lambda j: (0, 0, j))] * n
        + [pl.BlockSpec(memory_space=pl.ANY)] * len(before),
        out_specs=[
            cols,
            cols,
            pl.BlockSpec((bn, feat), lambda j: (h * nb + j, 0)),
            pl.BlockSpec((8, 128), lambda j: (0, 0)),
        ],
        out_shape=[
            jax.ShapeDtypeStruct((feat, hid), F32),
            jax.ShapeDtypeStruct((feat, hid), F32),
            jax.ShapeDtypeStruct((hid, feat), F32),
            jax.ShapeDtypeStruct((8, 128), F32),
        ],
        input_output_aliases={2 + n + i: i for i in range(len(before))},
        compiler_params=params(),
        cost_estimate=pl.CostEstimate(
            flops=6 * tok * feat * slab,
            bytes_accessed=12 * feat * slab,
            transcendentals=0,
        ),
        name="weight_grads",
    )(xt, c, *fulls, *before)


HERE = pl.BlockSpec(memory_space=pltpu.VMEM)
FLAG = pl.BlockSpec(memory_space=pltpu.SMEM)
REST = pl.BlockSpec(memory_space=pl.ANY)


def results_of(gate, up, hidden_grad):
    sigma = jax.nn.sigmoid(gate)
    activated = gate * sigma
    return (
        (activated * up).astype(BF),
        (hidden_grad * up * sigma * (1.0 + gate * (1.0 - sigma))).astype(BF),
        (hidden_grad * activated).astype(BF),
    )


def small(kernel, name, shapes, args, flags=(), behind=()):
    n = len(flags) + len(args)
    m = n + len(behind)
    size = sum(math.prod(a.shape) * a.dtype.itemsize for a in list(args) + list(shapes))
    return pl.pallas_call(
        lambda *refs: kernel(*refs[:n], *refs[m:]),
        in_specs=[FLAG] * len(flags) + [HERE] * len(args) + [REST] * len(behind),
        out_specs=[HERE] * len(shapes),
        out_shape=list(shapes),
        compiler_params=params(),
        cost_estimate=pl.CostEstimate(flops=size, bytes_accessed=size, transcendentals=0),
        name=name,
    )(*flags, *args, *behind)


def halve(came, part, start, rows, wire):
    def kernel(came_ref, part_ref, send_ref, keep_ref):
        keep_ref[...] = came_ref[:, :rows].astype(F32) + part_ref[:, start : start + rows]
        send_ref[...] = (
            came_ref[:, rows:].astype(F32) + part_ref[:, start + rows : start + 2 * rows]
        ).astype(wire)

    shape = (3, rows, came.shape[2])
    return small(
        kernel,
        "halve",
        [jax.ShapeDtypeStruct(shape, wire), jax.ShapeDtypeStruct(shape, F32)],
        [came, part],
    )


def finish(keep, half, behind):
    def kernel(keep_ref, half_ref, done_ref):
        own = [keep_ref[i] + half_ref[i].astype(F32) for i in range(3)]
        for i, values in enumerate(results_of(*own)):
            done_ref[i] = values

    return small(
        kernel, "finish", [jax.ShapeDtypeStruct(keep.shape, BF)], [keep, half], (), behind
    )[0]


def choose(is_end, at_end, start, done, half, behind):
    rows = done.shape[1]

    def kernel(flag_ref, end_ref, done_ref, half_ref, out_ref):
        @pl.when(flag_ref[0] == 1)
        def _():
            out_ref[...] = end_ref[:, start : start + 2 * rows]

        @pl.when(flag_ref[0] == 0)
        def _():
            out_ref[:, :rows] = done_ref[...]
            out_ref[:, rows:] = half_ref[...]

    shape = jax.ShapeDtypeStruct((3, 2 * rows, done.shape[2]), BF)
    return small(
        kernel, "choose", [shape], [at_end, done, half], [is_end], behind
    )[0]


def body(tokens, gate_weight, up_weight, down_weight, cotangent):
    count = lax.axis_size("row")
    side = math.isqrt(count)
    place = lax.axis_index("row")
    across = place % side
    down = place // side
    core = across % 2
    upper = (down >= side // 2).astype(jnp.int32)
    groups = side // 2
    mid = side // 2
    wire = BF if side <= 4 else F32

    w_gate = gate_weight[0]
    w_up = up_weight[0]
    w_down = down_weight[0]
    hid = w_gate.shape[1]
    rows = tokens.shape[1]
    slab = hid // SLABS

    def swap(values, bits):
        return lax.ppermute(values, "row", [(i, i ^ bits) for i in range(count)])

    def along(values, moves):
        route = [
            (src * side + i, dst * side + i) for src, dst in moves for i in range(side)
        ]
        return lax.ppermute(values, "row", route)

    def middle(values):
        route = []
        for d in range(side):
            for i in range(side):
                to = (side - 1 - d, i) if d in (mid - 1, mid) else (d, i ^ 1)
                route.append((d * side + i, to[0] * side + to[1]))
        return lax.ppermute(values, "row", route)

    first = core == upper

    def pair(own):
        other = swap(own, 1)
        return jnp.where(
            first, jnp.concatenate([own, other], 0), jnp.concatenate([other, own], 0)
        )

    x_own, c_own = pair(tokens[0]), pair(cotangent[0])
    order = [(0, 0), (0, 1)] + [(g, h) for h in (0, 1) for g in range(1, groups)]
    for h in range(2, SLABS):
        order += [(g, h) for g in reversed(range(groups))]
    sums, sends = {}, {}
    inputs = {0: (x_own, c_own)}

    def prepare(gs, h, *behind):
        x, c = inputs[gs[0]] if len(gs) == 1 else inputs["all"]
        p, s = partials(x, c, w_gate, w_up, w_down, h, slab, wire, behind)
        for n, g in enumerate(gs):
            sums[g, h], sends[g, h] = (p, 2 * rows * n), (s, 2 * rows * n)

    def rows_of(entry):
        values, start = entry
        return lax.slice_in_dim(values, start, start + 2 * rows, axis=1)

    prepare([0], 0)
    for g in range(1, groups):
        inputs[g] = swap(x_own, 2 * g), swap(c_own, 2 * g)
    x_all, c_all = [
        jnp.concatenate([inputs[g][i] for g in range(groups)], 0) for i in range(2)
    ]
    inputs["all"] = x_all, c_all
    xt_all = x_all.T

    fulls = {}
    outs = [None] * groups
    grads = ()
    marks = []

    def settle(g, h, full):
        nonlocal grads
        fulls[g, h] = full
        lo = h * slab
        wg = lax.slice_in_dim(w_gate, lo, lo + slab, axis=1)
        wu = lax.slice_in_dim(w_up, lo, lo + slab, axis=1)
        wd = lax.slice_in_dim(w_down, lo, lo + slab, axis=0)
        step = (mm(full[0], wd, 1, 0), mm(full[1], wg, 1, 1) + mm(full[2], wu, 1, 1))
        outs[g] = step if outs[g] is None else (outs[g][0] + step[0], outs[g][1] + step[1])
        marks.extend(outs[g])
        if all((i, h) in fulls for i in range(groups)):
            *grads, mark = weight_grads(
                xt_all, c_all, [fulls[i, h] for i in range(groups)], h, hid, grads
            )
            marks.append(mark)

    if mid == 2:
        pairs = [(d, d ^ 1) for d in range(side)]
        is_end = ((down == 0) | (down == side - 1)).astype(jnp.int32).reshape(1)
        steps = len(order)
        made = {1: [([0], 1)]}
        made[2] = [([g], h) for h in (0, 1) for g in range(1, groups)]
        for h in range(2, SLABS):
            made[3 + 2 * (h - 2)] = [(list(range(groups)), h)]
        arrived, results = {}, {}

        def depart(t, *behind):
            if t < LAG:
                load = rows_of(sends[order[t]])
            elif t < steps:
                load = choose(is_end, *sends[order[t]], *results[t - LAG], behind)
            else:
                load = choose(is_end, *sends[order[-1]], *results[t - LAG], behind)
            arrived[t] = along(load, pairs)
            return load

        depart(0)
        prepare([0], 1, sends[0, 0][0])
        load = depart(1)
        for t in range(steps + LAG):
            came = arrived[t]
            marks.clear()
            behind = []
            if t < steps:
                send, keep = halve(came, *sums[order[t]], rows, wire)
                half = middle(send)
                behind = [send]
            for gs, h in made.get(t + 2, ()):
                prepare(gs, h, *(behind or [came]))
                marks.append(sends[gs[0], h][0])
            if t >= LAG:
                settle(*order[t - LAG], choose(is_end, came, 0, *results[t - LAG], behind))
            if t + 2 < steps + LAG:
                load = depart(t + 2, *marks)
            if t < steps:
                done = finish(keep, half, [load])
                results[t] = done, middle(done)
    else:
        prepare([0], 1)
        for g in range(1, groups):
            for h in (0, 1):
                prepare([g], h)
        for h in range(2, SLABS):
            prepare(list(range(groups)), h)
        for g, h in order:
            total = rows_of(sums[g, h])
            for r in range(mid - 1):
                moves = [(r, r + 1), (side - 1 - r, side - 2 - r)]
                total = total + along(total.astype(wire), moves).astype(F32)
            half = middle(total[:, rows:].astype(wire))
            done = jnp.stack(results_of(*(total[:, :rows] + half.astype(F32))))
            full = jnp.concatenate([done, middle(done)], 1)
            for r in reversed(range(mid - 1)):
                came = along(full, [(r + 1, r), (side - 2 - r, side - 1 - r)])
                full = jnp.where((down == r) | (down == side - 1 - r), came, full)
            settle(g, h, full)

    def core_sum(values):
        lower, higher = values[:rows], values[rows:]
        keep = jnp.where(first, lower, higher)
        send = jnp.where(first, higher, lower)
        return keep + swap(send, 1)

    mixed_grad = []
    for i in range(2):
        result = None
        for g in reversed(range(groups)):
            summed = core_sum(outs[g][i])
            if g > 0:
                summed = swap(summed, 2 * g)
            result = summed if result is None else result + summed
        mixed_grad.append(result.astype(BF)[None])
    return tuple(mixed_grad) + tuple(g[None] for g in grads)


def solution(mesh):
    spec = P(("groups", "row"), None, None)
    weight = P("row", None, None)
    return jax.shard_map(
        body,
        mesh=mesh,
        in_specs=(spec, weight, weight, weight, spec),
        out_specs=(spec,) * 5,
        check_vma=False,
    )
```

time: 426 us -> 145 us (0.34)
  waiting for transfers between devices: 376 us -> 26.5 us
  starting transfers between devices: 14.3 us -> 47.4 us
  Pallas kernels: 0 us -> 31.6 us
  local copies, waits for them, and re-layouts: 2.73 us -> 21.3 us
  matrix products: 24.1 us -> 11.5 us
    ppermute x10 -> x37, waiting for transfers between devices: 376 us -> 26.5 us  [the longest x11 14.9 us: along(): return lax.ppermute(values, 'row', route)]
    ppermute x10 -> x37, starting transfers between devices: 14.3 us -> 47.4 us  [the longest x11 37.8 us: along(): return lax.ppermute(values, 'row', route)]
    pallas_call x0 -> x42, Pallas kernels: none -> 31.6 us  [the longest x4 12.8 us: weight_grads(): pl.pallas_call(lambda *refs: grads_kernel(n, *refs), grid=(nb,), in_specs...]
    unnamed x11 -> x52, local copies, waits for them, and re-layouts: 1.81 us -> 20.1 us
    dot_general x9 -> x24, matrix products: 24.1 us -> 11.5 us  [mm(): lax.dot_general(left, right, (((ldim,), (rdim,)), ((), ())), preferred_el...]
  transfers between devices with their start and end apart: 10 -> 37, of which waited for: 8 -> 9; matrix products, arithmetic and copies ran while one was open for 5% -> 11% of each run, Pallas kernels for 0% -> 21%
where the time goes in v1:
time: 145 us
  starting transfers between devices  47.4 us (33%)
  Pallas kernels  31.6 us (22%)
  waiting for transfers between devices  26.5 us (18%)
  local copies, waits for them, and re-layouts  21.3 us (15%)
  matrix products  11.5 us (8%)
  other arithmetic  4.72 us (3%)
  between operations  1.53 us (1%)
    ppermute x11, starting transfers between devices, along(): return lax.ppermute(values, 'row', route)  37.8 us
    unnamed x52, local copies, waits for them, and re-layouts  20.1 us
    ppermute x11, waiting for transfers between devices, along(): return lax.ppermute(values, 'row', route)  14.9 us
    pallas_call x4, Pallas kernels, weight_grads(): pl.pallas_call(lambda *refs: grads_kernel(n, *refs), grid=(nb,), in_specs...  12.8 us
    ppermute x10, waiting for transfers between devices, swap(): return lax.ppermute(values, 'row', [(i, i ^ bits) for i in range(count)])  11.6 us
    dot_general x24, matrix products, mm(): lax.dot_general(left, right, (((ldim,), (rdim,)), ((), ())), preferred_el...  11.5 us
    pallas_call x6, Pallas kernels, partials(): pl.pallas_call(partial_kernel, grid=(nb,), in_specs=[whole, whole, cols,...  9.43 us
    pallas_call x32, Pallas kernels, small(): pl.pallas_call(lambda *refs: kernel(*refs[:n], *refs[m:]), in_specs=[FLAG...  9.39 us
  transfers between devices with their start and end apart: 37, of which 9 were waited for; matrix products, arithmetic and copies ran while one was open for 11% of the time, Pallas kernels for 21%

profile of v1, /device:TPU:0, one launch (start us, length us, event | category | flops | bytes accessed | tf_op | source)
XLA Modules:
  0.0 144.7 jit_solution(16369370581893757304)
XLA Ops:
  6.6 2.2 %copy-done.3 = bf16[1,1024,2048]{2,1,0:T(8,128)(2,1)S(1)} copy-done((bf16[1,1024,2048]{2,1,0:T(8,128)(2,1)S(1)}, bf16[1,1024,2048]{2,1,0:T(8,128)(2,1)}, u32[]{:S(2)}) %copy-start.3) | copy-done | bytes 4194328
  8.8 2.2 %copy-done.7 = bf16[1,2048,1024]{2,1,0:T(8,128)(2,1)S(1)} copy-done((bf16[1,2048,1024]{2,1,0:T(8,128)(2,1)S(1)}, bf16[1,2048,1024]{2,1,0:T(8,128)(2,1)}, u32[]{:S(2)}) %copy-start.7) | copy-done | bytes 4194328
  12.4 3.0 %collective-permute-start.5 = (bf16[3,128,512]{2,1,0:T(8,128)(2,1)S(1)}, bf16[3,128,512]{2,1,0:T(8,128)(2,1)S(1)}, u32[]{:S(2)}, u32[]{:S(2)}) collective-permute-start(bf16[3,128,512]{2,1,0:T(8,128)(2,1)S(1)} %get-tuple-element.48.refs_0_), channel_id=1, source_target_pairs={{0,4},{1,5},{2,6},{3,7},{4,0},{5,1},{6,2},{7,3},{8,12},{9,13},{10,... | collective-permute-start | bytes 1179656 | tf_op jit(solution)/shard_map/ppermute | solution.py:228
  19.5 5.8 %collective-permute-done.5.refs_0_ = bf16[3,128,512]{2,1,0:T(8,128)(2,1)S(1)} collective-permute-done((bf16[3,128,512]{2,1,0:T(8,128)(2,1)S(1)}, bf16[3,128,512]{2,1,0:T(8,128)(2,1)S(1)}, u32[]{:S(2)}, u32[]{:S(2)}) %collective-permute-start.5) | collective-permute-done | bytes 393248 | tf_op jit(solution)/shard_map/ppermute | solution.py:228
  26.4 2.7 %collective-permute-done.3.c_ref = bf16[128,1024]{1,0:T(8,128)(2,1)S(1)} collective-permute-done((bf16[128,1024]{1,0:T(8,128)(2,1)S(1)}, bf16[128,1024]{1,0:T(8,128)(2,1)S(1)}, u32[]{:S(2)}, u32[]{:S(2)}) %collective-permute-start.3) | collective-permute-done | bytes 262176 | tf_op jit(solution)/shard_map/ppermute | solution.py:222
  29.1 2.2 %copy-done.1 = bf16[1,1024,2048]{2,1,0:T(8,128)(2,1)S(1)} copy-done((bf16[1,1024,2048]{2,1,0:T(8,128)(2,1)S(1)}, bf16[1,1024,2048]{2,1,0:T(8,128)(2,1)}, u32[]{:S(2)}) %copy-start.1) | copy-done | bytes 4194328
  31.3 2.2 %copy-done.4 = bf16[1,1024,2048]{2,1,0:T(8,128)(2,1)S(1)} copy-done((bf16[1,1024,2048]{2,1,0:T(8,128)(2,1)S(1)}, bf16[1,1024,2048]{2,1,0:T(8,128)(2,1)}, u32[]{:S(2)}) %copy-start.4) | copy-done | bytes 4194328
  33.5 2.2 %copy-done.8 = bf16[1,2048,1024]{2,1,0:T(8,128)(2,1)S(1)} copy-done((bf16[1,2048,1024]{2,1,0:T(8,128)(2,1)S(1)}, bf16[1,2048,1024]{2,1,0:T(8,128)(2,1)}, u32[]{:S(2)}) %copy-start.8) | copy-done | bytes 4194328
  43.1 4.8 %collective-permute-start.13 = (bf16[3,128,512]{2,1,0:T(8,128)(2,1)}, bf16[3,128,512]{2,1,0:T(8,128)(2,1)}, u32[]{:S(2)}, u32[]{:S(2)}) collective-permute-start(bf16[3,128,512]{2,1,0:T(8,128)(2,1)} %choose.16.refs_2_), channel_id=1, source_target_pairs={{0,4},{1,5},{2,6},{3,7},{4,0},{5,1},{6,2},{7,3},{8,12},{9,13},{10,... | collective-permute-start | bytes 1179656 | tf_op jit(solution)/shard_map/ppermute | solution.py:228
  53.3 5.9 %collective-permute-start.17 = (bf16[3,128,512]{2,1,0:T(8,128)(2,1)S(1)}, bf16[3,128,512]{2,1,0:T(8,128)(2,1)S(1)}, u32[]{:S(2)}, u32[]{:S(2)}) collective-permute-start(bf16[3,128,512]{2,1,0:T(8,128)(2,1)S(1)} %choose.17.refs_2_), channel_id=1, source_target_pairs={{0,4},{1,5},{2,6},{3,7},{4,0},{5,1},{6,2},{7,3},{8,12},{9,13},{10,... | collective-permute-start | bytes 1179656 | tf_op jit(solution)/shard_map/ppermute | solution.py:228
  69.2 2.2 %copy-done.9 = bf16[1,2048,1024]{2,1,0:T(8,128)(2,1)S(1)} copy-done((bf16[1,2048,1024]{2,1,0:T(8,128)(2,1)S(1)}, bf16[1,2048,1024]{2,1,0:T(8,128)(2,1)}, u32[]{:S(2)}) %copy-start.9) | copy-done | bytes 4194328
  73.4 2.9 %collective-permute-start.14 = (bf16[3,128,512]{2,1,0:T(8,128)(2,1)S(1)}, bf16[3,128,512]{2,1,0:T(8,128)(2,1)S(1)}, u32[]{:S(2)}, u32[]{:S(2)}) collective-permute-start(bf16[3,128,512]{2,1,0:T(8,128)(2,1)S(1)} %choose.19.refs_2_), channel_id=1, source_target_pairs={{0,4},{1,5},{2,6},{3,7},{4,0},{5,1},{6,2},{7,3},{8,12},{9,13},{10,... | collective-permute-start | bytes 1179656 | tf_op jit(solution)/shard_map/ppermute | solution.py:228
  79.6 4.9 %collective-permute-start.18 = (bf16[3,128,512]{2,1,0:T(8,128)(2,1)S(1)}, bf16[3,128,512]{2,1,0:T(8,128)(2,1)S(1)}, u32[]{:S(2)}, u32[]{:S(2)}) collective-permute-start(bf16[3,128,512]{2,1,0:T(8,128)(2,1)S(1)} %choose.22.refs_2_), channel_id=1, source_target_pairs={{0,4},{1,5},{2,6},{3,7},{4,0},{5,1},{6,2},{7,3},{8,12},{9,13},{10,... | collective-permute-start | bytes 1179656 | tf_op jit(solution)/shard_map/ppermute | solution.py:228
  87.5 3.2 %weight_grads.4 = (f32[1024,2048]{1,0:T(8,128)}, f32[1024,2048]{1,0:T(8,128)}, f32[2048,1024]{1,0:T(8,128)}, f32[8,128]{1,0:T(8,128)S(1)}) custom-call(bf16[1024,256]{1,0:T(8,128)(2,1)S(1)} %copy.19.refs_0_, bf16[256,1024]{1,0:T(8,128)(2,1)S(1)} %pad_maximum_fusion.1.c_ref.refs_1_, bf16[3,128,512]{2,1,0:T(8,128)(2,1)S(1)} %choose.18.refs_2_, ...), custom_call_target="tpu_custom_call" | custom-call | flops 805306368 | bytes 6291456 | tf_op jit(solution)/shard_map/weight_grads/pallas_call | solution.py:94
  91.1 2.5 %collective-permute-start.21 = (bf16[3,128,512]{2,1,0:T(8,128)(2,1)S(1)}, bf16[3,128,512]{2,1,0:T(8,128)(2,1)S(1)}, u32[]{:S(2)}, u32[]{:S(2)}) collective-permute-start(bf16[3,128,512]{2,1,0:T(8,128)(2,1)S(1)} %choose.24.refs_2_), channel_id=1, source_target_pairs={{0,4},{1,5},{2,6},{3,7},{4,0},{5,1},{6,2},{7,3},{8,12},{9,13},{10,... | collective-permute-start | bytes 1179656 | tf_op jit(solution)/shard_map/ppermute | solution.py:228
  95.6 3.2 %weight_grads.5 = (f32[1024,2048]{1,0:T(8,128)}, f32[1024,2048]{1,0:T(8,128)}, f32[2048,1024]{1,0:T(8,128)}, f32[8,128]{1,0:T(8,128)S(1)}) custom-call(bf16[1024,256]{1,0:T(8,128)(2,1)S(1)} %copy.19.refs_0_, bf16[256,1024]{1,0:T(8,128)(2,1)S(1)} %pad_maximum_fusion.1.c_ref.refs_1_, ...), custom_call_target="tpu_custom_call", output_to_operand_aliasing={{0}: (4, {}), {1}: (5, {}), {2}: (6, {})} | custom-call | flops 805306368 | bytes 6291456 | tf_op jit(solution)/shard_map/weight_grads/pallas_call | solution.py:94
  99.2 3.6 %collective-permute-start.29 = (bf16[3,128,512]{2,1,0:T(8,128)(2,1)S(1)}, bf16[3,128,512]{2,1,0:T(8,128)(2,1)S(1)}, u32[]{:S(2)}, u32[]{:S(2)}) collective-permute-start(bf16[3,128,512]{2,1,0:T(8,128)(2,1)S(1)} %choose.26.refs_2_), channel_id=1, source_target_pairs={{0,4},{1,5},{2,6},{3,7},{4,0},{5,1},{6,2},{7,3},{8,12},{9,13},{10,... | collective-permute-start | bytes 1179656 | tf_op jit(solution)/shard_map/ppermute | solution.py:228
  105.1 5.9 %collective-permute-start.26 = (bf16[3,128,512]{2,1,0:T(8,128)(2,1)S(1)}, bf16[3,128,512]{2,1,0:T(8,128)(2,1)S(1)}, u32[]{:S(2)}, u32[]{:S(2)}) collective-permute-start(bf16[3,128,512]{2,1,0:T(8,128)(2,1)S(1)} %choose.27.refs_2_), channel_id=1, source_target_pairs={{0,4},{1,5},{2,6},{3,7},{4,0},{5,1},{6,2},{7,3},{8,12},{9,13},{10,... | collective-permute-start | bytes 1179656 | tf_op jit(solution)/shard_map/ppermute | solution.py:228
  113.9 3.2 %weight_grads.6 = (f32[1024,2048]{1,0:T(8,128)}, f32[1024,2048]{1,0:T(8,128)}, f32[2048,1024]{1,0:T(8,128)}, f32[8,128]{1,0:T(8,128)S(1)}) custom-call(bf16[1024,256]{1,0:T(8,128)(2,1)S(1)} %copy.19.refs_0_, bf16[256,1024]{1,0:T(8,128)(2,1)S(1)} %pad_maximum_fusion.1.c_ref.refs_1_, ...), custom_call_target="tpu_custom_call", output_to_operand_aliasing={{0}: (4, {}), {1}: (5, {}), {2}: (6, {})} | custom-call | flops 805306368 | bytes 6291456 | tf_op jit(solution)/shard_map/weight_grads/pallas_call | solution.py:94
  117.5 3.1 %collective-permute-start.32 = (bf16[3,128,512]{2,1,0:T(8,128)(2,1)S(1)}, bf16[3,128,512]{2,1,0:T(8,128)(2,1)S(1)}, u32[]{:S(2)}, u32[]{:S(2)}) collective-permute-start(bf16[3,128,512]{2,1,0:T(8,128)(2,1)S(1)} %choose.30), channel_id=1, source_target_pairs={{0,4},{1,5},{2,6},{3,7},{4,0},{5,1},{6,2},{7,3},{8,12},{9,13},{10,... | collective-permute-start | bytes 1179656 | tf_op jit(solution)/shard_map/ppermute | solution.py:228
  122.6 5.3 %collective-permute-done.32.refs_1_ = bf16[3,128,512]{2,1,0:T(8,128)(2,1)S(1)} collective-permute-done((bf16[3,128,512]{2,1,0:T(8,128)(2,1)S(1)}, bf16[3,128,512]{2,1,0:T(8,128)(2,1)S(1)}, u32[]{:S(2)}, u32[]{:S(2)}) %collective-permute-start.32) | collective-permute-done | bytes 393248 | tf_op jit(solution)/shard_map/ppermute | solution.py:228
  132.3 3.2 %weight_grads.7 = (f32[1024,2048]{1,0:T(8,128)}, f32[1024,2048]{1,0:T(8,128)}, f32[2048,1024]{1,0:T(8,128)}, f32[8,128]{1,0:T(8,128)}) custom-call(bf16[1024,256]{1,0:T(8,128)(2,1)S(1)} %copy.19.refs_0_, bf16[256,1024]{1,0:T(8,128)(2,1)S(1)} %pad_maximum_fusion.1.c_ref.refs_1_, ...), custom_call_target="tpu_custom_call", output_to_operand_aliasing={{0}: (4, {}), {1}: (5, {}), {2}: (6, {})} | custom-call | flops 805306368 | bytes 6291456 | tf_op jit(solution)/shard_map/weight_grads/pallas_call | solution.py:94
  135.5 3.8 %collective-permute-done.28 = f32[64,1024]{1,0:T(8,128)S(1)} collective-permute-done((f32[64,1024]{1,0:T(8,128)S(1)}, f32[64,1024]{1,0:T(8,128)S(1)}, u32[]{:S(2)}, u32[]{:S(2)}) %collective-permute-start.28) | collective-permute-done | bytes 262176 | tf_op jit(solution)/shard_map/ppermute | solution.py:222
  140.0 4.0 %collective-permute-done.35 = f32[64,1024]{1,0:T(8,128)S(1)} collective-permute-done((f32[64,1024]{1,0:T(8,128)S(1)}, f32[64,1024]{1,0:T(8,128)S(1)}, u32[]{:S(2)}, u32[]{:S(2)}) %collective-permute-start.35) | collective-permute-done | bytes 262176 | tf_op jit(solution)/shard_map/ppermute | solution.py:222
  (181 shorter events, 59.1 us)
Async XLA Ops:
  12.4 12.9 %collective-permute-start.5 = (bf16[3,128,512]{2,1,0:T(8,128)(2,1)S(1)}, bf16[3,128,512]{2,1,0:T(8,128)(2,1)S(1)}, u32[]{:S(2)}, u32[]{:S(2)}) collective-permute-start(bf16[3,128,512]{2,1,0:T(8,128)(2,1)S(1)} %get-tuple-element.48.refs_0_), channel_id=1, source_target_pairs={{0,4},{1,5},{2,6},{3,7},{4,0},{5,1},{6,2},{7,3},{8,12},{9,13},{10,... | collective-permute-start | bytes 1179656 | tf_op jit(solution)/shard_map/ppermute | solution.py:228
  15.4 10.1 %collective-permute-start.1 = (bf16[128,1024]{1,0:T(8,128)(2,1)S(1)}, bf16[128,1024]{1,0:T(8,128)(2,1)S(1)}, u32[]{:S(2)}, u32[]{:S(2)}) collective-permute-start(bf16[128,1024]{1,0:T(8,128)(2,1)S(1)} %maximum_select_fusion.x_ref), channel_id=1, source_target_pairs={{0,2},{1,3},{2,0},{3,1},{4,6},{5,7},{6,4},{7,5},{8,10},{9,11},{10,... | collective-permute-start | bytes 786440 | tf_op jit(solution)/shard_map/ppermute | solution.py:222
  16.9 12.2 %collective-permute-start.3 = (bf16[128,1024]{1,0:T(8,128)(2,1)S(1)}, bf16[128,1024]{1,0:T(8,128)(2,1)S(1)}, u32[]{:S(2)}, u32[]{:S(2)}) collective-permute-start(bf16[128,1024]{1,0:T(8,128)(2,1)S(1)} %maximum_select_fusion.1.c_ref), channel_id=1, source_target_pairs={{0,2},{1,3},{2,0},{3,1},{4,6},{5,7},{6,4},{7,5},{8,10},{9,11},{10,... | collective-permute-start | bytes 786440 | tf_op jit(solution)/shard_map/ppermute | solution.py:222
  19.4 19.0 %collective-permute-start.4 = (bf16[3,128,512]{2,1,0:T(8,128)(2,1)}, bf16[3,128,512]{2,1,0:T(8,128)(2,1)S(1)}, u32[]{:S(2)}, u32[]{:S(2)}) collective-permute-start(bf16[3,128,512]{2,1,0:T(8,128)(2,1)} %get-tuple-element.49), channel_id=1, source_target_pairs={{0,4},{1,5},{2,6},{3,7},{4,0},{5,1},{6,2},{7,3},{8,12},{9,13},{10,... | collective-permute-start | bytes 1179656 | tf_op jit(solution)/shard_map/ppermute | solution.py:228
  25.4 12.8 %collective-permute-start.9 = (bf16[3,64,512]{2,1,0:T(8,128)(2,1)S(1)}, bf16[3,64,512]{2,1,0:T(8,128)(2,1)S(1)}, u32[]{:S(2)}, u32[]{:S(2)}) collective-permute-start(bf16[3,64,512]{2,1,0:T(8,128)(2,1)S(1)} %get-tuple-element.54.refs_0_), channel_id=1, source_target_pairs={{0,1},{1,0},{2,3},{3,2},{4,8},{5,9},{6,10},{7,11},{8,4},{9,5},{10,... | collective-permute-start | bytes 589832 | tf_op jit(solution)/shard_map/ppermute | solution.py:236
  37.0 11.7 %collective-permute-start.6 = (bf16[3,128,512]{2,1,0:T(8,128)(2,1)S(1)}, bf16[3,128,512]{2,1,0:T(8,128)(2,1)S(1)}, u32[]{:S(2)}, u32[]{:S(2)}) collective-permute-start(bf16[3,128,512]{2,1,0:T(8,128)(2,1)S(1)} %get-tuple-element.55.refs_2_), channel_id=1, source_target_pairs={{0,4},{1,5},{2,6},{3,7},{4,0},{5,1},{6,2},{7,3},{8,12},{9,13},{10,... | collective-permute-start | bytes 1179656 | tf_op jit(solution)/shard_map/ppermute | solution.py:228
  38.5 9.4 %collective-permute-start.8 = (bf16[3,64,512]{2,1,0:T(8,128)(2,1)S(1)}, bf16[3,64,512]{2,1,0:T(8,128)(2,1)S(1)}, u32[]{:S(2)}, u32[]{:S(2)}) collective-permute-start(bf16[3,64,512]{2,1,0:T(8,128)(2,1)S(1)} %get-tuple-element.51.refs_0_), channel_id=1, source_target_pairs={{0,1},{1,0},{2,3},{3,2},{4,8},{5,9},{6,10},{7,11},{8,4},{9,5},{10,... | collective-permute-start | bytes 589832 | tf_op jit(solution)/shard_map/ppermute | solution.py:236
  43.1 18.2 %collective-permute-start.13 = (bf16[3,128,512]{2,1,0:T(8,128)(2,1)}, bf16[3,128,512]{2,1,0:T(8,128)(2,1)}, u32[]{:S(2)}, u32[]{:S(2)}) collective-permute-start(bf16[3,128,512]{2,1,0:T(8,128)(2,1)} %choose.16.refs_2_), channel_id=1, source_target_pairs={{0,4},{1,5},{2,6},{3,7},{4,0},{5,1},{6,2},{7,3},{8,12},{9,13},{10,... | collective-permute-start | bytes 1179656 | tf_op jit(solution)/shard_map/ppermute | solution.py:228
  50.3 8.9 %collective-permute-start.7 = (bf16[3,64,512]{2,1,0:T(8,128)(2,1)}, bf16[3,64,512]{2,1,0:T(8,128)(2,1)}, u32[]{:S(2)}, u32[]{:S(2)}) collective-permute-start(bf16[3,64,512]{2,1,0:T(8,128)(2,1)} %get-tuple-element.58), channel_id=1, source_target_pairs={{0,1},{1,0},{2,3},{3,2},{4,8},{5,9},{6,10},{7,11},{8,4},{9,5},{10,... | collective-permute-start | bytes 589832 | tf_op jit(solution)/shard_map/ppermute | solution.py:236
  53.3 23.2 %collective-permute-start.17 = (bf16[3,128,512]{2,1,0:T(8,128)(2,1)S(1)}, bf16[3,128,512]{2,1,0:T(8,128)(2,1)S(1)}, u32[]{:S(2)}, u32[]{:S(2)}) collective-permute-start(bf16[3,128,512]{2,1,0:T(8,128)(2,1)S(1)} %choose.17.refs_2_), channel_id=1, source_target_pairs={{0,4},{1,5},{2,6},{3,7},{4,0},{5,1},{6,2},{7,3},{8,12},{9,13},{10,... | collective-permute-start | bytes 1179656 | tf_op jit(solution)/shard_map/ppermute | solution.py:228
  61.2 12.2 %collective-permute-start.12 = (bf16[3,64,512]{2,1,0:T(8,128)(2,1)S(1)}, bf16[3,64,512]{2,1,0:T(8,128)(2,1)S(1)}, u32[]{:S(2)}, u32[]{:S(2)}) collective-permute-start(bf16[3,64,512]{2,1,0:T(8,128)(2,1)S(1)} %finish.10.refs_2_), channel_id=1, source_target_pairs={{0,1},{1,0},{2,3},{3,2},{4,8},{5,9},{6,10},{7,11},{8,4},{9,5},{10,... | collective-permute-start | bytes 589832 | tf_op jit(solution)/shard_map/ppermute | solution.py:236
  63.5 12.8 %collective-permute-start.15 = (bf16[3,64,512]{2,1,0:T(8,128)(2,1)S(1)}, bf16[3,64,512]{2,1,0:T(8,128)(2,1)S(1)}, u32[]{:S(2)}, u32[]{:S(2)}) collective-permute-start(bf16[3,64,512]{2,1,0:T(8,128)(2,1)S(1)} %get-tuple-element.63.refs_0_.refs_4_), channel_id=1, source_target_pairs={{0,1},{1,0},{2,3},{3,2},{4,8},{5,9},{6,10},{7,11},{8,4},{9,5},{10,... | collective-permute-start | bytes 589832 | tf_op jit(solution)/shard_map/ppermute | solution.py:236
  73.4 12.9 %collective-permute-start.14 = (bf16[3,128,512]{2,1,0:T(8,128)(2,1)S(1)}, bf16[3,128,512]{2,1,0:T(8,128)(2,1)S(1)}, u32[]{:S(2)}, u32[]{:S(2)}) collective-permute-start(bf16[3,128,512]{2,1,0:T(8,128)(2,1)S(1)} %choose.19.refs_2_), channel_id=1, source_target_pairs={{0,4},{1,5},{2,6},{3,7},{4,0},{5,1},{6,2},{7,3},{8,12},{9,13},{10,... | collective-permute-start | bytes 1179656 | tf_op jit(solution)/shard_map/ppermute | solution.py:228
  79.6 14.2 %collective-permute-start.18 = (bf16[3,128,512]{2,1,0:T(8,128)(2,1)S(1)}, bf16[3,128,512]{2,1,0:T(8,128)(2,1)S(1)}, u32[]{:S(2)}, u32[]{:S(2)}) collective-permute-start(bf16[3,128,512]{2,1,0:T(8,128)(2,1)S(1)} %choose.22.refs_2_), channel_id=1, source_target_pairs={{0,4},{1,5},{2,6},{3,7},{4,0},{5,1},{6,2},{7,3},{8,12},{9,13},{10,... | collective-permute-start | bytes 1179656 | tf_op jit(solution)/shard_map/ppermute | solution.py:228
  91.1 12.3 %collective-permute-start.21 = (bf16[3,128,512]{2,1,0:T(8,128)(2,1)S(1)}, bf16[3,128,512]{2,1,0:T(8,128)(2,1)S(1)}, u32[]{:S(2)}, u32[]{:S(2)}) collective-permute-start(bf16[3,128,512]{2,1,0:T(8,128)(2,1)S(1)} %choose.24.refs_2_), channel_id=1, source_target_pairs={{0,4},{1,5},{2,6},{3,7},{4,0},{5,1},{6,2},{7,3},{8,12},{9,13},{10,... | collective-permute-start | bytes 1179656 | tf_op jit(solution)/shard_map/ppermute | solution.py:228
  93.9 8.9 %collective-permute-start.22 = (bf16[3,64,512]{2,1,0:T(8,128)(2,1)S(1)}, bf16[3,64,512]{2,1,0:T(8,128)(2,1)S(1)}, u32[]{:S(2)}, u32[]{:S(2)}) collective-permute-start(bf16[3,64,512]{2,1,0:T(8,128)(2,1)S(1)} %get-tuple-element.70.refs_4_), channel_id=1, source_target_pairs={{0,1},{1,0},{2,3},{3,2},{4,8},{5,9},{6,10},{7,11},{8,4},{9,5},{10,... | collective-permute-start | bytes 589832 | tf_op jit(solution)/shard_map/ppermute | solution.py:236
  99.2 13.6 %collective-permute-start.29 = (bf16[3,128,512]{2,1,0:T(8,128)(2,1)S(1)}, bf16[3,128,512]{2,1,0:T(8,128)(2,1)S(1)}, u32[]{:S(2)}, u32[]{:S(2)}) collective-permute-start(bf16[3,128,512]{2,1,0:T(8,128)(2,1)S(1)} %choose.26.refs_2_), channel_id=1, source_target_pairs={{0,4},{1,5},{2,6},{3,7},{4,0},{5,1},{6,2},{7,3},{8,12},{9,13},{10,... | collective-permute-start | bytes 1179656 | tf_op jit(solution)/shard_map/ppermute | solution.py:228
  105.1 15.5 %collective-permute-start.26 = (bf16[3,128,512]{2,1,0:T(8,128)(2,1)S(1)}, bf16[3,128,512]{2,1,0:T(8,128)(2,1)S(1)}, u32[]{:S(2)}, u32[]{:S(2)}) collective-permute-start(bf16[3,128,512]{2,1,0:T(8,128)(2,1)S(1)} %choose.27.refs_2_), channel_id=1, source_target_pairs={{0,4},{1,5},{2,6},{3,7},{4,0},{5,1},{6,2},{7,3},{8,12},{9,13},{10,... | collective-permute-start | bytes 1179656 | tf_op jit(solution)/shard_map/ppermute | solution.py:228
  117.5 10.5 %collective-permute-start.32 = (bf16[3,128,512]{2,1,0:T(8,128)(2,1)S(1)}, bf16[3,128,512]{2,1,0:T(8,128)(2,1)S(1)}, u32[]{:S(2)}, u32[]{:S(2)}) collective-permute-start(bf16[3,128,512]{2,1,0:T(8,128)(2,1)S(1)} %choose.30), channel_id=1, source_target_pairs={{0,4},{1,5},{2,6},{3,7},{4,0},{5,1},{6,2},{7,3},{8,12},{9,13},{10,... | collective-permute-start | bytes 1179656 | tf_op jit(solution)/shard_map/ppermute | solution.py:228
  121.5 8.5 %collective-permute-start.27 = (f32[64,1024]{1,0:T(8,128)S(1)}, f32[64,1024]{1,0:T(8,128)S(1)}, u32[]{:S(2)}, u32[]{:S(2)}) collective-permute-start(f32[64,1024]{1,0:T(8,128)S(1)} %slice_select_fusion.3), channel_id=1, source_target_pairs={{0,1},{1,0},{2,3},{3,2},{4,5},{5,4},{6,7},{7,6},{8,9},{9,8},{10,11... | collective-permute-start | bytes 786440 | tf_op jit(solution)/shard_map/ppermute | solution.py:222
  122.1 9.6 %collective-permute-start.34 = (f32[64,1024]{1,0:T(8,128)S(1)}, f32[64,1024]{1,0:T(8,128)S(1)}, u32[]{:S(2)}, u32[]{:S(2)}) collective-permute-start(f32[64,1024]{1,0:T(8,128)S(1)} %slice_select_fusion.1), channel_id=1, source_target_pairs={{0,1},{1,0},{2,3},{3,2},{4,5},{5,4},{6,7},{7,6},{8,9},{9,8},{10,11... | collective-permute-start | bytes 786440 | tf_op jit(solution)/shard_map/ppermute | solution.py:222
  129.4 10.6 %collective-permute-start.36 = (f32[64,1024]{1,0:T(8,128)S(1)}, f32[64,1024]{1,0:T(8,128)S(1)}, u32[]{:S(2)}, u32[]{:S(2)}) collective-permute-start(f32[64,1024]{1,0:T(8,128)S(1)} %slice_select_fusion), channel_id=1, source_target_pairs={{0,1},{1,0},{2,3},{3,2},{4,5},{5,4},{6,7},{7,6},{8,9},{9,8},{10,11... | collective-permute-start | bytes 786440 | tf_op jit(solution)/shard_map/ppermute | solution.py:222
  130.0 9.2 %collective-permute-start.28 = (f32[64,1024]{1,0:T(8,128)S(1)}, f32[64,1024]{1,0:T(8,128)S(1)}, u32[]{:S(2)}, u32[]{:S(2)}) collective-permute-start(f32[64,1024]{1,0:T(8,128)S(1)} %select_add_fusion.1), channel_id=1, source_target_pairs={{0,2},{1,3},{2,0},{3,1},{4,6},{5,7},{6,4},{7,5},{8,10},{9,11},{10,... | collective-permute-start | bytes 786440 | tf_op jit(solution)/shard_map/ppermute | solution.py:222
  131.7 12.2 %collective-permute-start.35 = (f32[64,1024]{1,0:T(8,128)S(1)}, f32[64,1024]{1,0:T(8,128)S(1)}, u32[]{:S(2)}, u32[]{:S(2)}) collective-permute-start(f32[64,1024]{1,0:T(8,128)S(1)} %select_add_fusion), channel_id=1, source_target_pairs={{0,2},{1,3},{2,0},{3,1},{4,6},{5,7},{6,4},{7,5},{8,10},{9,11},{10,... | collective-permute-start | bytes 786440 | tf_op jit(solution)/shard_map/ppermute | solution.py:222
  (39 other events, 198.9 us)

commit v2 on v1

--- a/solution.py
+++ b/solution.py
@@ -11,7 +11,7 @@
 F32 = jnp.float32
 SLABS = 4
 LAG = 3
-VMEM = 16 * 2**20
+MIB = 2**20
 
 
 def mm(left, right, ldim, rdim):
@@ -20,8 +20,8 @@
     )
 
 
-def params():
-    return pltpu.CompilerParams(vmem_limit_bytes=VMEM)
+def params(mib):
+    return pltpu.CompilerParams(vmem_limit_bytes=mib * MIB)
 
 
 def partial_kernel(x_ref, c_ref, wg_ref, wu_ref, wd_ref, *refs):
@@ -58,10 +58,10 @@
         + [pl.BlockSpec(memory_space=pl.ANY)] * len(behind),
         out_specs=[out, out],
         out_shape=[
-            jax.ShapeDtypeStruct((3, m, slab), F32),
-            jax.ShapeDtypeStruct((3, m, slab), wire),
+            in_vmem((3, m, slab), F32),
+            in_vmem((3, m, slab), wire),
         ],
-        compiler_params=params(),
+        compiler_params=params(14),
         cost_estimate=pl.CostEstimate(
             flops=6 * m * feat * slab,
             bytes_accessed=6 * feat * slab + 18 * m * slab,
@@ -113,7 +113,7 @@
             jax.ShapeDtypeStruct((8, 128), F32),
         ],
         input_output_aliases={2 + n + i: i for i in range(len(before))},
-        compiler_params=params(),
+        compiler_params=params(16),
         cost_estimate=pl.CostEstimate(
             flops=6 * tok * feat * slab,
             bytes_accessed=12 * feat * slab,
@@ -123,6 +123,14 @@
     )(xt, c, *fulls, *before)
 
 
+def in_hbm(values):
+    return pltpu.with_memory_space_constraint(values, pltpu.HBM)
+
+
+def in_vmem(shape, dtype):
+    return pltpu.VMEM(shape, dtype)
+
+
 HERE = pl.BlockSpec(memory_space=pltpu.VMEM)
 FLAG = pl.BlockSpec(memory_space=pltpu.SMEM)
 REST = pl.BlockSpec(memory_space=pl.ANY)
@@ -138,22 +146,22 @@
     )
 
 
-def small(kernel, name, shapes, args, flags=(), behind=()):
+def small(kernel, name, shapes, args, flags=(), behind=(), mib=4, spec=HERE):
     n = len(flags) + len(args)
     m = n + len(behind)
-    size = sum(math.prod(a.shape) * a.dtype.itemsize for a in list(args) + list(shapes))
+    size = sum(math.prod(a.shape) * 2 for a in list(args) + list(shapes))
     return pl.pallas_call(
         lambda *refs: kernel(*refs[:n], *refs[m:]),
-        in_specs=[FLAG] * len(flags) + [HERE] * len(args) + [REST] * len(behind),
+        in_specs=[FLAG] * len(flags) + [spec] * len(args) + [REST] * len(behind),
         out_specs=[HERE] * len(shapes),
         out_shape=list(shapes),
-        compiler_params=params(),
+        compiler_params=params(mib),
         cost_estimate=pl.CostEstimate(flops=size, bytes_accessed=size, transcendentals=0),
         name=name,
     )(*flags, *args, *behind)
 
 
-def halve(came, part, start, rows, wire):
+def halve(came, part, start, rows, wire, behind):
     def kernel(came_ref, part_ref, send_ref, keep_ref):
         keep_ref[...] = came_ref[:, :rows].astype(F32) + part_ref[:, start : start + rows]
         send_ref[...] = (
@@ -164,8 +172,10 @@
     return small(
         kernel,
         "halve",
-        [jax.ShapeDtypeStruct(shape, wire), jax.ShapeDtypeStruct(shape, F32)],
+        [in_vmem(shape, wire), in_vmem(shape, F32)],
         [came, part],
+        (),
+        behind,
     )
 
 
@@ -176,26 +186,107 @@
             done_ref[i] = values
 
     return small(
-        kernel, "finish", [jax.ShapeDtypeStruct(keep.shape, BF)], [keep, half], (), behind
+        kernel, "finish", [in_vmem(keep.shape, BF)], [keep, half], (), behind
     )[0]
 
 
-def choose(is_end, at_end, start, done, half, behind):
+def stage(blocks, behind=()):
+    n = len(blocks)
+    m = n + len(behind)
+
+    def kernel(*refs):
+        copies = [
+            pltpu.make_async_copy(refs[i], refs[m + i], refs[-1].at[i]) for i in range(n)
+        ]
+        for copy in copies:
+            copy.start()
+        for copy in copies:
+            copy.wait()
+
+    size = sum(math.prod(b.shape) * 2 for b in blocks)
+    return pl.pallas_call(
+        kernel,
+        in_specs=[REST] * m,
+        out_specs=[HERE] * n,
+        out_shape=[in_vmem(b.shape, b.dtype) for b in blocks],
+        scratch_shapes=[pltpu.SemaphoreType.DMA((n,))],
+        compiler_params=params(4),
+        cost_estimate=pl.CostEstimate(flops=size, bytes_accessed=size, transcendentals=0),
+        name="stage",
+    )(*[in_hbm(b) for b in blocks], *behind)
+
+
+def gather(pairs):
+    n = len(pairs)
+    rows, feat = pairs[0][0].shape
+
+    def kernel(*refs):
+        x_ref, c_ref, xt_ref = refs[2 * n :]
+        for i in range(n):
+            cut = slice(i * rows, (i + 1) * rows)
+            x_ref[cut] = refs[i][...]
+            c_ref[cut] = refs[n + i][...]
+            xt_ref[:, cut] = refs[i][...].T
+
+    tok = n * rows
+    return small(
+        kernel,
+        "gather",
+        [in_vmem((tok, feat), BF), in_vmem((tok, feat), BF), in_vmem((feat, tok), BF)],
+        [p[0] for p in pairs] + [p[1] for p in pairs],
+        mib=8,
+    )
+
+
+def pair(flags, blocks):
+    rows, feat = blocks[0].shape
+
+    def kernel(flag_ref, *refs):
+        for a_ref, b_ref, out_ref in (refs[0:2] + refs[4:5], refs[2:4] + refs[5:6]):
+
+            @pl.when(flag_ref[0] % 2 == 0)
+            def _():
+                out_ref[:rows] = a_ref[...]
+                out_ref[rows:] = b_ref[...]
+
+            @pl.when(flag_ref[0] % 2 == 1)
+            def _():
+                out_ref[:rows] = b_ref[...]
+                out_ref[rows:] = a_ref[...]
+
+    return small(kernel, "pair", [in_vmem((2 * rows, feat), BF)] * 2, blocks, [flags])
+
+
+def split(flags, values):
+    rows, feat = values.shape[0] // 2, values.shape[1]
+
+    def kernel(flag_ref, in_ref, send_ref, keep_ref):
+        for flag in range(2):
+
+            @pl.when(flag_ref[0] % 2 == flag)
+            def _():
+                keep_ref[...] = in_ref[flag * rows : (flag + 1) * rows]
+                send_ref[...] = in_ref[(1 - flag) * rows : (2 - flag) * rows]
+
+    return small(kernel, "split", [in_vmem((rows, feat), F32)] * 2, [values], [flags])
+
+
+def choose(flags, at_end, start, done, half, behind):
     rows = done.shape[1]
 
     def kernel(flag_ref, end_ref, done_ref, half_ref, out_ref):
-        @pl.when(flag_ref[0] == 1)
+        @pl.when(flag_ref[0] >= 2)
         def _():
             out_ref[...] = end_ref[:, start : start + 2 * rows]
 
-        @pl.when(flag_ref[0] == 0)
+        @pl.when(flag_ref[0] < 2)
         def _():
             out_ref[:, :rows] = done_ref[...]
             out_ref[:, rows:] = half_ref[...]
 
-    shape = jax.ShapeDtypeStruct((3, 2 * rows, done.shape[2]), BF)
+    shape = in_vmem((3, 2 * rows, done.shape[2]), BF)
     return small(
-        kernel, "choose", [shape], [at_end, done, half], [is_end], behind
+        kernel, "choose", [shape], [at_end, done, half], [flags], behind
     )[0]
 
 
@@ -235,24 +326,24 @@
                 route.append((d * side + i, to[0] * side + to[1]))
         return lax.ppermute(values, "row", route)
 
-    first = core == upper
-
-    def pair(own):
-        other = swap(own, 1)
-        return jnp.where(
-            first, jnp.concatenate([own, other], 0), jnp.concatenate([other, own], 0)
-        )
-
-    x_own, c_own = pair(tokens[0]), pair(cotangent[0])
-    order = [(0, 0), (0, 1)] + [(g, h) for h in (0, 1) for g in range(1, groups)]
-    for h in range(2, SLABS):
-        order += [(g, h) for g in reversed(range(groups))]
+    is_end = ((down == 0) | (down == side - 1)).astype(jnp.int32)
+    flags = ((core != upper).astype(jnp.int32) + 2 * is_end).reshape(1)
+
+    x_mine, c_mine = stage([tokens[0], cotangent[0]])
+    x_own, c_own = pair(
+        flags,
+        [x_mine, swap(tokens[0], 1), c_mine, swap(cotangent[0], 1)],
+    )
+    lead = SLABS // 2
+    order = [(0, h) for h in range(lead)]
+    order += [(g, h) for h in range(SLABS) for g in range(1, groups)]
+    order += [(0, h) for h in range(lead, SLABS)]
     sums, sends = {}, {}
     inputs = {0: (x_own, c_own)}
 
     def prepare(gs, h, *behind):
         x, c = inputs[gs[0]] if len(gs) == 1 else inputs["all"]
-        p, s = partials(x, c, w_gate, w_up, w_down, h, slab, wire, behind)
+        p, s = partials(x, c, *weights, h, slab, wire, behind)
         for n, g in enumerate(gs):
             sums[g, h], sends[g, h] = (p, 2 * rows * n), (s, 2 * rows * n)
 
@@ -260,16 +351,22 @@
         values, start = entry
         return lax.slice_in_dim(values, start, start + 2 * rows, axis=1)
 
+    weights = [in_hbm(w) for w in (w_gate, w_up, w_down)]
     prepare([0], 0)
     for g in range(1, groups):
         inputs[g] = swap(x_own, 2 * g), swap(c_own, 2 * g)
-    x_all, c_all = [
-        jnp.concatenate([inputs[g][i] for g in range(groups)], 0) for i in range(2)
-    ]
+    x_all, c_all, xt_all = gather([inputs[g] for g in range(groups)])
     inputs["all"] = x_all, c_all
-    xt_all = x_all.T
+
+    def core_sum(values):
+        send, keep = split(flags, values)
+        return keep + swap(send, 1)
 
     fulls = {}
+    received = [None, None]
+    last = {}
+    for g, h in order:
+        last[g] = h
     outs = [None] * groups
     grads = ()
     marks = []
@@ -284,6 +381,10 @@
         step = (mm(full[0], wd, 1, 0), mm(full[1], wg, 1, 1) + mm(full[2], wu, 1, 1))
         outs[g] = step if outs[g] is None else (outs[g][0] + step[0], outs[g][1] + step[1])
         marks.extend(outs[g])
+        if g > 0 and h == last[g]:
+            for i in range(2):
+                came = swap(outs[g][i].astype(wire), 2 * g).astype(F32)
+                received[i] = came if received[i] is None else received[i] + came
         if all((i, h) in fulls for i in range(groups)):
             *grads, mark = weight_grads(
                 xt_all, c_all, [fulls[i, h] for i in range(groups)], h, hid, grads
@@ -292,51 +393,59 @@
 
     if mid == 2:
         pairs = [(d, d ^ 1) for d in range(side)]
-        is_end = ((down == 0) | (down == side - 1)).astype(jnp.int32).reshape(1)
         steps = len(order)
-        made = {1: [([0], 1)]}
-        made[2] = [([g], h) for h in (0, 1) for g in range(1, groups)]
-        for h in range(2, SLABS):
-            made[3 + 2 * (h - 2)] = [(list(range(groups)), h)]
+        made = {t: [([g], h)] for t, (g, h) in enumerate(order) if h < lead}
+        for h in range(lead, SLABS):
+            made[order.index((1, h))] = [(list(range(groups)), h)]
         arrived, results = {}, {}
 
         def depart(t, *behind):
             if t < LAG:
                 load = rows_of(sends[order[t]])
             elif t < steps:
-                load = choose(is_end, *sends[order[t]], *results[t - LAG], behind)
+                load = choose(flags, *sends[order[t]], *results[t - LAG], behind)
             else:
-                load = choose(is_end, *sends[order[-1]], *results[t - LAG], behind)
+                load = choose(flags, *sends[order[-1]], *results[t - LAG], behind)
             arrived[t] = along(load, pairs)
             return load
 
         depart(0)
         prepare([0], 1, sends[0, 0][0])
         load = depart(1)
+        w_gate, w_up, w_down = weights = stage([w_gate, w_up, w_down], [load])
+        waiting = None
         for t in range(steps + LAG):
             came = arrived[t]
             marks.clear()
-            behind = []
+            behind = [load]
+            started = None
             if t < steps:
-                send, keep = halve(came, *sums[order[t]], rows, wire)
-                half = middle(send)
+                send, keep = halve(came, *sums[order[t]], rows, wire, behind)
+                started = keep, middle(send)
                 behind = [send]
+            if waiting is not None:
+                done = finish(*waiting, behind)
+                results[t - 1] = done, middle(done)
+                behind = [done]
+            waiting = started
             for gs, h in made.get(t + 2, ()):
-                prepare(gs, h, *(behind or [came]))
+                prepare(gs, h, *behind)
                 marks.append(sends[gs[0], h][0])
             if t >= LAG:
-                settle(*order[t - LAG], choose(is_end, came, 0, *results[t - LAG], behind))
+                settle(*order[t - LAG], choose(flags, came, 0, *results[t - LAG], behind))
+            if t == steps - 1:
+                done = finish(*waiting, marks)
+                results[t] = done, middle(done)
+                marks.append(done)
+                waiting = None
             if t + 2 < steps + LAG:
                 load = depart(t + 2, *marks)
-            if t < steps:
-                done = finish(keep, half, [load])
-                results[t] = done, middle(done)
     else:
-        prepare([0], 1)
-        for g in range(1, groups):
-            for h in (0, 1):
-                prepare([g], h)
-        for h in range(2, SLABS):
+        for h in range(lead):
+            for g in range(groups):
+                if g + h > 0:
+                    prepare([g], h)
+        for h in range(lead, SLABS):
             prepare(list(range(groups)), h)
         for g, h in order:
             total = rows_of(sums[g, h])
@@ -351,22 +460,10 @@
                 full = jnp.where((down == r) | (down == side - 1 - r), came, full)
             settle(g, h, full)
 
-    def core_sum(values):
-        lower, higher = values[:rows], values[rows:]
-        keep = jnp.where(first, lower, higher)
-        send = jnp.where(first, higher, lower)
-        return keep + swap(send, 1)
-
-    mixed_grad = []
-    for i in range(2):
-        result = None
-        for g in reversed(range(groups)):
-            summed = core_sum(outs[g][i])
-            if g > 0:
-                summed = swap(summed, 2 * g)
-            result = summed if result is None else result + summed
-        mixed_grad.append(result.astype(BF)[None])
-    return tuple(mixed_grad) + tuple(g[None] for g in grads)
+    return (
+        tuple(core_sum(received[i] + outs[0][i]).astype(BF)[None] for i in range(2))
+        + tuple(g[None] for g in grads)
+    )
 
 
 def solution(mesh):

time: 145 us -> 117 us (0.81)
  local copies, waits for them, and re-layouts: 21.3 us -> 0 us
  waiting for transfers between devices: 26.5 us -> 12.8 us
  starting transfers between devices: 47.4 us -> 58.7 us
  other arithmetic: 4.72 us -> 1.37 us
    unnamed x52 -> x0, local copies, waits for them, and re-layouts: 20.1 us -> none
    ppermute x11, starting transfers between devices: 37.8 us -> 49 us  [along(): return lax.ppermute(values, 'row', route)]
    ppermute x10 -> x8, waiting for transfers between devices: 11.6 us -> 2.22 us  [swap(): return lax.ppermute(values, 'row', [(i, i ^ bits) for i in range(count)])]
    pallas_call x32 -> x36, Pallas kernels: 9.39 us -> 2.49 us  [small(): pl.pallas_call(lambda *refs: kernel(*refs[:n], *refs[m:]), in_specs=[FLAG...]
    pallas_call x0 -> x2, Pallas kernels: none -> 5.67 us  [stage(): pl.pallas_call(kernel, in_specs=[REST] * m, out_specs=[HERE] * n, out_sha...]
    ppermute x11, waiting for transfers between devices: 14.9 us -> 10.5 us  [along(): return lax.ppermute(values, 'row', route)]
    select_n x6 -> x0, other arithmetic: 2.2 us -> none  [the longest x2 2.08 us: pair(): jnp.where(first, jnp.concatenate([own, other], 0), jnp.concatenate([other...]
    pallas_call x6, Pallas kernels: 9.43 us -> 11.1 us  [partials(): pl.pallas_call(partial_kernel, grid=(nb,), in_specs=[whole, whole, cols,...]
  transfers between devices with their start and end apart: 37 -> 35, of which waited for: 9 -> 7; matrix products, arithmetic and copies ran while one was open for 11% -> 9% of each run, Pallas kernels for 21% -> 25%
where the time goes in v2:
time: 117 us
  starting transfers between devices  58.7 us (50%)
  Pallas kernels  32.1 us (27%)
  waiting for transfers between devices  12.8 us (11%)
  matrix products  10.4 us (9%)
  between operations  1.4 us (1%)
  other arithmetic  1.37 us (1%)
    ppermute x11, starting transfers between devices, along(): return lax.ppermute(values, 'row', route)  49 us
    pallas_call x4, Pallas kernels, weight_grads(): pl.pallas_call(lambda *refs: grads_kernel(n, *refs), grid=(nb,), in_specs...  12.8 us
    pallas_call x6, Pallas kernels, partials(): pl.pallas_call(partial_kernel, grid=(nb,), in_specs=[whole, whole, cols,...  11.1 us
    ppermute x11, waiting for transfers between devices, along(): return lax.ppermute(values, 'row', route)  10.5 us
    dot_general x24, matrix products, mm(): lax.dot_general(left, right, (((ldim,), (rdim,)), ((), ())), preferred_el...  10.4 us
    pallas_call x2, Pallas kernels, stage(): pl.pallas_call(kernel, in_specs=[REST] * m, out_specs=[HERE] * n, out_sha...  5.67 us
    ppermute x8, starting transfers between devices, swap(): return lax.ppermute(values, 'row', [(i, i ^ bits) for i in range(count)])  5.34 us
    ppermute x16, starting transfers between devices, middle(): return lax.ppermute(values, 'row', route)  4.4 us
  transfers between devices with their start and end apart: 35, of which 7 were waited for; matrix products, arithmetic and copies ran while one was open for 9% of the time, Pallas kernels for 25%

profile of v2, /device:TPU:0, one launch (start us, length us, event | category | flops | bytes accessed | tf_op | source)
XLA Modules:
  0.0 116.8 jit_solution(16212688774435305020)
XLA Ops:
  2.8 2.5 %partials.6 = (f32[3,128,512]{2,1,0:T(8,128)S(1)}, bf16[3,128,512]{2,1,0:T(8,128)(2,1)S(1)}) custom-call(bf16[128,1024]{1,0:T(8,128)(2,1)S(1)} %get-tuple-element.63.refs_0_.x_ref, bf16[128,1024]{1,0:T(8,128)(2,1)S(1)} %get-tuple-element.64.refs_2_.c_ref, bf16[1024,2048]{1,0:T(8,128)(2,1)} %bitcast.96, bf16[1024,2048]{1,0:T(8,128)(2,1)} %bitcast.99, ...), custom_call_target="tpu_custom_call" | custom-call | flops 402653184 | bytes 4325376 | tf_op jit(solution)/shard_map/partials/pallas_call | solution.py:48
  5.3 2.8 %collective-permute-start.4 = (bf16[3,128,512]{2,1,0:T(8,128)(2,1)S(1)}, bf16[3,128,512]{2,1,0:T(8,128)(2,1)S(1)}, u32[]{:S(2)}, u32[]{:S(2)}) collective-permute-start(bf16[3,128,512]{2,1,0:T(8,128)(2,1)S(1)} %get-tuple-element.67.refs_0_), channel_id=1, source_target_pairs={{0,4},{1,5},{2,6},{3,7},{4,0},{5,1},{6,2},{7,3},{8,12},{9,13},{10,... | collective-permute-start | bytes 1179656 | tf_op jit(solution)/shard_map/ppermute | solution.py:319
  8.1 2.5 %partials.7 = (f32[3,128,512]{2,1,0:T(8,128)S(1)}, bf16[3,128,512]{2,1,0:T(8,128)(2,1)S(1)}) custom-call(bf16[128,1024]{1,0:T(8,128)(2,1)S(1)} %get-tuple-element.63.refs_0_.x_ref, bf16[128,1024]{1,0:T(8,128)(2,1)S(1)} %get-tuple-element.64.refs_2_.c_ref, bf16[1024,2048]{1,0:T(8,128)(2,1)} %bitcast.97, bf16[1024,2048]{1,0:T(8,128)(2,1)} %bitcast.100, ...), custom_call_target="tpu_custom_call" | custom-call | flops 402653184 | bytes 4325376 | tf_op jit(solution)/shard_map/partials/pallas_call | solution.py:48
  10.6 2.0 %collective-permute-start.2 = (bf16[128,1024]{1,0:T(8,128)(2,1)S(1)}, bf16[128,1024]{1,0:T(8,128)(2,1)S(1)}, u32[]{:S(2)}, u32[]{:S(2)}) collective-permute-start(bf16[128,1024]{1,0:T(8,128)(2,1)S(1)} %get-tuple-element.63.refs_0_.x_ref), channel_id=1, source_target_pairs={{0,2},{1,3},{2,0},{3,1},{4,6},{5,7},{6,4},{7,5},{8,10},{9,11},{10,... | collective-permute-start | bytes 786440 | tf_op jit(solution)/shard_map/ppermute | solution.py:313
  12.7 5.2 %collective-permute-done.4.refs_0_ = bf16[3,128,512]{2,1,0:T(8,128)(2,1)S(1)} collective-permute-done((bf16[3,128,512]{2,1,0:T(8,128)(2,1)S(1)}, bf16[3,128,512]{2,1,0:T(8,128)(2,1)S(1)}, u32[]{:S(2)}, u32[]{:S(2)}) %collective-permute-start.4) | collective-permute-done | bytes 393248 | tf_op jit(solution)/shard_map/ppermute | solution.py:319
  18.1 4.7 %stage.3 = (bf16[1024,2048]{1,0:T(8,128)(2,1)S(1)}, bf16[1024,2048]{1,0:T(8,128)(2,1)S(1)}, bf16[2048,1024]{1,0:T(8,128)(2,1)S(1)}) custom-call(bf16[1024,2048]{1,0:T(8,128)(2,1)} %bitcast.98, bf16[1024,2048]{1,0:T(8,128)(2,1)} %bitcast.101, bf16[2048,1024]{1,0:T(8,128)(2,1)} %bitcast.104, bf16[3,128,512]{2,1,0:T(8,128)(2,1)S(1)} %get-tuple-element.68.refs_3_.refs_2_), custom_call_target="tpu_custom_call" | custom-call | flops 12582912 | bytes 12582912 | tf_op jit(solution)/shard_map/stage/pallas_call | solution.py:207
  22.8 1.8 %collective-permute-done.3.refs_3_.c_ref = bf16[128,1024]{1,0:T(8,128)(2,1)S(1)} collective-permute-done((bf16[128,1024]{1,0:T(8,128)(2,1)S(1)}, bf16[128,1024]{1,0:T(8,128)(2,1)S(1)}, u32[]{:S(2)}, u32[]{:S(2)}) %collective-permute-start.3) | collective-permute-done | bytes 262176 | tf_op jit(solution)/shard_map/ppermute | solution.py:313
  25.9 1.9 %collective-permute-start.5 = (bf16[3,128,512]{2,1,0:T(8,128)(2,1)S(1)}, bf16[3,128,512]{2,1,0:T(8,128)(2,1)S(1)}, u32[]{:S(2)}, u32[]{:S(2)}) collective-permute-start(bf16[3,128,512]{2,1,0:T(8,128)(2,1)S(1)} %get-tuple-element.74.refs_2_), channel_id=1, source_target_pairs={{0,4},{1,5},{2,6},{3,7},{4,0},{5,1},{6,2},{7,3},{8,12},{9,13},{10,... | collective-permute-start | bytes 1179656 | tf_op jit(solution)/shard_map/ppermute | solution.py:319
  28.6 1.4 %partials.9 = (f32[3,128,512]{2,1,0:T(8,128)S(1)}, bf16[3,128,512]{2,1,0:T(8,128)(2,1)S(1)}) custom-call(bf16[128,1024]{1,0:T(8,128)(2,1)S(1)} %collective-permute-done.2.refs_1_.x_ref, bf16[128,1024]{1,0:T(8,128)(2,1)S(1)} %collective-permute-done.3.refs_3_.c_ref, bf16[1024,2048]{1,0:T(8,128)(2,1)S(1)} %get-tuple-element.69.wg_ref, ...), custom_call_target="tpu_custom_call" | custom-call | flops 402653184 | bytes 4325376 | tf_op jit(solution)/shard_map/partials/pallas_call | solution.py:48
  30.1 6.9 %collective-permute-start.10 = (bf16[3,128,512]{2,1,0:T(8,128)(2,1)S(1)}, bf16[3,128,512]{2,1,0:T(8,128)(2,1)S(1)}, u32[]{:S(2)}, u32[]{:S(2)}) collective-permute-start(bf16[3,128,512]{2,1,0:T(8,128)(2,1)S(1)} %choose.16.refs_2_), channel_id=1, source_target_pairs={{0,4},{1,5},{2,6},{3,7},{4,0},{5,1},{6,2},{7,3},{8,12},{9,13},{10,... | collective-permute-start | bytes 1179656 | tf_op jit(solution)/shard_map/ppermute | solution.py:319
  39.0 1.7 %partials.10 = (f32[3,256,512]{2,1,0:T(8,128)S(1)}, bf16[3,256,512]{2,1,0:T(8,128)(2,1)S(1)}) custom-call(bf16[256,1024]{1,0:T(8,128)(2,1)S(1)} %get-tuple-element.65.x_ref, bf16[256,1024]{1,0:T(8,128)(2,1)S(1)} %get-tuple-element.66.c_ref.refs_1_, bf16[1024,2048]{1,0:T(8,128)(2,1)S(1)} %get-tuple-element.69.wg_ref, ...), custom_call_target="tpu_custom_call" | custom-call | flops 805306368 | bytes 5505024 | tf_op jit(solution)/shard_map/partials/pallas_call | solution.py:48
  40.8 5.8 %collective-permute-start.15 = (bf16[3,128,512]{2,1,0:T(8,128)(2,1)S(1)}, bf16[3,128,512]{2,1,0:T(8,128)(2,1)S(1)}, u32[]{:S(2)}, u32[]{:S(2)}) collective-permute-start(bf16[3,128,512]{2,1,0:T(8,128)(2,1)S(1)} %choose.17.refs_2_), channel_id=1, source_target_pairs={{0,4},{1,5},{2,6},{3,7},{4,0},{5,1},{6,2},{7,3},{8,12},{9,13},{10,... | collective-permute-start | bytes 1179656 | tf_op jit(solution)/shard_map/ppermute | solution.py:319
  48.5 1.7 %partials.11 = (f32[3,256,512]{2,1,0:T(8,128)S(1)}, bf16[3,256,512]{2,1,0:T(8,128)(2,1)S(1)}) custom-call(bf16[256,1024]{1,0:T(8,128)(2,1)S(1)} %get-tuple-element.65.x_ref, bf16[256,1024]{1,0:T(8,128)(2,1)S(1)} %get-tuple-element.66.c_ref.refs_1_, bf16[1024,2048]{1,0:T(8,128)(2,1)S(1)} %get-tuple-element.69.wg_ref, ...), custom_call_target="tpu_custom_call" | custom-call | flops 805306368 | bytes 5505024 | tf_op jit(solution)/shard_map/partials/pallas_call | solution.py:48
  50.6 6.6 %collective-permute-start.14 = (bf16[3,128,512]{2,1,0:T(8,128)(2,1)S(1)}, bf16[3,128,512]{2,1,0:T(8,128)(2,1)S(1)}, u32[]{:S(2)}, u32[]{:S(2)}) collective-permute-start(bf16[3,128,512]{2,1,0:T(8,128)(2,1)S(1)} %choose.19.refs_2_), channel_id=1, source_target_pairs={{0,4},{1,5},{2,6},{3,7},{4,0},{5,1},{6,2},{7,3},{8,12},{9,13},{10,... | collective-permute-start | bytes 1179656 | tf_op jit(solution)/shard_map/ppermute | solution.py:319
  59.4 7.2 %collective-permute-start.19 = (bf16[3,128,512]{2,1,0:T(8,128)(2,1)S(1)}, bf16[3,128,512]{2,1,0:T(8,128)(2,1)S(1)}, u32[]{:S(2)}, u32[]{:S(2)}) collective-permute-start(bf16[3,128,512]{2,1,0:T(8,128)(2,1)S(1)} %choose.21.refs_2_), channel_id=1, source_target_pairs={{0,4},{1,5},{2,6},{3,7},{4,0},{5,1},{6,2},{7,3},{8,12},{9,13},{10,... | collective-permute-start | bytes 1179656 | tf_op jit(solution)/shard_map/ppermute | solution.py:319
  68.4 3.2 %weight_grads.4 = (f32[1024,2048]{1,0:T(8,128)}, f32[1024,2048]{1,0:T(8,128)}, f32[2048,1024]{1,0:T(8,128)}, f32[8,128]{1,0:T(8,128)S(1)}) custom-call(bf16[1024,256]{1,0:T(8,128)(2,1)S(1)} %get-tuple-element.94.refs_0_, bf16[256,1024]{1,0:T(8,128)(2,1)S(1)} %get-tuple-element.66.c_ref.refs_1_, bf16[3,128,512]{2,1,0:T(8,128)(2,1)S(1)} %choose.18.refs_2_, ...), custom_call_target="tpu_custom_call" | custom-call | flops 805306368 | bytes 6291456 | tf_op jit(solution)/shard_map/weight_grads/pallas_call | solution.py:94
  72.0 3.1 %collective-permute-start.22 = (bf16[3,128,512]{2,1,0:T(8,128)(2,1)S(1)}, bf16[3,128,512]{2,1,0:T(8,128)(2,1)S(1)}, u32[]{:S(2)}, u32[]{:S(2)}) collective-permute-start(bf16[3,128,512]{2,1,0:T(8,128)(2,1)S(1)} %choose.23.refs_2_), channel_id=1, source_target_pairs={{0,4},{1,5},{2,6},{3,7},{4,0},{5,1},{6,2},{7,3},{8,12},{9,13},{10,... | collective-permute-start | bytes 1179656 | tf_op jit(solution)/shard_map/ppermute | solution.py:319
  76.9 3.2 %weight_grads.5 = (f32[1024,2048]{1,0:T(8,128)}, f32[1024,2048]{1,0:T(8,128)}, f32[2048,1024]{1,0:T(8,128)}, f32[8,128]{1,0:T(8,128)S(1)}) custom-call(bf16[1024,256]{1,0:T(8,128)(2,1)S(1)} %get-tuple-element.94.refs_0_, bf16[256,1024]{1,0:T(8,128)(2,1)S(1)} %get-tuple-element.66.c_ref.refs_1_, ...), custom_call_target="tpu_custom_call", output_to_operand_aliasing={{0}: (4, {}), {1}: (5, {}), {2}: (6, {})} | custom-call | flops 805306368 | bytes 6291456 | tf_op jit(solution)/shard_map/weight_grads/pallas_call | solution.py:94
  80.6 4.6 %collective-permute-start.25 = (bf16[3,128,512]{2,1,0:T(8,128)(2,1)S(1)}, bf16[3,128,512]{2,1,0:T(8,128)(2,1)S(1)}, u32[]{:S(2)}, u32[]{:S(2)}) collective-permute-start(bf16[3,128,512]{2,1,0:T(8,128)(2,1)S(1)} %choose.25.refs_2_), channel_id=1, source_target_pairs={{0,4},{1,5},{2,6},{3,7},{4,0},{5,1},{6,2},{7,3},{8,12},{9,13},{10,... | collective-permute-start | bytes 1179656 | tf_op jit(solution)/shard_map/ppermute | solution.py:319
  87.7 8.8 %collective-permute-start.29 = (bf16[3,128,512]{2,1,0:T(8,128)(2,1)S(1)}, bf16[3,128,512]{2,1,0:T(8,128)(2,1)S(1)}, u32[]{:S(2)}, u32[]{:S(2)}) collective-permute-start(bf16[3,128,512]{2,1,0:T(8,128)(2,1)S(1)} %choose.27.refs_4_), channel_id=1, source_target_pairs={{0,4},{1,5},{2,6},{3,7},{4,0},{5,1},{6,2},{7,3},{8,12},{9,13},{10,... | collective-permute-start | bytes 1179656 | tf_op jit(solution)/shard_map/ppermute | solution.py:319
  99.2 1.5 %collective-permute-start.28 = (bf16[128,1024]{1,0:T(8,128)(2,1)S(1)}, bf16[128,1024]{1,0:T(8,128)(2,1)S(1)}, u32[]{:S(2)}, u32[]{:S(2)}) collective-permute-start(bf16[128,1024]{1,0:T(8,128)(2,1)S(1)} %get-tuple-element.117), channel_id=1, source_target_pairs={{0,2},{1,3},{2,0},{3,1},{4,6},{5,7},{6,4},{7,5},{8,10},{9,11},{10,... | collective-permute-start | bytes 786440 | tf_op jit(solution)/shard_map/ppermute | solution.py:313
  101.2 3.8 %collective-permute-done.29.refs_1_ = bf16[3,128,512]{2,1,0:T(8,128)(2,1)S(1)} collective-permute-done((bf16[3,128,512]{2,1,0:T(8,128)(2,1)S(1)}, bf16[3,128,512]{2,1,0:T(8,128)(2,1)S(1)}, u32[]{:S(2)}, u32[]{:S(2)}) %collective-permute-start.29) | collective-permute-done | bytes 393248 | tf_op jit(solution)/shard_map/ppermute | solution.py:319
  105.0 3.2 %weight_grads.6 = (f32[1024,2048]{1,0:T(8,128)}, f32[1024,2048]{1,0:T(8,128)}, f32[2048,1024]{1,0:T(8,128)}, f32[8,128]{1,0:T(8,128)}) custom-call(bf16[1024,256]{1,0:T(8,128)(2,1)S(1)} %get-tuple-element.94.refs_0_, bf16[256,1024]{1,0:T(8,128)(2,1)S(1)} %get-tuple-element.66.c_ref.refs_1_, ...), custom_call_target="tpu_custom_call", output_to_operand_aliasing={{0}: (4, {}), {1}: (5, {}), {2}: (6, {})} | custom-call | flops 805306368 | bytes 6291456 | tf_op jit(solution)/shard_map/weight_grads/pallas_call | solution.py:94
  112.2 3.2 %weight_grads.7 = (f32[1024,2048]{1,0:T(8,128)}, f32[1024,2048]{1,0:T(8,128)}, f32[2048,1024]{1,0:T(8,128)}, f32[8,128]{1,0:T(8,128)}) custom-call(bf16[1024,256]{1,0:T(8,128)(2,1)S(1)} %get-tuple-element.94.refs_0_, bf16[256,1024]{1,0:T(8,128)(2,1)S(1)} %get-tuple-element.66.c_ref.refs_1_, ...), custom_call_target="tpu_custom_call", output_to_operand_aliasing={{0}: (4, {}), {1}: (5, {}), {2}: (6, {})} | custom-call | flops 805306368 | bytes 6291456 | tf_op jit(solution)/shard_map/weight_grads/pallas_call | solution.py:94
  (120 shorter events, 26.2 us)
Async XLA Ops:
  5.3 12.7 %collective-permute-start.4 = (bf16[3,128,512]{2,1,0:T(8,128)(2,1)S(1)}, bf16[3,128,512]{2,1,0:T(8,128)(2,1)S(1)}, u32[]{:S(2)}, u32[]{:S(2)}) collective-permute-start(bf16[3,128,512]{2,1,0:T(8,128)(2,1)S(1)} %get-tuple-element.67.refs_0_), channel_id=1, source_target_pairs={{0,4},{1,5},{2,6},{3,7},{4,0},{5,1},{6,2},{7,3},{8,12},{9,13},{10,... | collective-permute-start | bytes 1179656 | tf_op jit(solution)/shard_map/ppermute | solution.py:319
  10.5 17.3 %collective-permute-start.7 = (bf16[3,128,512]{2,1,0:T(8,128)(2,1)S(1)}, bf16[3,128,512]{2,1,0:T(8,128)(2,1)S(1)}, u32[]{:S(2)}, u32[]{:S(2)}) collective-permute-start(bf16[3,128,512]{2,1,0:T(8,128)(2,1)S(1)} %get-tuple-element.68.refs_3_.refs_2_), channel_id=1, source_target_pairs={{0,4},{1,5},{2,6},{3,7},{4,0},{5,1},{6,2},{7,3},{8,12},{9,13},{10,... | collective-permute-start | bytes 1179656 | tf_op jit(solution)/shard_map/ppermute | solution.py:319
  10.6 12.2 %collective-permute-start.2 = (bf16[128,1024]{1,0:T(8,128)(2,1)S(1)}, bf16[128,1024]{1,0:T(8,128)(2,1)S(1)}, u32[]{:S(2)}, u32[]{:S(2)}) collective-permute-start(bf16[128,1024]{1,0:T(8,128)(2,1)S(1)} %get-tuple-element.63.refs_0_.x_ref), channel_id=1, source_target_pairs={{0,2},{1,3},{2,0},{3,1},{4,6},{5,7},{6,4},{7,5},{8,10},{9,11},{10,... | collective-permute-start | bytes 786440 | tf_op jit(solution)/shard_map/ppermute | solution.py:313
  12.6 12.0 %collective-permute-start.3 = (bf16[128,1024]{1,0:T(8,128)(2,1)S(1)}, bf16[128,1024]{1,0:T(8,128)(2,1)S(1)}, u32[]{:S(2)}, u32[]{:S(2)}) collective-permute-start(bf16[128,1024]{1,0:T(8,128)(2,1)S(1)} %get-tuple-element.64.refs_2_.c_ref), channel_id=1, source_target_pairs={{0,2},{1,3},{2,0},{3,1},{4,6},{5,7},{6,4},{7,5},{8,10},{9,11},{10,... | collective-permute-start | bytes 786440 | tf_op jit(solution)/shard_map/ppermute | solution.py:313
  18.0 9.9 %collective-permute-start.6 = (bf16[3,64,512]{2,1,0:T(8,128)(2,1)S(1)}, bf16[3,64,512]{2,1,0:T(8,128)(2,1)S(1)}, u32[]{:S(2)}, u32[]{:S(2)}) collective-permute-start(bf16[3,64,512]{2,1,0:T(8,128)(2,1)S(1)} %get-tuple-element.73.refs_0_), channel_id=1, source_target_pairs={{0,1},{1,0},{2,3},{3,2},{4,8},{5,9},{6,10},{7,11},{8,4},{9,5},{10,... | collective-permute-start | bytes 589832 | tf_op jit(solution)/shard_map/ppermute | solution.py:327
  25.9 12.1 %collective-permute-start.5 = (bf16[3,128,512]{2,1,0:T(8,128)(2,1)S(1)}, bf16[3,128,512]{2,1,0:T(8,128)(2,1)S(1)}, u32[]{:S(2)}, u32[]{:S(2)}) collective-permute-start(bf16[3,128,512]{2,1,0:T(8,128)(2,1)S(1)} %get-tuple-element.74.refs_2_), channel_id=1, source_target_pairs={{0,4},{1,5},{2,6},{3,7},{4,0},{5,1},{6,2},{7,3},{8,12},{9,13},{10,... | collective-permute-start | bytes 1179656 | tf_op jit(solution)/shard_map/ppermute | solution.py:319
  28.1 10.0 %collective-permute-start.11 = (bf16[3,64,512]{2,1,0:T(8,128)(2,1)S(1)}, bf16[3,64,512]{2,1,0:T(8,128)(2,1)S(1)}, u32[]{:S(2)}, u32[]{:S(2)}) collective-permute-start(bf16[3,64,512]{2,1,0:T(8,128)(2,1)S(1)} %get-tuple-element.78.refs_2_), channel_id=1, source_target_pairs={{0,1},{1,0},{2,3},{3,2},{4,8},{5,9},{6,10},{7,11},{8,4},{9,5},{10,... | collective-permute-start | bytes 589832 | tf_op jit(solution)/shard_map/ppermute | solution.py:327
  30.1 16.5 %collective-permute-start.10 = (bf16[3,128,512]{2,1,0:T(8,128)(2,1)S(1)}, bf16[3,128,512]{2,1,0:T(8,128)(2,1)S(1)}, u32[]{:S(2)}, u32[]{:S(2)}) collective-permute-start(bf16[3,128,512]{2,1,0:T(8,128)(2,1)S(1)} %choose.16.refs_2_), channel_id=1, source_target_pairs={{0,4},{1,5},{2,6},{3,7},{4,0},{5,1},{6,2},{7,3},{8,12},{9,13},{10,... | collective-permute-start | bytes 1179656 | tf_op jit(solution)/shard_map/ppermute | solution.py:319
  38.3 8.5 %collective-permute-start.9 = (bf16[3,64,512]{2,1,0:T(8,128)(2,1)S(1)}, bf16[3,64,512]{2,1,0:T(8,128)(2,1)S(1)}, u32[]{:S(2)}, u32[]{:S(2)}) collective-permute-start(bf16[3,64,512]{2,1,0:T(8,128)(2,1)S(1)} %get-tuple-element.81.refs_2_), channel_id=1, source_target_pairs={{0,1},{1,0},{2,3},{3,2},{4,8},{5,9},{6,10},{7,11},{8,4},{9,5},{10,... | collective-permute-start | bytes 589832 | tf_op jit(solution)/shard_map/ppermute | solution.py:327
  40.8 16.3 %collective-permute-start.15 = (bf16[3,128,512]{2,1,0:T(8,128)(2,1)S(1)}, bf16[3,128,512]{2,1,0:T(8,128)(2,1)S(1)}, u32[]{:S(2)}, u32[]{:S(2)}) collective-permute-start(bf16[3,128,512]{2,1,0:T(8,128)(2,1)S(1)} %choose.17.refs_2_), channel_id=1, source_target_pairs={{0,4},{1,5},{2,6},{3,7},{4,0},{5,1},{6,2},{7,3},{8,12},{9,13},{10,... | collective-permute-start | bytes 1179656 | tf_op jit(solution)/shard_map/ppermute | solution.py:319
  46.7 10.6 %collective-permute-start.17 = (bf16[3,64,512]{2,1,0:T(8,128)(2,1)S(1)}, bf16[3,64,512]{2,1,0:T(8,128)(2,1)S(1)}, u32[]{:S(2)}, u32[]{:S(2)}) collective-permute-start(bf16[3,64,512]{2,1,0:T(8,128)(2,1)S(1)} %get-tuple-element.85.refs_2_), channel_id=1, source_target_pairs={{0,1},{1,0},{2,3},{3,2},{4,8},{5,9},{6,10},{7,11},{8,4},{9,5},{10,... | collective-permute-start | bytes 589832 | tf_op jit(solution)/shard_map/ppermute | solution.py:327
  50.6 16.0 %collective-permute-start.14 = (bf16[3,128,512]{2,1,0:T(8,128)(2,1)S(1)}, bf16[3,128,512]{2,1,0:T(8,128)(2,1)S(1)}, u32[]{:S(2)}, u32[]{:S(2)}) collective-permute-start(bf16[3,128,512]{2,1,0:T(8,128)(2,1)S(1)} %choose.19.refs_2_), channel_id=1, source_target_pairs={{0,4},{1,5},{2,6},{3,7},{4,0},{5,1},{6,2},{7,3},{8,12},{9,13},{10,... | collective-permute-start | bytes 1179656 | tf_op jit(solution)/shard_map/ppermute | solution.py:319
  57.2 9.5 %collective-permute-start.16 = (bf16[3,64,512]{2,1,0:T(8,128)(2,1)S(1)}, bf16[3,64,512]{2,1,0:T(8,128)(2,1)S(1)}, u32[]{:S(2)}, u32[]{:S(2)}) collective-permute-start(bf16[3,64,512]{2,1,0:T(8,128)(2,1)S(1)} %get-tuple-element.89.refs_2_), channel_id=1, source_target_pairs={{0,1},{1,0},{2,3},{3,2},{4,8},{5,9},{6,10},{7,11},{8,4},{9,5},{10,... | collective-permute-start | bytes 589832 | tf_op jit(solution)/shard_map/ppermute | solution.py:327
  59.4 15.6 %collective-permute-start.19 = (bf16[3,128,512]{2,1,0:T(8,128)(2,1)S(1)}, bf16[3,128,512]{2,1,0:T(8,128)(2,1)S(1)}, u32[]{:S(2)}, u32[]{:S(2)}) collective-permute-start(bf16[3,128,512]{2,1,0:T(8,128)(2,1)S(1)} %choose.21.refs_2_), channel_id=1, source_target_pairs={{0,4},{1,5},{2,6},{3,7},{4,0},{5,1},{6,2},{7,3},{8,12},{9,13},{10,... | collective-permute-start | bytes 1179656 | tf_op jit(solution)/shard_map/ppermute | solution.py:319
  66.6 8.6 %collective-permute-start.20 = (bf16[3,64,512]{2,1,0:T(8,128)(2,1)S(1)}, bf16[3,64,512]{2,1,0:T(8,128)(2,1)S(1)}, u32[]{:S(2)}, u32[]{:S(2)}) collective-permute-start(bf16[3,64,512]{2,1,0:T(8,128)(2,1)S(1)} %get-tuple-element.92.refs_2_), channel_id=1, source_target_pairs={{0,1},{1,0},{2,3},{3,2},{4,8},{5,9},{6,10},{7,11},{8,4},{9,5},{10,... | collective-permute-start | bytes 589832 | tf_op jit(solution)/shard_map/ppermute | solution.py:327
  72.0 13.3 %collective-permute-start.22 = (bf16[3,128,512]{2,1,0:T(8,128)(2,1)S(1)}, bf16[3,128,512]{2,1,0:T(8,128)(2,1)S(1)}, u32[]{:S(2)}, u32[]{:S(2)}) collective-permute-start(bf16[3,128,512]{2,1,0:T(8,128)(2,1)S(1)} %choose.23.refs_2_), channel_id=1, source_target_pairs={{0,4},{1,5},{2,6},{3,7},{4,0},{5,1},{6,2},{7,3},{8,12},{9,13},{10,... | collective-permute-start | bytes 1179656 | tf_op jit(solution)/shard_map/ppermute | solution.py:319
  75.1 10.3 %collective-permute-start.23 = (bf16[3,64,512]{2,1,0:T(8,128)(2,1)S(1)}, bf16[3,64,512]{2,1,0:T(8,128)(2,1)S(1)}, u32[]{:S(2)}, u32[]{:S(2)}) collective-permute-start(bf16[3,64,512]{2,1,0:T(8,128)(2,1)S(1)} %get-tuple-element.96.refs_2_), channel_id=1, source_target_pairs={{0,1},{1,0},{2,3},{3,2},{4,8},{5,9},{6,10},{7,11},{8,4},{9,5},{10,... | collective-permute-start | bytes 589832 | tf_op jit(solution)/shard_map/ppermute | solution.py:327
  75.3 5.1 %collective-permute-start.24 = (bf16[3,64,512]{2,1,0:T(8,128)(2,1)S(1)}, bf16[3,64,512]{2,1,0:T(8,128)(2,1)S(1)}, u32[]{:S(2)}, u32[]{:S(2)}) collective-permute-start(bf16[3,64,512]{2,1,0:T(8,128)(2,1)S(1)} %finish.13.refs_4_.refs_2_), channel_id=1, source_target_pairs={{0,1},{1,0},{2,3},{3,2},{4,8},{5,9},{6,10},{7,11},{8,4},{9,5},{10,... | collective-permute-start | bytes 589832 | tf_op jit(solution)/shard_map/ppermute | solution.py:327
  80.6 15.8 %collective-permute-start.25 = (bf16[3,128,512]{2,1,0:T(8,128)(2,1)S(1)}, bf16[3,128,512]{2,1,0:T(8,128)(2,1)S(1)}, u32[]{:S(2)}, u32[]{:S(2)}) collective-permute-start(bf16[3,128,512]{2,1,0:T(8,128)(2,1)S(1)} %choose.25.refs_2_), channel_id=1, source_target_pairs={{0,4},{1,5},{2,6},{3,7},{4,0},{5,1},{6,2},{7,3},{8,12},{9,13},{10,... | collective-permute-start | bytes 1179656 | tf_op jit(solution)/shard_map/ppermute | solution.py:319
  87.5 10.3 %collective-permute-start.30 = (bf16[3,64,512]{2,1,0:T(8,128)(2,1)S(1)}, bf16[3,64,512]{2,1,0:T(8,128)(2,1)S(1)}, u32[]{:S(2)}, u32[]{:S(2)}) collective-permute-start(bf16[3,64,512]{2,1,0:T(8,128)(2,1)S(1)} %finish.15.refs_6_.refs_2_), channel_id=1, source_target_pairs={{0,1},{1,0},{2,3},{3,2},{4,8},{5,9},{6,10},{7,11},{8,4},{9,5},{10,... | collective-permute-start | bytes 589832 | tf_op jit(solution)/shard_map/ppermute | solution.py:327
  87.7 17.3 %collective-permute-start.29 = (bf16[3,128,512]{2,1,0:T(8,128)(2,1)S(1)}, bf16[3,128,512]{2,1,0:T(8,128)(2,1)S(1)}, u32[]{:S(2)}, u32[]{:S(2)}) collective-permute-start(bf16[3,128,512]{2,1,0:T(8,128)(2,1)S(1)} %choose.27.refs_4_), channel_id=1, source_target_pairs={{0,4},{1,5},{2,6},{3,7},{4,0},{5,1},{6,2},{7,3},{8,12},{9,13},{10,... | collective-permute-start | bytes 1179656 | tf_op jit(solution)/shard_map/ppermute | solution.py:319
  97.9 11.3 %collective-permute-start.31 = (bf16[3,128,512]{2,1,0:T(8,128)(2,1)S(1)}, bf16[3,128,512]{2,1,0:T(8,128)(2,1)S(1)}, u32[]{:S(2)}, u32[]{:S(2)}) collective-permute-start(bf16[3,128,512]{2,1,0:T(8,128)(2,1)S(1)} %choose.29.refs_4_), channel_id=1, source_target_pairs={{0,4},{1,5},{2,6},{3,7},{4,0},{5,1},{6,2},{7,3},{8,12},{9,13},{10,... | collective-permute-start | bytes 1179656 | tf_op jit(solution)/shard_map/ppermute | solution.py:319
  99.2 10.9 %collective-permute-start.28 = (bf16[128,1024]{1,0:T(8,128)(2,1)S(1)}, bf16[128,1024]{1,0:T(8,128)(2,1)S(1)}, u32[]{:S(2)}, u32[]{:S(2)}) collective-permute-start(bf16[128,1024]{1,0:T(8,128)(2,1)S(1)} %get-tuple-element.117), channel_id=1, source_target_pairs={{0,2},{1,3},{2,0},{3,1},{4,6},{5,7},{6,4},{7,5},{8,10},{9,11},{10,... | collective-permute-start | bytes 786440 | tf_op jit(solution)/shard_map/ppermute | solution.py:313
  100.7 10.3 %collective-permute-start.33 = (bf16[128,1024]{1,0:T(8,128)(2,1)S(1)}, bf16[128,1024]{1,0:T(8,128)(2,1)S(1)}, u32[]{:S(2)}, u32[]{:S(2)}) collective-permute-start(bf16[128,1024]{1,0:T(8,128)(2,1)S(1)} %get-tuple-element.119), channel_id=1, source_target_pairs={{0,2},{1,3},{2,0},{3,1},{4,6},{5,7},{6,4},{7,5},{8,10},{9,11},{10,... | collective-permute-start | bytes 786440 | tf_op jit(solution)/shard_map/ppermute | solution.py:313
  (11 other events, 32.0 us)

commit v3 on v2

v3 whole, which is shorter than its diff:
```python
import math

import jax
import jax.numpy as jnp
from jax import lax
from jax.experimental import pallas as pl
from jax.experimental.pallas import tpu as pltpu
from jax.sharding import PartitionSpec as P

BF = jnp.bfloat16
F32 = jnp.float32
WIDE = 4
PIECES = 1
LAG = 3
LATE = 2
MIB = 2**20


def mm(left, right, ldim, rdim):
    return lax.dot_general(
        left, right, (((ldim,), (rdim,)), ((), ())), preferred_element_type=F32
    )


def params(mib):
    return pltpu.CompilerParams(vmem_limit_bytes=mib * MIB)


def partials(x, c, weights, chunks, width, wire, behind):
    m, feat = x.shape
    n = len(chunks)
    k = 5 + len(behind)

    def kernel(*refs):
        x_ref, c_ref, wg_ref, wu_ref, wd_ref = refs[:5]
        for j in range(n):

            @pl.when(pl.program_id(0) == j)
            def _():
                for i, part in enumerate(
                    (
                        mm(x_ref[...], wg_ref[...], 1, 0),
                        mm(x_ref[...], wu_ref[...], 1, 0),
                        mm(c_ref[...], wd_ref[...], 1, 1),
                    )
                ):
                    refs[k + j][i] = part
                    refs[k + n + j][i] = part.astype(wire)

    cols = pl.BlockSpec((feat, width), lambda j: (0, chunks[0] + j))
    whole = pl.BlockSpec((m, feat), lambda j: (0, 0))
    shape = (3, m, width)
    return pl.pallas_call(
        kernel,
        grid=(n,),
        in_specs=[whole, whole, cols, cols, pl.BlockSpec((width, feat), lambda j: (chunks[0] + j, 0))]
        + [REST] * len(behind),
        out_specs=[pl.BlockSpec(shape, lambda j: (0, 0, 0))] * (2 * n),
        out_shape=[in_vmem(shape, F32)] * n + [in_vmem(shape, wire)] * n,
        compiler_params=params(16),
        cost_estimate=pl.CostEstimate(
            flops=6 * m * feat * width * n,
            bytes_accessed=6 * feat * width * n,
            transcendentals=0,
        ),
        name="partials",
    )(x, c, *weights, *behind)


def grads_kernel(n, xt_ref, c_ref, *refs):
    fulls = refs[:n]
    gate_ref, up_ref, down_ref, mark_ref = refs[-4:]
    mark_ref[...] = jnp.zeros_like(mark_ref)
    hidden, gate_delta, up_delta = [
        jnp.concatenate([f[i] for f in fulls], 0) for i in range(3)
    ]
    gate_ref[...] = mm(xt_ref[...], gate_delta, 1, 0)
    up_ref[...] = mm(xt_ref[...], up_delta, 1, 0)
    down_ref[...] = mm(hidden, c_ref[...], 0, 0)


def weight_grads(xt, c, fulls, h, hid, before, behind):
    feat, tok = xt.shape
    slab = fulls[0].shape[2]
    rows = fulls[0].shape[1]
    bn = min(256, slab)
    nb = slab // bn
    n = len(fulls)
    cols = pl.BlockSpec((feat, bn), lambda j: (0, h * nb + j))
    return pl.pallas_call(
        lambda *refs: grads_kernel(n, *refs),
        grid=(nb,),
        in_specs=[
            pl.BlockSpec((feat, tok), lambda j: (0, 0)),
            pl.BlockSpec((tok, feat), lambda j: (0, 0)),
        ]
        + [pl.BlockSpec((3, rows, bn), lambda j: (0, 0, j))] * n
        + [REST] * (len(before) + len(behind)),
        out_specs=[
            cols,
            cols,
            pl.BlockSpec((bn, feat), lambda j: (h * nb + j, 0)),
            pl.BlockSpec((8, 128), lambda j: (0, 0)),
        ],
        out_shape=[
            jax.ShapeDtypeStruct((feat, hid), F32),
            jax.ShapeDtypeStruct((feat, hid), F32),
            jax.ShapeDtypeStruct((hid, feat), F32),
            jax.ShapeDtypeStruct((8, 128), F32),
        ],
        input_output_aliases={2 + n + i: i for i in range(len(before))},
        compiler_params=params(16),
        cost_estimate=pl.CostEstimate(
            flops=6 * tok * feat * slab,
            bytes_accessed=12 * feat * slab,
            transcendentals=0,
        ),
        name="weight_grads",
    )(xt, c, *fulls, *before, *behind)


def in_hbm(values):
    return pltpu.with_memory_space_constraint(values, pltpu.HBM)


def in_vmem(shape, dtype):
    return pltpu.VMEM(shape, dtype)


HERE = pl.BlockSpec(memory_space=pltpu.VMEM)
FLAG = pl.BlockSpec(memory_space=pltpu.SMEM)
REST = pl.BlockSpec(memory_space=pl.ANY)


def results_of(gate, up, hidden_grad):
    sigma = jax.nn.sigmoid(gate)
    activated = gate * sigma
    return (
        (activated * up).astype(BF),
        (hidden_grad * up * sigma * (1.0 + gate * (1.0 - sigma))).astype(BF),
        (hidden_grad * activated).astype(BF),
    )


def small(kernel, name, shapes, args, flags=(), behind=(), mib=4, spec=HERE):
    n = len(flags) + len(args)
    m = n + len(behind)
    size = sum(math.prod(a.shape) * 2 for a in list(args) + list(shapes))
    return pl.pallas_call(
        lambda *refs: kernel(*refs[:n], *refs[m:]),
        in_specs=[FLAG] * len(flags) + [spec] * len(args) + [REST] * len(behind),
        out_specs=[HERE] * len(shapes),
        out_shape=list(shapes),
        compiler_params=params(mib),
        cost_estimate=pl.CostEstimate(flops=size, bytes_accessed=size, transcendentals=0),
        name=name,
    )(*flags, *args, *behind)


def combine(came, part, start, rows, behind):
    def kernel(came_ref, part_ref, send_ref, keep_ref):
        total = came_ref[...].astype(F32) + part_ref[:, start : start + rows]
        keep_ref[...] = total
        send_ref[...] = total.astype(BF)

    shape = came.shape
    return small(
        kernel, "combine", [in_vmem(shape, BF), in_vmem(shape, F32)], [came, part], (), behind
    )


def finish(keep, came, behind):
    def kernel(keep_ref, came_ref, done_ref):
        own = [keep_ref[i] + came_ref[i].astype(F32) for i in range(3)]
        for i, values in enumerate(results_of(*own)):
            done_ref[i] = values

    return small(
        kernel, "finish", [in_vmem(keep.shape, BF)], [keep, came], (), behind
    )[0]


def stage(blocks, behind=()):
    n = len(blocks)
    m = n + len(behind)

    def kernel(*refs):
        copies = [
            pltpu.make_async_copy(refs[i], refs[m + i], refs[-1].at[i]) for i in range(n)
        ]
        for copy in copies:
            copy.start()
        for copy in copies:
            copy.wait()

    size = sum(math.prod(b.shape) * 2 for b in blocks)
    return pl.pallas_call(
        kernel,
        in_specs=[REST] * m,
        out_specs=[HERE] * n,
        out_shape=[in_vmem(b.shape, b.dtype) for b in blocks],
        scratch_shapes=[pltpu.SemaphoreType.DMA((n,))],
        compiler_params=params(4),
        cost_estimate=pl.CostEstimate(flops=size, bytes_accessed=size, transcendentals=0),
        name="stage",
    )(*[in_hbm(b) for b in blocks], *behind)


def gather(pairs):
    n = len(pairs)
    rows, feat = pairs[0][0].shape

    def kernel(*refs):
        x_ref, c_ref, xt_ref = refs[2 * n :]
        for i in range(n):
            cut = slice(i * rows, (i + 1) * rows)
            x_ref[cut] = refs[i][...]
            c_ref[cut] = refs[n + i][...]
            xt_ref[:, cut] = refs[i][...].T

    tok = n * rows
    return small(
        kernel,
        "gather",
        [in_vmem((tok, feat), BF), in_vmem((tok, feat), BF), in_vmem((feat, tok), BF)],
        [p[0] for p in pairs] + [p[1] for p in pairs],
        mib=8,
    )


def pair(flags, blocks):
    rows, feat = blocks[0].shape

    def kernel(flag_ref, *refs):
        for a_ref, b_ref, out_ref in (refs[0:2] + refs[4:5], refs[2:4] + refs[5:6]):

            @pl.when(flag_ref[0] % 2 == 0)
            def _():
                out_ref[:rows] = a_ref[...]
                out_ref[rows:] = b_ref[...]

            @pl.when(flag_ref[0] % 2 == 1)
            def _():
                out_ref[:rows] = b_ref[...]
                out_ref[rows:] = a_ref[...]

    return small(kernel, "pair", [in_vmem((2 * rows, feat), BF)] * 2, blocks, [flags])


def split(flags, values):
    rows, feat = values.shape[0] // 2, values.shape[1]

    def kernel(flag_ref, in_ref, send_ref, keep_ref):
        for flag in range(2):

            @pl.when(flag_ref[0] % 2 == flag)
            def _():
                keep_ref[...] = in_ref[flag * rows : (flag + 1) * rows]
                send_ref[...] = in_ref[(1 - flag) * rows : (2 - flag) * rows]

    return small(kernel, "split", [in_vmem((rows, feat), F32)] * 2, [values], [flags])


def choose(flags, at_end, start, done, behind):
    rows, width = done[0].shape[1:]
    n = len(at_end)

    def kernel(flag_ref, *refs):
        for j in range(n):
            cols = slice(j * width, (j + 1) * width)

            @pl.when(flag_ref[0] >= 2)
            def _():
                refs[-1][:, :, cols] = refs[j][:, start : start + rows]

            @pl.when(flag_ref[0] < 2)
            def _():
                refs[-1][:, :, cols] = refs[n + j][...]

    shape = in_vmem((3, rows, n * width), BF)
    return small(kernel, "choose", [shape], [*at_end, *done], [flags], behind)[0]


def body(tokens, gate_weight, up_weight, down_weight, cotangent):
    count = lax.axis_size("row")
    side = math.isqrt(count)
    place = lax.axis_index("row")
    across = place % side
    down = place // side
    core = across % 2
    groups = side // 2
    mid = side // 2
    wire = BF if side <= 4 else F32

    w_gate = gate_weight[0]
    w_up = up_weight[0]
    w_down = down_weight[0]
    hid = w_gate.shape[1]
    rows = tokens.shape[1]
    total_chunks = WIDE * PIECES
    width = hid // total_chunks

    def swap(values, bits):
        return lax.ppermute(values, "row", [(i, i ^ bits) for i in range(count)])

    def along(values, moves):
        route = [
            (src * side + i, dst * side + i) for src, dst in moves for i in range(side)
        ]
        return lax.ppermute(values, "row", route)

    def middle(values):
        route = []
        for d in range(side):
            for i in range(side):
                to = (side - 1 - d, i) if d in (mid - 1, mid) else (d, i ^ 1)
                route.append((d * side + i, to[0] * side + to[1]))
        return lax.ppermute(values, "row", route)

    is_end = ((down == 0) | (down == side - 1)).astype(jnp.int32)
    flags = (core + 2 * is_end).reshape(1)

    x_mine, c_mine = stage([tokens[0], cotangent[0]])
    x_own, c_own = pair(
        flags,
        [x_mine, swap(tokens[0], 1), c_mine, swap(cotangent[0], 1)],
    )
    last = total_chunks - PIECES * LATE
    order = [(0, c) for c in range(last)]
    order += [(g, c) for g in range(1, groups) for c in range(total_chunks)]
    order += [(0, c) for c in range(last, total_chunks)]
    sums, sends = {}, {}
    inputs = {0: (x_own, c_own)}

    weights = [in_hbm(w) for w in (w_gate, w_up, w_down)]

    def prepare(gs, chunks, *behind):
        x, c = inputs[gs[0]] if len(gs) == 1 else inputs["all"]
        made = partials(x, c, weights, chunks, width, wire, behind)
        for j, chunk in enumerate(chunks):
            for n, g in enumerate(gs):
                sums[g, chunk] = made[j], 2 * rows * n
                sends[g, chunk] = made[len(chunks) + j], 2 * rows * n
        return made[0]

    def rows_of(entry):
        values, start = entry
        return lax.slice_in_dim(values, start, start + 2 * rows, axis=1)

    prepare([0], [0])
    for g in range(1, groups):
        inputs[g] = swap(x_own, 2 * g), swap(c_own, 2 * g)
    x_all, c_all, xt_all = gather([inputs[g] for g in range(groups)])
    inputs["all"] = x_all, c_all

    def core_sum(values):
        send, keep = split(flags, values)
        return keep + swap(send, 1)

    fulls = {}
    received = [None, None]
    outs = [None] * groups
    grads = ()
    marks = []

    def settle(g, h, full):
        fulls[g, h] = full
        lo, hi = h * PIECES * width, (h + 1) * PIECES * width
        wg = lax.slice_in_dim(w_gate, lo, hi, axis=1)
        wu = lax.slice_in_dim(w_up, lo, hi, axis=1)
        wd = lax.slice_in_dim(w_down, lo, hi, axis=0)
        step = (mm(full[0], wd, 1, 0), mm(full[1], wg, 1, 1) + mm(full[2], wu, 1, 1))
        outs[g] = step if outs[g] is None else (outs[g][0] + step[0], outs[g][1] + step[1])
        marks.extend(outs[g])
        if g > 0 and h == WIDE - 1:
            for i in range(2):
                came = swap(outs[g][i].astype(wire), 2 * g).astype(F32)
                received[i] = came if received[i] is None else received[i] + came

    def weigh(h, behind):
        nonlocal grads
        *grads, mark = weight_grads(
            xt_all, c_all, [fulls[g, h] for g in range(groups)], h, hid, grads, behind
        )
        marks.append(mark)

    if mid == 2:
        pairs = [(d, d ^ 1) for d in range(side)]
        steps = len(order)
        step_of = {key: t for t, key in enumerate(order)}
        made = {}
        for c in range(PIECES, last, PIECES):
            made.setdefault(step_of[0, c] - 3, []).append(([0], range(c, c + PIECES)))
        for c in range(0, last, PIECES):
            made.setdefault(step_of[1, c] - 3 + (c == 0), []).append(([1], range(c, c + PIECES)))
        for c in range(last, total_chunks, PIECES):
            made.setdefault(step_of[1, c] - 3, []).append(([0, 1], range(c, c + PIECES)))
        arrived, results = {}, {}

        def depart(t, *behind):
            if t < LAG:
                load = rows_of(sends[order[t]])
            else:
                at_end, start = sends[order[min(t, steps - 1)]]
                load = choose(flags, [at_end], start, [results[t - LAG]], behind)
            arrived[t] = along(load, pairs)
            return load

        depart(0)
        last_made = sends[0, 0][0]
        if PIECES > 1:
            last_made = prepare([0], [1], last_made)
        for t in (-2, -1):
            for gs, chunks in made.get(t, ()):
                last_made = prepare(gs, list(chunks), last_made)
            if t == -2:
                depart(1)
        behind = [last_made]
        staged = []
        waiting = None
        ready = []
        for t in range(steps + LAG):
            started = None
            if t < steps:
                send, keep = combine(arrived[t], *sums[order[t]], 2 * rows, behind)
                started = keep, middle(send)
                behind = [send]
            if waiting is not None:
                results[t - 1] = finish(*waiting, behind)
                behind = [results[t - 1]]
            waiting = started
            for gs, chunks in made.get(t, ()):
                behind = [prepare(gs, list(chunks), *behind)]
            if t + 2 < steps + LAG:
                load = depart(t + 2, *behind)
                if t + 2 >= LAG:
                    behind = [load]
            if t < 3:
                staged += stage([(w_gate, w_up, w_down)[t]], behind)
                behind = staged[-1:]
                if t == 2:
                    w_gate, w_up, w_down = weights = staged
            if t >= LAG:
                g, c = order[t - LAG]
                if c % PIECES == PIECES - 1:
                    past = range(t - LAG - PIECES + 1, t - LAG + 1)
                    done = [results[u] for u in past]
                    came = [arrived[u + LAG] for u in past]
                    marks.clear()
                    settle(g, c // PIECES, choose(flags, came, 0, done, behind))
                    behind = list(marks)
            for h in range(WIDE - 1):
                if h not in ready and all((i, h) in fulls for i in range(groups)):
                    ready.append(h)
                    marks.clear()
                    weigh(h, behind)
                    behind = list(marks)
        weigh(WIDE - 1, [])
    else:
        for g in range(groups):
            for h in range(WIDE):
                chunks = [h * PIECES + j for j in range(PIECES)]
                chunks = [c for c in chunks if (g, c) not in sums]
                if chunks:
                    prepare([g], chunks)
                pieces = []
                for c in range(h * PIECES, (h + 1) * PIECES):
                    total = rows_of(sums[g, c])
                    for r in range(mid - 1):
                        moves = [(r, r + 1), (side - 1 - r, side - 2 - r)]
                        total = total + along(total.astype(wire), moves).astype(F32)
                    total = total + middle(total.astype(wire)).astype(F32)
                    full = jnp.stack(results_of(*total))
                    for r in reversed(range(mid - 1)):
                        came = along(full, [(r + 1, r), (side - 2 - r, side - 1 - r)])
                        full = jnp.where((down == r) | (down == side - 1 - r), came, full)
                    pieces.append(full)
                settle(g, h, jnp.concatenate(pieces, 2))
        for h in range(WIDE):
            weigh(h, [])

    return (
        tuple(core_sum(received[i] + outs[0][i]).astype(BF)[None] for i in range(2))
        + tuple(g[None] for g in grads)
    )


def solution(mesh):
    spec = P(("groups", "row"), None, None)
    weight = P("row", None, None)
    return jax.shard_map(
        body,
        mesh=mesh,
        in_specs=(spec, weight, weight, weight, spec),
        out_specs=(spec,) * 5,
        check_vma=False,
    )
```

time: 117 us -> 112 us (0.957)
  starting transfers between devices: 58.7 us -> 40.8 us
  Pallas kernels: 32.1 us -> 40.2 us
  waiting for transfers between devices: 12.8 us -> 18 us
    ppermute x11, starting transfers between devices: 49 us -> 34.8 us  [along(): return lax.ppermute(values, 'row', route)]
    pallas_call x6, Pallas kernels: 11.1 us -> 16.3 us  [partials(): pl.pallas_call(kernel, grid=(n,), in_specs=[whole, whole, cols, cols, pl....]
    ppermute x16 -> x8, starting transfers between devices: 4.4 us -> 0.57 us  [middle(): return lax.ppermute(values, 'row', route)]
    ppermute x8, waiting for transfers between devices: 2.22 us -> 4.99 us  [swap(): return lax.ppermute(values, 'row', [(i, i ^ bits) for i in range(count)])]
    ppermute x11, waiting for transfers between devices: 10.5 us -> 13 us  [along(): return lax.ppermute(values, 'row', route)]
    pallas_call x2 -> x4, Pallas kernels: 5.67 us -> 7.57 us  [stage(): pl.pallas_call(kernel, in_specs=[REST] * m, out_specs=[HERE] * n, out_sha...]
  transfers between devices with their start and end apart: 35 -> 27, of which waited for: 7 -> 9; matrix products, arithmetic and copies ran while one was open for 9% -> 10% of each run, Pallas kernels for 25% -> 33%
where the time goes in v3:
time: 112 us
  starting transfers between devices  40.8 us (36%)
  Pallas kernels  40.2 us (36%)
  waiting for transfers between devices  18 us (16%)
  matrix products  10.2 us (9%)
  between operations  1.4 us (1%)
  other arithmetic  1.37 us (1%)
    ppermute x11, starting transfers between devices, along(): return lax.ppermute(values, 'row', route)  34.8 us
    pallas_call x6, Pallas kernels, partials(): pl.pallas_call(kernel, grid=(n,), in_specs=[whole, whole, cols, cols, pl....  16.3 us
    ppermute x11, waiting for transfers between devices, along(): return lax.ppermute(values, 'row', route)  13 us
    pallas_call x4, Pallas kernels, weight_grads(): pl.pallas_call(lambda *refs: grads_kernel(n, *refs), grid=(nb,), in_specs...  12.8 us
    dot_general x24, matrix products, mm(): lax.dot_general(left, right, (((ldim,), (rdim,)), ((), ())), preferred_el...  10.2 us
    pallas_call x4, Pallas kernels, stage(): pl.pallas_call(kernel, in_specs=[REST] * m, out_specs=[HERE] * n, out_sha...  7.57 us
    ppermute x8, starting transfers between devices, swap(): return lax.ppermute(values, 'row', [(i, i ^ bits) for i in range(count)])  5.4 us
    ppermute x8, waiting for transfers between devices, swap(): return lax.ppermute(values, 'row', [(i, i ^ bits) for i in range(count)])  4.99 us
  transfers between devices with their start and end apart: 27, of which 9 were waited for; matrix products, arithmetic and copies ran while one was open for 10% of the time, Pallas kernels for 33%

profile of v3, /device:TPU:0, one launch (start us, length us, event | category | flops | bytes accessed | tf_op | source)
XLA Modules:
  0.0 112.0 jit_solution(8026925297493897401)
XLA Ops:
  2.8 2.6 %partials.6 = (f32[3,128,512]{2,1,0:T(8,128)S(1)}, bf16[3,128,512]{2,1,0:T(8,128)(2,1)S(1)}) custom-call(bf16[128,1024]{1,0:T(8,128)(2,1)S(1)} %get-tuple-element.61.refs_0_, bf16[128,1024]{1,0:T(8,128)(2,1)S(1)} %get-tuple-element.62.refs_2_.refs_1_, bf16[1024,2048]{1,0:T(8,128)(2,1)} %bitcast.93, bf16[1024,2048]{1,0:T(8,128)(2,1)} %bitcast.100, ...), custom_call_target="tpu_custom_call" | custom-call | flops 402653184 | bytes 3145728 | tf_op jit(solution)/shard_map/partials/pallas_call | solution.py:53
  5.4 2.8 %collective-permute-start.5 = (bf16[3,128,512]{2,1,0:T(8,128)(2,1)S(1)}, bf16[3,128,512]{2,1,0:T(8,128)(2,1)S(1)}, u32[]{:S(2)}, u32[]{:S(2)}) collective-permute-start(bf16[3,128,512]{2,1,0:T(8,128)(2,1)S(1)} %get-tuple-element.65.refs_5_), channel_id=1, source_target_pairs={{0,4},{1,5},{2,6},{3,7},{4,0},{5,1},{6,2},{7,3},{8,12},{9,13},{10,... | collective-permute-start | bytes 1179656 | tf_op jit(solution)/shard_map/ppermute | solution.py:310
  10.3 2.6 %partials.7 = (f32[3,128,512]{2,1,0:T(8,128)S(1)}, bf16[3,128,512]{2,1,0:T(8,128)(2,1)S(1)}) custom-call(bf16[128,1024]{1,0:T(8,128)(2,1)S(1)} %get-tuple-element.61.refs_0_, bf16[128,1024]{1,0:T(8,128)(2,1)S(1)} %get-tuple-element.62.refs_2_.refs_1_, bf16[1024,2048]{1,0:T(8,128)(2,1)} %bitcast.94, bf16[1024,2048]{1,0:T(8,128)(2,1)} %bitcast.101, ...), custom_call_target="tpu_custom_call" | custom-call | flops 402653184 | bytes 3145728 | tf_op jit(solution)/shard_map/partials/pallas_call | solution.py:53
  13.1 5.1 %collective-permute-done.5.refs_0_ = bf16[3,128,512]{2,1,0:T(8,128)(2,1)S(1)} collective-permute-done((bf16[3,128,512]{2,1,0:T(8,128)(2,1)S(1)}, bf16[3,128,512]{2,1,0:T(8,128)(2,1)S(1)}, u32[]{:S(2)}, u32[]{:S(2)}) %collective-permute-start.5) | collective-permute-done | bytes 393248 | tf_op jit(solution)/shard_map/ppermute | solution.py:310
  18.3 3.8 %collective-permute-done.3.refs_3_.refs_1_ = bf16[128,1024]{1,0:T(8,128)(2,1)S(1)} collective-permute-done((bf16[128,1024]{1,0:T(8,128)(2,1)S(1)}, bf16[128,1024]{1,0:T(8,128)(2,1)S(1)}, u32[]{:S(2)}, u32[]{:S(2)}) %collective-permute-start.3) | collective-permute-done | bytes 262176 | tf_op jit(solution)/shard_map/ppermute | solution.py:304
  22.1 2.6 %partials.8 = (f32[3,128,512]{2,1,0:T(8,128)S(1)}, bf16[3,128,512]{2,1,0:T(8,128)(2,1)S(1)}) custom-call(bf16[128,1024]{1,0:T(8,128)(2,1)S(1)} %collective-permute-done.2.refs_1_.refs_0_, bf16[128,1024]{1,0:T(8,128)(2,1)S(1)} %collective-permute-done.3.refs_3_.refs_1_, bf16[1024,2048]{1,0:T(8,128)(2,1)} %bitcast.95, bf16[1024,2048]{1,0:T(8,128)(2,1)} %bitcast.102, ...), custom_call_target="tpu_custom_call" | custom-call | flops 402653184 | bytes 3145728 | tf_op jit(solution)/shard_map/partials/pallas_call | solution.py:53
  25.4 2.7 %partials.9 = (f32[3,128,512]{2,1,0:T(8,128)S(1)}, bf16[3,128,512]{2,1,0:T(8,128)(2,1)S(1)}) custom-call(bf16[128,1024]{1,0:T(8,128)(2,1)S(1)} %collective-permute-done.2.refs_1_.refs_0_, bf16[128,1024]{1,0:T(8,128)(2,1)S(1)} %collective-permute-done.3.refs_3_.refs_1_, bf16[1024,2048]{1,0:T(8,128)(2,1)} %bitcast.96, bf16[1024,2048]{1,0:T(8,128)(2,1)} %bitcast.103, ...), custom_call_target="tpu_custom_call" | custom-call | flops 402653184 | bytes 3145728 | tf_op jit(solution)/shard_map/partials/pallas_call | solution.py:53
  28.1 2.2 %stage.5.refs_2_ = bf16[1024,2048]{1,0:T(8,128)(2,1)S(1)} custom-call(bf16[1024,2048]{1,0:T(8,128)(2,1)} %bitcast.97, f32[3,128,512]{2,1,0:T(8,128)S(1)} %get-tuple-element.71.refs_1_), custom_call_target="tpu_custom_call" | custom-call | flops 4194304 | bytes 4194304 | tf_op jit(solution)/shard_map/stage/pallas_call | solution.py:197
  30.7 2.9 %partials.10 = (f32[3,256,512]{2,1,0:T(8,128)S(1)}, bf16[3,256,512]{2,1,0:T(8,128)(2,1)S(1)}) custom-call(bf16[256,1024]{1,0:T(8,128)(2,1)S(1)} %get-tuple-element.63.refs_0_, bf16[256,1024]{1,0:T(8,128)(2,1)S(1)} %get-tuple-element.64.refs_1_, bf16[1024,2048]{1,0:T(8,128)(2,1)} %bitcast.98, bf16[1024,2048]{1,0:T(8,128)(2,1)} %bitcast.104, ...), custom_call_target="tpu_custom_call" | custom-call | flops 805306368 | bytes 3145728 | tf_op jit(solution)/shard_map/partials/pallas_call | solution.py:53
  33.6 3.3 %collective-permute-start.10 = (bf16[3,128,512]{2,1,0:T(8,128)(2,1)S(1)}, bf16[3,128,512]{2,1,0:T(8,128)(2,1)S(1)}, u32[]{:S(2)}, u32[]{:S(2)}) collective-permute-start(bf16[3,128,512]{2,1,0:T(8,128)(2,1)S(1)} %choose.16.refs_1_), channel_id=1, source_target_pairs={{0,4},{1,5},{2,6},{3,7},{4,0},{5,1},{6,2},{7,3},{8,12},{9,13},{10,... | collective-permute-start | bytes 1179656 | tf_op jit(solution)/shard_map/ppermute | solution.py:310
  39.5 2.9 %partials.11 = (f32[3,256,512]{2,1,0:T(8,128)S(1)}, bf16[3,256,512]{2,1,0:T(8,128)(2,1)S(1)}) custom-call(bf16[256,1024]{1,0:T(8,128)(2,1)S(1)} %get-tuple-element.63.refs_0_, bf16[256,1024]{1,0:T(8,128)(2,1)S(1)} %get-tuple-element.64.refs_1_, bf16[1024,2048]{1,0:T(8,128)(2,1)} %bitcast.99, bf16[1024,2048]{1,0:T(8,128)(2,1)} %bitcast.106, ...), custom_call_target="tpu_custom_call" | custom-call | flops 805306368 | bytes 3145728 | tf_op jit(solution)/shard_map/partials/pallas_call | solution.py:53
  42.4 2.8 %collective-permute-start.12 = (bf16[3,128,512]{2,1,0:T(8,128)(2,1)S(1)}, bf16[3,128,512]{2,1,0:T(8,128)(2,1)S(1)}, u32[]{:S(2)}, u32[]{:S(2)}) collective-permute-start(bf16[3,128,512]{2,1,0:T(8,128)(2,1)S(1)} %choose.17.refs_1_), channel_id=1, source_target_pairs={{0,4},{1,5},{2,6},{3,7},{4,0},{5,1},{6,2},{7,3},{8,12},{9,13},{10,... | collective-permute-start | bytes 1179656 | tf_op jit(solution)/shard_map/ppermute | solution.py:310
  47.9 3.6 %collective-permute-start.11 = (bf16[3,128,512]{2,1,0:T(8,128)(2,1)S(1)}, bf16[3,128,512]{2,1,0:T(8,128)(2,1)S(1)}, u32[]{:S(2)}, u32[]{:S(2)}) collective-permute-start(bf16[3,128,512]{2,1,0:T(8,128)(2,1)S(1)} %choose.18.refs_3_), channel_id=1, source_target_pairs={{0,4},{1,5},{2,6},{3,7},{4,0},{5,1},{6,2},{7,3},{8,12},{9,13},{10,... | collective-permute-start | bytes 1179656 | tf_op jit(solution)/shard_map/ppermute | solution.py:310
  52.8 2.4 %collective-permute-done.12.refs_0_.refs_1_ = bf16[3,128,512]{2,1,0:T(8,128)(2,1)S(1)} collective-permute-done((bf16[3,128,512]{2,1,0:T(8,128)(2,1)S(1)}, bf16[3,128,512]{2,1,0:T(8,128)(2,1)S(1)}, u32[]{:S(2)}, u32[]{:S(2)}) %collective-permute-start.12) | collective-permute-done | bytes 393248 | tf_op jit(solution)/shard_map/ppermute | solution.py:310
  55.7 4.3 %collective-permute-start.15 = (bf16[3,128,512]{2,1,0:T(8,128)(2,1)S(1)}, bf16[3,128,512]{2,1,0:T(8,128)(2,1)S(1)}, u32[]{:S(2)}, u32[]{:S(2)}) collective-permute-start(bf16[3,128,512]{2,1,0:T(8,128)(2,1)S(1)} %choose.20.refs_3_), channel_id=1, source_target_pairs={{0,4},{1,5},{2,6},{3,7},{4,0},{5,1},{6,2},{7,3},{8,12},{9,13},{10,... | collective-permute-start | bytes 1179656 | tf_op jit(solution)/shard_map/ppermute | solution.py:310
  61.4 2.3 %collective-permute-done.11.refs_0_.refs_1_ = bf16[3,128,512]{2,1,0:T(8,128)(2,1)S(1)} collective-permute-done((bf16[3,128,512]{2,1,0:T(8,128)(2,1)S(1)}, bf16[3,128,512]{2,1,0:T(8,128)(2,1)S(1)}, u32[]{:S(2)}, u32[]{:S(2)}) %collective-permute-start.11) | collective-permute-done | bytes 393248 | tf_op jit(solution)/shard_map/ppermute | solution.py:310
  64.1 5.6 %collective-permute-start.17 = (bf16[3,128,512]{2,1,0:T(8,128)(2,1)S(1)}, bf16[3,128,512]{2,1,0:T(8,128)(2,1)S(1)}, u32[]{:S(2)}, u32[]{:S(2)}) collective-permute-start(bf16[3,128,512]{2,1,0:T(8,128)(2,1)S(1)} %choose.22.refs_3_), channel_id=1, source_target_pairs={{0,4},{1,5},{2,6},{3,7},{4,0},{5,1},{6,2},{7,3},{8,12},{9,13},{10,... | collective-permute-start | bytes 1179656 | tf_op jit(solution)/shard_map/ppermute | solution.py:310
  71.1 3.2 %weight_grads.4 = (f32[1024,2048]{1,0:T(8,128)}, f32[1024,2048]{1,0:T(8,128)}, f32[2048,1024]{1,0:T(8,128)}, f32[8,128]{1,0:T(8,128)S(1)}) custom-call(bf16[1024,256]{1,0:T(8,128)(2,1)S(1)} %get-tuple-element.89.refs_0_, bf16[256,1024]{1,0:T(8,128)(2,1)S(1)} %get-tuple-element.64.refs_1_, bf16[3,128,512]{2,1,0:T(8,128)(2,1)S(1)} %choose.19.refs_2_, ...), custom_call_target="tpu_custom_call" | custom-call | flops 805306368 | bytes 6291456 | tf_op jit(solution)/shard_map/weight_grads/pallas_call | solution.py:90
  74.8 3.3 %collective-permute-start.19 = (bf16[3,128,512]{2,1,0:T(8,128)(2,1)S(1)}, bf16[3,128,512]{2,1,0:T(8,128)(2,1)S(1)}, u32[]{:S(2)}, u32[]{:S(2)}) collective-permute-start(bf16[3,128,512]{2,1,0:T(8,128)(2,1)S(1)} %choose.24.refs_3_), channel_id=1, source_target_pairs={{0,4},{1,5},{2,6},{3,7},{4,0},{5,1},{6,2},{7,3},{8,12},{9,13},{10,... | collective-permute-start | bytes 1179656 | tf_op jit(solution)/shard_map/ppermute | solution.py:310
  79.6 3.2 %weight_grads.5 = (f32[1024,2048]{1,0:T(8,128)}, f32[1024,2048]{1,0:T(8,128)}, f32[2048,1024]{1,0:T(8,128)}, f32[8,128]{1,0:T(8,128)S(1)}) custom-call(bf16[1024,256]{1,0:T(8,128)(2,1)S(1)} %get-tuple-element.89.refs_0_, bf16[256,1024]{1,0:T(8,128)(2,1)S(1)} %get-tuple-element.64.refs_1_, ...), custom_call_target="tpu_custom_call", output_to_operand_aliasing={{0}: (4, {}), {1}: (5, {}), {2}: (6, {})} | custom-call | flops 805306368 | bytes 6291456 | tf_op jit(solution)/shard_map/weight_grads/pallas_call | solution.py:90
  86.7 6.6 %collective-permute-start.23 = (bf16[3,128,512]{2,1,0:T(8,128)(2,1)S(1)}, bf16[3,128,512]{2,1,0:T(8,128)(2,1)S(1)}, u32[]{:S(2)}, u32[]{:S(2)}) collective-permute-start(bf16[3,128,512]{2,1,0:T(8,128)(2,1)S(1)} %choose.28.refs_3_), channel_id=1, source_target_pairs={{0,4},{1,5},{2,6},{3,7},{4,0},{5,1},{6,2},{7,3},{8,12},{9,13},{10,... | collective-permute-start | bytes 1179656 | tf_op jit(solution)/shard_map/ppermute | solution.py:310
  98.8 3.2 %weight_grads.6 = (f32[1024,2048]{1,0:T(8,128)}, f32[1024,2048]{1,0:T(8,128)}, f32[2048,1024]{1,0:T(8,128)}, f32[8,128]{1,0:T(8,128)S(1)}) custom-call(bf16[1024,256]{1,0:T(8,128)(2,1)S(1)} %get-tuple-element.89.refs_0_, bf16[256,1024]{1,0:T(8,128)(2,1)S(1)} %get-tuple-element.64.refs_1_, ...), custom_call_target="tpu_custom_call", output_to_operand_aliasing={{0}: (4, {}), {1}: (5, {}), {2}: (6, {})} | custom-call | flops 805306368 | bytes 6291456 | tf_op jit(solution)/shard_map/weight_grads/pallas_call | solution.py:90
  102.0 2.6 %collective-permute-done.23.refs_1_ = bf16[3,128,512]{2,1,0:T(8,128)(2,1)S(1)} collective-permute-done((bf16[3,128,512]{2,1,0:T(8,128)(2,1)S(1)}, bf16[3,128,512]{2,1,0:T(8,128)(2,1)S(1)}, u32[]{:S(2)}, u32[]{:S(2)}) %collective-permute-start.23) | collective-permute-done | bytes 393248 | tf_op jit(solution)/shard_map/ppermute | solution.py:310
  107.4 3.2 %weight_grads.7 = (f32[1024,2048]{1,0:T(8,128)}, f32[1024,2048]{1,0:T(8,128)}, f32[2048,1024]{1,0:T(8,128)}, f32[8,128]{1,0:T(8,128)}) custom-call(bf16[1024,256]{1,0:T(8,128)(2,1)S(1)} %get-tuple-element.89.refs_0_, bf16[256,1024]{1,0:T(8,128)(2,1)S(1)} %get-tuple-element.64.refs_1_, ...), custom_call_target="tpu_custom_call", output_to_operand_aliasing={{0}: (4, {}), {1}: (5, {}), {2}: (6, {})} | custom-call | flops 805306368 | bytes 6291456 | tf_op jit(solution)/shard_map/weight_grads/pallas_call | solution.py:90
  (106 shorter events, 30.7 us)
Async XLA Ops:
  5.4 12.7 %collective-permute-start.5 = (bf16[3,128,512]{2,1,0:T(8,128)(2,1)S(1)}, bf16[3,128,512]{2,1,0:T(8,128)(2,1)S(1)}, u32[]{:S(2)}, u32[]{:S(2)}) collective-permute-start(bf16[3,128,512]{2,1,0:T(8,128)(2,1)S(1)} %get-tuple-element.65.refs_5_), channel_id=1, source_target_pairs={{0,4},{1,5},{2,6},{3,7},{4,0},{5,1},{6,2},{7,3},{8,12},{9,13},{10,... | collective-permute-start | bytes 1179656 | tf_op jit(solution)/shard_map/ppermute | solution.py:310
  8.3 10.1 %collective-permute-start.2 = (bf16[128,1024]{1,0:T(8,128)(2,1)S(1)}, bf16[128,1024]{1,0:T(8,128)(2,1)S(1)}, u32[]{:S(2)}, u32[]{:S(2)}) collective-permute-start(bf16[128,1024]{1,0:T(8,128)(2,1)S(1)} %get-tuple-element.61.refs_0_), channel_id=1, source_target_pairs={{0,2},{1,3},{2,0},{3,1},{4,6},{5,7},{6,4},{7,5},{8,10},{9,11},{10,... | collective-permute-start | bytes 786440 | tf_op jit(solution)/shard_map/ppermute | solution.py:304
  9.8 12.3 %collective-permute-start.3 = (bf16[128,1024]{1,0:T(8,128)(2,1)S(1)}, bf16[128,1024]{1,0:T(8,128)(2,1)S(1)}, u32[]{:S(2)}, u32[]{:S(2)}) collective-permute-start(bf16[128,1024]{1,0:T(8,128)(2,1)S(1)} %get-tuple-element.62.refs_2_.refs_1_), channel_id=1, source_target_pairs={{0,2},{1,3},{2,0},{3,1},{4,6},{5,7},{6,4},{7,5},{8,10},{9,11},{10,... | collective-permute-start | bytes 786440 | tf_op jit(solution)/shard_map/ppermute | solution.py:304
  12.9 17.4 %collective-permute-start.4 = (bf16[3,128,512]{2,1,0:T(8,128)(2,1)S(1)}, bf16[3,128,512]{2,1,0:T(8,128)(2,1)S(1)}, u32[]{:S(2)}, u32[]{:S(2)}) collective-permute-start(bf16[3,128,512]{2,1,0:T(8,128)(2,1)S(1)} %get-tuple-element.66), channel_id=1, source_target_pairs={{0,4},{1,5},{2,6},{3,7},{4,0},{5,1},{6,2},{7,3},{8,12},{9,13},{10,... | collective-permute-start | bytes 1179656 | tf_op jit(solution)/shard_map/ppermute | solution.py:310
  18.3 12.2 %collective-permute-start.8 = (bf16[3,128,512]{2,1,0:T(8,128)(2,1)S(1)}, bf16[3,128,512]{2,1,0:T(8,128)(2,1)S(1)}, u32[]{:S(2)}, u32[]{:S(2)}) collective-permute-start(bf16[3,128,512]{2,1,0:T(8,128)(2,1)S(1)} %get-tuple-element.69.refs_5_), channel_id=1, source_target_pairs={{0,1},{1,0},{2,3},{3,2},{4,8},{5,9},{6,10},{7,11},{8,4},{9,5},{10,... | collective-permute-start | bytes 1179656 | tf_op jit(solution)/shard_map/ppermute | solution.py:318
  24.8 14.3 %collective-permute-start.7 = (bf16[3,128,512]{2,1,0:T(8,128)(2,1)S(1)}, bf16[3,128,512]{2,1,0:T(8,128)(2,1)S(1)}, u32[]{:S(2)}, u32[]{:S(2)}) collective-permute-start(bf16[3,128,512]{2,1,0:T(8,128)(2,1)S(1)} %get-tuple-element.74), channel_id=1, source_target_pairs={{0,4},{1,5},{2,6},{3,7},{4,0},{5,1},{6,2},{7,3},{8,12},{9,13},{10,... | collective-permute-start | bytes 1179656 | tf_op jit(solution)/shard_map/ppermute | solution.py:310
  30.4 8.9 %collective-permute-start.6 = (bf16[3,128,512]{2,1,0:T(8,128)(2,1)S(1)}, bf16[3,128,512]{2,1,0:T(8,128)(2,1)S(1)}, u32[]{:S(2)}, u32[]{:S(2)}) collective-permute-start(bf16[3,128,512]{2,1,0:T(8,128)(2,1)S(1)} %get-tuple-element.73.refs_2_), channel_id=1, source_target_pairs={{0,1},{1,0},{2,3},{3,2},{4,8},{5,9},{6,10},{7,11},{8,4},{9,5},{10,... | collective-permute-start | bytes 1179656 | tf_op jit(solution)/shard_map/ppermute | solution.py:318
  33.6 13.9 %collective-permute-start.10 = (bf16[3,128,512]{2,1,0:T(8,128)(2,1)S(1)}, bf16[3,128,512]{2,1,0:T(8,128)(2,1)S(1)}, u32[]{:S(2)}, u32[]{:S(2)}) collective-permute-start(bf16[3,128,512]{2,1,0:T(8,128)(2,1)S(1)} %choose.16.refs_1_), channel_id=1, source_target_pairs={{0,4},{1,5},{2,6},{3,7},{4,0},{5,1},{6,2},{7,3},{8,12},{9,13},{10,... | collective-permute-start | bytes 1179656 | tf_op jit(solution)/shard_map/ppermute | solution.py:310
  39.2 8.5 %collective-permute-start.9 = (bf16[3,128,512]{2,1,0:T(8,128)(2,1)S(1)}, bf16[3,128,512]{2,1,0:T(8,128)(2,1)S(1)}, u32[]{:S(2)}, u32[]{:S(2)}) collective-permute-start(bf16[3,128,512]{2,1,0:T(8,128)(2,1)S(1)} %get-tuple-element.78.refs_2_), channel_id=1, source_target_pairs={{0,1},{1,0},{2,3},{3,2},{4,8},{5,9},{6,10},{7,11},{8,4},{9,5},{10,... | collective-permute-start | bytes 1179656 | tf_op jit(solution)/shard_map/ppermute | solution.py:318
  42.4 12.8 %collective-permute-start.12 = (bf16[3,128,512]{2,1,0:T(8,128)(2,1)S(1)}, bf16[3,128,512]{2,1,0:T(8,128)(2,1)S(1)}, u32[]{:S(2)}, u32[]{:S(2)}) collective-permute-start(bf16[3,128,512]{2,1,0:T(8,128)(2,1)S(1)} %choose.17.refs_1_), channel_id=1, source_target_pairs={{0,4},{1,5},{2,6},{3,7},{4,0},{5,1},{6,2},{7,3},{8,12},{9,13},{10,... | collective-permute-start | bytes 1179656 | tf_op jit(solution)/shard_map/ppermute | solution.py:310
  47.6 7.9 %collective-permute-start.14 = (bf16[3,128,512]{2,1,0:T(8,128)(2,1)S(1)}, bf16[3,128,512]{2,1,0:T(8,128)(2,1)S(1)}, u32[]{:S(2)}, u32[]{:S(2)}) collective-permute-start(bf16[3,128,512]{2,1,0:T(8,128)(2,1)S(1)} %get-tuple-element.83.refs_2_), channel_id=1, source_target_pairs={{0,1},{1,0},{2,3},{3,2},{4,8},{5,9},{6,10},{7,11},{8,4},{9,5},{10,... | collective-permute-start | bytes 1179656 | tf_op jit(solution)/shard_map/ppermute | solution.py:318
  47.9 15.8 %collective-permute-start.11 = (bf16[3,128,512]{2,1,0:T(8,128)(2,1)S(1)}, bf16[3,128,512]{2,1,0:T(8,128)(2,1)S(1)}, u32[]{:S(2)}, u32[]{:S(2)}) collective-permute-start(bf16[3,128,512]{2,1,0:T(8,128)(2,1)S(1)} %choose.18.refs_3_), channel_id=1, source_target_pairs={{0,4},{1,5},{2,6},{3,7},{4,0},{5,1},{6,2},{7,3},{8,12},{9,13},{10,... | collective-permute-start | bytes 1179656 | tf_op jit(solution)/shard_map/ppermute | solution.py:310
  55.4 8.5 %collective-permute-start.13 = (bf16[3,128,512]{2,1,0:T(8,128)(2,1)S(1)}, bf16[3,128,512]{2,1,0:T(8,128)(2,1)S(1)}, u32[]{:S(2)}, u32[]{:S(2)}) collective-permute-start(bf16[3,128,512]{2,1,0:T(8,128)(2,1)S(1)} %get-tuple-element.85.refs_2_), channel_id=1, source_target_pairs={{0,1},{1,0},{2,3},{3,2},{4,8},{5,9},{6,10},{7,11},{8,4},{9,5},{10,... | collective-permute-start | bytes 1179656 | tf_op jit(solution)/shard_map/ppermute | solution.py:318
  55.7 18.6 %collective-permute-start.15 = (bf16[3,128,512]{2,1,0:T(8,128)(2,1)S(1)}, bf16[3,128,512]{2,1,0:T(8,128)(2,1)S(1)}, u32[]{:S(2)}, u32[]{:S(2)}) collective-permute-start(bf16[3,128,512]{2,1,0:T(8,128)(2,1)S(1)} %choose.20.refs_3_), channel_id=1, source_target_pairs={{0,4},{1,5},{2,6},{3,7},{4,0},{5,1},{6,2},{7,3},{8,12},{9,13},{10,... | collective-permute-start | bytes 1179656 | tf_op jit(solution)/shard_map/ppermute | solution.py:310
  63.8 10.7 %collective-permute-start.16 = (bf16[3,128,512]{2,1,0:T(8,128)(2,1)S(1)}, bf16[3,128,512]{2,1,0:T(8,128)(2,1)S(1)}, u32[]{:S(2)}, u32[]{:S(2)}) collective-permute-start(bf16[3,128,512]{2,1,0:T(8,128)(2,1)S(1)} %get-tuple-element.87.refs_2_), channel_id=1, source_target_pairs={{0,1},{1,0},{2,3},{3,2},{4,8},{5,9},{6,10},{7,11},{8,4},{9,5},{10,... | collective-permute-start | bytes 1179656 | tf_op jit(solution)/shard_map/ppermute | solution.py:318
  64.1 18.6 %collective-permute-start.17 = (bf16[3,128,512]{2,1,0:T(8,128)(2,1)S(1)}, bf16[3,128,512]{2,1,0:T(8,128)(2,1)S(1)}, u32[]{:S(2)}, u32[]{:S(2)}) collective-permute-start(bf16[3,128,512]{2,1,0:T(8,128)(2,1)S(1)} %choose.22.refs_3_), channel_id=1, source_target_pairs={{0,4},{1,5},{2,6},{3,7},{4,0},{5,1},{6,2},{7,3},{8,12},{9,13},{10,... | collective-permute-start | bytes 1179656 | tf_op jit(solution)/shard_map/ppermute | solution.py:310
  74.4 8.5 %collective-permute-start.18 = (bf16[3,128,512]{2,1,0:T(8,128)(2,1)S(1)}, bf16[3,128,512]{2,1,0:T(8,128)(2,1)S(1)}, u32[]{:S(2)}, u32[]{:S(2)}) collective-permute-start(bf16[3,128,512]{2,1,0:T(8,128)(2,1)S(1)} %get-tuple-element.91.refs_2_), channel_id=1, source_target_pairs={{0,1},{1,0},{2,3},{3,2},{4,8},{5,9},{6,10},{7,11},{8,4},{9,5},{10,... | collective-permute-start | bytes 1179656 | tf_op jit(solution)/shard_map/ppermute | solution.py:318
  74.8 18.5 %collective-permute-start.19 = (bf16[3,128,512]{2,1,0:T(8,128)(2,1)S(1)}, bf16[3,128,512]{2,1,0:T(8,128)(2,1)S(1)}, u32[]{:S(2)}, u32[]{:S(2)}) collective-permute-start(bf16[3,128,512]{2,1,0:T(8,128)(2,1)S(1)} %choose.24.refs_3_), channel_id=1, source_target_pairs={{0,4},{1,5},{2,6},{3,7},{4,0},{5,1},{6,2},{7,3},{8,12},{9,13},{10,... | collective-permute-start | bytes 1179656 | tf_op jit(solution)/shard_map/ppermute | solution.py:310
  83.2 14.2 %collective-permute-start.22 = (bf16[3,128,512]{2,1,0:T(8,128)(2,1)S(1)}, bf16[3,128,512]{2,1,0:T(8,128)(2,1)S(1)}, u32[]{:S(2)}, u32[]{:S(2)}) collective-permute-start(bf16[3,128,512]{2,1,0:T(8,128)(2,1)S(1)} %choose.26.refs_3_), channel_id=1, source_target_pairs={{0,4},{1,5},{2,6},{3,7},{4,0},{5,1},{6,2},{7,3},{8,12},{9,13},{10,... | collective-permute-start | bytes 1179656 | tf_op jit(solution)/shard_map/ppermute | solution.py:310
  86.7 17.9 %collective-permute-start.23 = (bf16[3,128,512]{2,1,0:T(8,128)(2,1)S(1)}, bf16[3,128,512]{2,1,0:T(8,128)(2,1)S(1)}, u32[]{:S(2)}, u32[]{:S(2)}) collective-permute-start(bf16[3,128,512]{2,1,0:T(8,128)(2,1)S(1)} %choose.28.refs_3_), channel_id=1, source_target_pairs={{0,4},{1,5},{2,6},{3,7},{4,0},{5,1},{6,2},{7,3},{8,12},{9,13},{10,... | collective-permute-start | bytes 1179656 | tf_op jit(solution)/shard_map/ppermute | solution.py:310
  94.1 12.3 %collective-permute-start.21 = (bf16[128,1024]{1,0:T(8,128)(2,1)S(1)}, bf16[128,1024]{1,0:T(8,128)(2,1)S(1)}, u32[]{:S(2)}, u32[]{:S(2)}) collective-permute-start(bf16[128,1024]{1,0:T(8,128)(2,1)S(1)} %get-tuple-element.113), channel_id=1, source_target_pairs={{0,2},{1,3},{2,0},{3,1},{4,6},{5,7},{6,4},{7,5},{8,10},{9,11},{10,... | collective-permute-start | bytes 786440 | tf_op jit(solution)/shard_map/ppermute | solution.py:304
  96.2 9.6 %collective-permute-start.25 = (bf16[128,1024]{1,0:T(8,128)(2,1)S(1)}, bf16[128,1024]{1,0:T(8,128)(2,1)S(1)}, u32[]{:S(2)}, u32[]{:S(2)}) collective-permute-start(bf16[128,1024]{1,0:T(8,128)(2,1)S(1)} %get-tuple-element.115), channel_id=1, source_target_pairs={{0,2},{1,3},{2,0},{3,1},{4,6},{5,7},{6,4},{7,5},{8,10},{9,11},{10,... | collective-permute-start | bytes 786440 | tf_op jit(solution)/shard_map/ppermute | solution.py:304
  106.4 4.2 %collective-permute-start.26 = (f32[64,1024]{1,0:T(8,128)S(1)}, f32[64,1024]{1,0:T(8,128)S(1)}, u32[]{:S(2)}, u32[]{:S(2)}) collective-permute-start(f32[64,1024]{1,0:T(8,128)S(1)} %get-tuple-element.106), channel_id=1, source_target_pairs={{0,1},{1,0},{2,3},{3,2},{4,5},{5,4},{6,7},{7,6},{8,9},{9,8},{10,11... | collective-permute-start | bytes 786440 | tf_op jit(solution)/shard_map/ppermute | solution.py:304
  106.9 4.4 %collective-permute-start.24 = (f32[64,1024]{1,0:T(8,128)S(1)}, f32[64,1024]{1,0:T(8,128)S(1)}, u32[]{:S(2)}, u32[]{:S(2)}) collective-permute-start(f32[64,1024]{1,0:T(8,128)S(1)} %get-tuple-element.104), channel_id=1, source_target_pairs={{0,1},{1,0},{2,3},{3,2},{4,5},{5,4},{6,7},{7,6},{8,9},{9,8},{10,11... | collective-permute-start | bytes 786440 | tf_op jit(solution)/shard_map/ppermute | solution.py:304
  (3 other events, 6.8 us)

commit v4 on v3

--- a/solution.py
+++ b/solution.py
@@ -180,30 +180,59 @@
     )[0]
 
 
-def stage(blocks, behind=()):
-    n = len(blocks)
+def stage(pieces, behind=()):
+    n = len(pieces)
     m = n + len(behind)
+    shapes = [shape for _, shape in pieces]
+    cuts = [max(1, shape[0] // 256) for shape in shapes]
 
     def kernel(*refs):
-        copies = [
-            pltpu.make_async_copy(refs[i], refs[m + i], refs[-1].at[i]) for i in range(n)
-        ]
+        sems = refs[-1]
+        copies = []
+        for i, shape in enumerate(shapes):
+            size = shape[0] // cuts[i]
+            for j in range(cuts[i]):
+                part = pl.ds(j * size, size)
+                copies.append(
+                    pltpu.make_async_copy(
+                        refs[i].at[part, pl.ds(0, shape[1])],
+                        refs[m + i].at[part],
+                        sems.at[len(copies)],
+                    )
+                )
         for copy in copies:
             copy.start()
         for copy in copies:
             copy.wait()
 
-    size = sum(math.prod(b.shape) * 2 for b in blocks)
+    size = sum(math.prod(shape) * 2 for shape in shapes)
     return pl.pallas_call(
         kernel,
         in_specs=[REST] * m,
         out_specs=[HERE] * n,
-        out_shape=[in_vmem(b.shape, b.dtype) for b in blocks],
-        scratch_shapes=[pltpu.SemaphoreType.DMA((n,))],
+        out_shape=[in_vmem(shape, BF) for shape in shapes],
+        scratch_shapes=[pltpu.SemaphoreType.DMA((sum(cuts),))],
         compiler_params=params(4),
         cost_estimate=pl.CostEstimate(flops=size, bytes_accessed=size, transcendentals=0),
         name="stage",
-    )(*[in_hbm(b) for b in blocks], *behind)
+    )(*[in_hbm(values) for values, _ in pieces], *behind)
+
+
+def close(keeps, cames):
+    n = len(keeps)
+
+    def kernel(*refs):
+        for i in range(n):
+            refs[2 * n + i][...] = (refs[i][...] + refs[n + i][...]).astype(BF)
+
+    shape = keeps[0].shape
+    return pl.pallas_call(
+        kernel,
+        in_specs=[HERE] * (2 * n),
+        out_shape=[jax.ShapeDtypeStruct(shape, BF)] * n,
+        compiler_params=params(4),
+        name="close",
+    )(*keeps, *cames)
 
 
 def gather(pairs):
@@ -320,7 +349,12 @@
     is_end = ((down == 0) | (down == side - 1)).astype(jnp.int32)
     flags = (core + 2 * is_end).reshape(1)
 
-    x_mine, c_mine = stage([tokens[0], cotangent[0]])
+    slab = width * PIECES
+    feat = w_gate.shape[0]
+    early = [(w_gate, (feat, slab)), (w_up, (feat, slab)), (w_down, (slab, feat))]
+    x_mine, c_mine, *weights = stage(
+        [(tokens[0], tokens.shape[1:]), (cotangent[0], tokens.shape[1:])] + early
+    )
     x_own, c_own = pair(
         flags,
         [x_mine, swap(tokens[0], 1), c_mine, swap(cotangent[0], 1)],
@@ -331,8 +365,6 @@
     order += [(0, c) for c in range(last, total_chunks)]
     sums, sends = {}, {}
     inputs = {0: (x_own, c_own)}
-
-    weights = [in_hbm(w) for w in (w_gate, w_up, w_down)]
 
     def prepare(gs, chunks, *behind):
         x, c = inputs[gs[0]] if len(gs) == 1 else inputs["all"]
@@ -348,14 +380,11 @@
         return lax.slice_in_dim(values, start, start + 2 * rows, axis=1)
 
     prepare([0], [0])
+    weights = [in_hbm(w) for w in (w_gate, w_up, w_down)]
     for g in range(1, groups):
         inputs[g] = swap(x_own, 2 * g), swap(c_own, 2 * g)
     x_all, c_all, xt_all = gather([inputs[g] for g in range(groups)])
     inputs["all"] = x_all, c_all
-
-    def core_sum(values):
-        send, keep = split(flags, values)
-        return keep + swap(send, 1)
 
     fulls = {}
     received = [None, None]
@@ -416,7 +445,10 @@
             if t == -2:
                 depart(1)
         behind = [last_made]
-        staged = []
+        w_gate, w_up, w_down = weights = stage(
+            [(w, w.shape) for w in (w_gate, w_up, w_down)], behind
+        )
+        behind = [w_gate]
         waiting = None
         ready = []
         for t in range(steps + LAG):
@@ -429,17 +461,18 @@
                 results[t - 1] = finish(*waiting, behind)
                 behind = [results[t - 1]]
             waiting = started
+            later = []
             for gs, chunks in made.get(t, ()):
-                behind = [prepare(gs, list(chunks), *behind)]
+                if t + 2 in [step_of[g, c] for g in gs for c in chunks]:
+                    behind = [prepare(gs, list(chunks), *behind)]
+                else:
+                    later.append((gs, list(chunks)))
             if t + 2 < steps + LAG:
                 load = depart(t + 2, *behind)
                 if t + 2 >= LAG:
                     behind = [load]
-            if t < 3:
-                staged += stage([(w_gate, w_up, w_down)[t]], behind)
-                behind = staged[-1:]
-                if t == 2:
-                    w_gate, w_up, w_down = weights = staged
+            for gs, chunks in later:
+                behind = [prepare(gs, chunks, *behind)]
             if t >= LAG:
                 g, c = order[t - LAG]
                 if c % PIECES == PIECES - 1:
@@ -479,10 +512,10 @@
         for h in range(WIDE):
             weigh(h, [])
 
-    return (
-        tuple(core_sum(received[i] + outs[0][i]).astype(BF)[None] for i in range(2))
-        + tuple(g[None] for g in grads)
-    )
+    halves = [split(flags, received[i] + outs[0][i]) for i in range(2)]
+    cames = [swap(send, 1) for send, _ in halves]
+    ends = close([keep for _, keep in halves], cames)
+    return tuple(end[None] for end in ends) + tuple(g[None] for g in grads)
 
 
 def solution(mesh):

time: 112 us -> 107 us (0.955)
  Pallas kernels: 40.2 us -> 30.9 us
  waiting for transfers between devices: 18 us -> 23.6 us
  other arithmetic: 1.37 us -> 0 us
    pallas_call x6, Pallas kernels: 16.3 us -> 6.97 us  [partials(): pl.pallas_call(kernel, grid=(n,), in_specs=[whole, whole, cols, cols, pl....]
    ppermute x11, waiting for transfers between devices: 13 us -> 20 us  [along(): return lax.ppermute(values, 'row', route)]
    ppermute x8, waiting for transfers between devices: 4.99 us -> 3.53 us  [swap(): return lax.ppermute(values, 'row', [(i, i ^ bits) for i in range(count)])]
    broadcast_in_dim x2 -> x0, other arithmetic: 1.37 us -> none  [body(): core_sum(received[i] + outs[0][i]).astype(BF)[None]]
    pallas_call x4 -> x2, Pallas kernels: 7.57 us -> 6.78 us  [stage(): pl.pallas_call(kernel, in_specs=[REST] * m, out_specs=[HERE] * n, out_sha...]
  transfers between devices with their start and end apart: 27 -> 27, of which waited for: 9 -> 9; matrix products, arithmetic and copies ran while one was open for 10% -> 9% of each run, Pallas kernels for 33% -> 27%
where the time goes in v4:
time: 107 us
  starting transfers between devices  40.9 us (38%)
  Pallas kernels  30.9 us (29%)
  waiting for transfers between devices  23.6 us (22%)
  matrix products  10.3 us (10%)
  between operations  1.3 us (1%)
    ppermute x11, starting transfers between devices, along(): return lax.ppermute(values, 'row', route)  35 us
    ppermute x11, waiting for transfers between devices, along(): return lax.ppermute(values, 'row', route)  20 us
    pallas_call x4, Pallas kernels, weight_grads(): pl.pallas_call(lambda *refs: grads_kernel(n, *refs), grid=(nb,), in_specs...  12.8 us
    dot_general x24, matrix products, mm(): lax.dot_general(left, right, (((ldim,), (rdim,)), ((), ())), preferred_el...  10.3 us
    pallas_call x6, Pallas kernels, partials(): pl.pallas_call(kernel, grid=(n,), in_specs=[whole, whole, cols, cols, pl....  6.97 us
    pallas_call x2, Pallas kernels, stage(): pl.pallas_call(kernel, in_specs=[REST] * m, out_specs=[HERE] * n, out_sha...  6.78 us
    ppermute x8, starting transfers between devices, swap(): return lax.ppermute(values, 'row', [(i, i ^ bits) for i in range(count)])  5.35 us
    pallas_call x36, Pallas kernels, small(): pl.pallas_call(lambda *refs: kernel(*refs[:n], *refs[m:]), in_specs=[FLAG...  3.59 us
  transfers between devices with their start and end apart: 27, of which 9 were waited for; matrix products, arithmetic and copies ran while one was open for 9% of the time, Pallas kernels for 27%

profile of v4, /device:TPU:0, one launch (start us, length us, event | category | flops | bytes accessed | tf_op | source)
XLA Modules:
  0.0 106.9 jit_solution(13224866723057199359)
XLA Ops:
  1.2 2.1 %stage.2 = (bf16[64,1024]{1,0:T(8,128)(2,1)S(1)}, bf16[64,1024]{1,0:T(8,128)(2,1)S(1)}, bf16[1024,512]{1,0:T(8,128)(2,1)S(1)}, bf16[1024,512]{1,0:T(8,128)(2,1)S(1)}, bf16[512,1024]{1,0:T(8,128)(2,1)S(1)}) custom-call(bf16[64,1024]{1,0:T(8,128)(2,1)} %bitcast.104, bf16[64,1024]{1,0:T(8,128)(2,1)} %bitcast.106, bf16[1024,2048]{1,0:T(8,128)(2,1)} %bitcast.94, ...), custom_call_target="tpu_custom_call" | custom-call | flops 3407872 | bytes 3407872 | tf_op jit(solution)/shard_map/stage/pallas_call | solution.py:209
  4.2 3.1 %collective-permute-start.4 = (bf16[3,128,512]{2,1,0:T(8,128)(2,1)S(1)}, bf16[3,128,512]{2,1,0:T(8,128)(2,1)S(1)}, u32[]{:S(2)}, u32[]{:S(2)}) collective-permute-start(bf16[3,128,512]{2,1,0:T(8,128)(2,1)S(1)} %get-tuple-element.76.refs_5_), channel_id=1, source_target_pairs={{0,4},{1,5},{2,6},{3,7},{4,0},{5,1},{6,2},{7,3},{8,12},{9,13},{10,... | collective-permute-start | bytes 1179656 | tf_op jit(solution)/shard_map/ppermute | solution.py:339
  9.3 2.6 %partials.7 = (f32[3,128,512]{2,1,0:T(8,128)S(1)}, bf16[3,128,512]{2,1,0:T(8,128)(2,1)S(1)}) custom-call(bf16[128,1024]{1,0:T(8,128)(2,1)S(1)} %get-tuple-element.69.refs_0_, bf16[128,1024]{1,0:T(8,128)(2,1)S(1)} %get-tuple-element.70.refs_2_.refs_1_, bf16[1024,2048]{1,0:T(8,128)(2,1)} %bitcast.95, bf16[1024,2048]{1,0:T(8,128)(2,1)} %bitcast.98, ...), custom_call_target="tpu_custom_call" | custom-call | flops 402653184 | bytes 3145728 | tf_op jit(solution)/shard_map/partials/pallas_call | solution.py:53
  12.1 4.7 %stage.3 = (bf16[1024,2048]{1,0:T(8,128)(2,1)S(1)}, bf16[1024,2048]{1,0:T(8,128)(2,1)S(1)}, bf16[2048,1024]{1,0:T(8,128)(2,1)S(1)}) custom-call(bf16[1024,2048]{1,0:T(8,128)(2,1)} %bitcast.96, bf16[1024,2048]{1,0:T(8,128)(2,1)} %bitcast.99, bf16[2048,1024]{1,0:T(8,128)(2,1)} %bitcast.102, f32[3,128,512]{2,1,0:T(8,128)S(1)} %get-tuple-element.77.refs_3_.refs_1_), custom_call_target="tpu_custom_call" | custom-call | flops 12582912 | bytes 12582912 | tf_op jit(solution)/shard_map/stage/pallas_call | solution.py:209
  17.4 3.5 %collective-permute-done.3.refs_3_.refs_1_ = bf16[128,1024]{1,0:T(8,128)(2,1)S(1)} collective-permute-done((bf16[128,1024]{1,0:T(8,128)(2,1)S(1)}, bf16[128,1024]{1,0:T(8,128)(2,1)S(1)}, u32[]{:S(2)}, u32[]{:S(2)}) %collective-permute-start.3) | collective-permute-done | bytes 262176 | tf_op jit(solution)/shard_map/ppermute | solution.py:333
  23.1 2.5 %collective-permute-done.6.refs_0_ = bf16[3,128,512]{2,1,0:T(8,128)(2,1)S(1)} collective-permute-done((bf16[3,128,512]{2,1,0:T(8,128)(2,1)S(1)}, bf16[3,128,512]{2,1,0:T(8,128)(2,1)S(1)}, u32[]{:S(2)}, u32[]{:S(2)}) %collective-permute-start.6) | collective-permute-done | bytes 393248 | tf_op jit(solution)/shard_map/ppermute | solution.py:339
  26.1 3.7 %collective-permute-start.10 = (bf16[3,128,512]{2,1,0:T(8,128)(2,1)S(1)}, bf16[3,128,512]{2,1,0:T(8,128)(2,1)S(1)}, u32[]{:S(2)}, u32[]{:S(2)}) collective-permute-start(bf16[3,128,512]{2,1,0:T(8,128)(2,1)S(1)} %choose.16.refs_5_), channel_id=1, source_target_pairs={{0,4},{1,5},{2,6},{3,7},{4,0},{5,1},{6,2},{7,3},{8,12},{9,13},{10,... | collective-permute-start | bytes 1179656 | tf_op jit(solution)/shard_map/ppermute | solution.py:339
  30.7 3.3 %collective-permute-done.8.refs_0_ = bf16[3,128,512]{2,1,0:T(8,128)(2,1)S(1)} collective-permute-done((bf16[3,128,512]{2,1,0:T(8,128)(2,1)S(1)}, bf16[3,128,512]{2,1,0:T(8,128)(2,1)S(1)}, u32[]{:S(2)}, u32[]{:S(2)}) %collective-permute-start.8) | collective-permute-done | bytes 393248 | tf_op jit(solution)/shard_map/ppermute | solution.py:339
  34.5 3.7 %collective-permute-start.12 = (bf16[3,128,512]{2,1,0:T(8,128)(2,1)S(1)}, bf16[3,128,512]{2,1,0:T(8,128)(2,1)S(1)}, u32[]{:S(2)}, u32[]{:S(2)}) collective-permute-start(bf16[3,128,512]{2,1,0:T(8,128)(2,1)S(1)} %choose.17.refs_5_), channel_id=1, source_target_pairs={{0,4},{1,5},{2,6},{3,7},{4,0},{5,1},{6,2},{7,3},{8,12},{9,13},{10,... | collective-permute-start | bytes 1179656 | tf_op jit(solution)/shard_map/ppermute | solution.py:339
  39.2 3.3 %collective-permute-done.10.refs_0_.refs_1_ = bf16[3,128,512]{2,1,0:T(8,128)(2,1)S(1)} collective-permute-done((bf16[3,128,512]{2,1,0:T(8,128)(2,1)S(1)}, bf16[3,128,512]{2,1,0:T(8,128)(2,1)S(1)}, u32[]{:S(2)}, u32[]{:S(2)}) %collective-permute-start.10) | collective-permute-done | bytes 393248 | tf_op jit(solution)/shard_map/ppermute | solution.py:339
  42.9 3.7 %collective-permute-start.11 = (bf16[3,128,512]{2,1,0:T(8,128)(2,1)S(1)}, bf16[3,128,512]{2,1,0:T(8,128)(2,1)S(1)}, u32[]{:S(2)}, u32[]{:S(2)}) collective-permute-start(bf16[3,128,512]{2,1,0:T(8,128)(2,1)S(1)} %choose.18.refs_3_), channel_id=1, source_target_pairs={{0,4},{1,5},{2,6},{3,7},{4,0},{5,1},{6,2},{7,3},{8,12},{9,13},{10,... | collective-permute-start | bytes 1179656 | tf_op jit(solution)/shard_map/ppermute | solution.py:339
  47.9 3.0 %collective-permute-done.12.refs_0_.refs_1_ = bf16[3,128,512]{2,1,0:T(8,128)(2,1)S(1)} collective-permute-done((bf16[3,128,512]{2,1,0:T(8,128)(2,1)S(1)}, bf16[3,128,512]{2,1,0:T(8,128)(2,1)S(1)}, u32[]{:S(2)}, u32[]{:S(2)}) %collective-permute-start.12) | collective-permute-done | bytes 393248 | tf_op jit(solution)/shard_map/ppermute | solution.py:339
  51.4 3.7 %collective-permute-start.15 = (bf16[3,128,512]{2,1,0:T(8,128)(2,1)S(1)}, bf16[3,128,512]{2,1,0:T(8,128)(2,1)S(1)}, u32[]{:S(2)}, u32[]{:S(2)}) collective-permute-start(bf16[3,128,512]{2,1,0:T(8,128)(2,1)S(1)} %choose.20.refs_3_), channel_id=1, source_target_pairs={{0,4},{1,5},{2,6},{3,7},{4,0},{5,1},{6,2},{7,3},{8,12},{9,13},{10,... | collective-permute-start | bytes 1179656 | tf_op jit(solution)/shard_map/ppermute | solution.py:339
  56.4 2.9 %collective-permute-done.11.refs_0_.refs_1_ = bf16[3,128,512]{2,1,0:T(8,128)(2,1)S(1)} collective-permute-done((bf16[3,128,512]{2,1,0:T(8,128)(2,1)S(1)}, bf16[3,128,512]{2,1,0:T(8,128)(2,1)S(1)}, u32[]{:S(2)}, u32[]{:S(2)}) %collective-permute-start.11) | collective-permute-done | bytes 393248 | tf_op jit(solution)/shard_map/ppermute | solution.py:339
  59.8 3.7 %collective-permute-start.17 = (bf16[3,128,512]{2,1,0:T(8,128)(2,1)S(1)}, bf16[3,128,512]{2,1,0:T(8,128)(2,1)S(1)}, u32[]{:S(2)}, u32[]{:S(2)}) collective-permute-start(bf16[3,128,512]{2,1,0:T(8,128)(2,1)S(1)} %choose.22.refs_3_), channel_id=1, source_target_pairs={{0,4},{1,5},{2,6},{3,7},{4,0},{5,1},{6,2},{7,3},{8,12},{9,13},{10,... | collective-permute-start | bytes 1179656 | tf_op jit(solution)/shard_map/ppermute | solution.py:339
  64.8 3.2 %weight_grads.4 = (f32[1024,2048]{1,0:T(8,128)}, f32[1024,2048]{1,0:T(8,128)}, f32[2048,1024]{1,0:T(8,128)}, f32[8,128]{1,0:T(8,128)S(1)}) custom-call(bf16[1024,256]{1,0:T(8,128)(2,1)S(1)} %get-tuple-element.103.refs_0_, bf16[256,1024]{1,0:T(8,128)(2,1)S(1)} %get-tuple-element.72.refs_1_, bf16[3,128,512]{2,1,0:T(8,128)(2,1)S(1)} %choose.19.refs_2_, ...), custom_call_target="tpu_custom_call" | custom-call | flops 805306368 | bytes 6291456 | tf_op jit(solution)/shard_map/weight_grads/pallas_call | solution.py:90
  68.5 3.4 %collective-permute-start.19 = (bf16[3,128,512]{2,1,0:T(8,128)(2,1)S(1)}, bf16[3,128,512]{2,1,0:T(8,128)(2,1)S(1)}, u32[]{:S(2)}, u32[]{:S(2)}) collective-permute-start(bf16[3,128,512]{2,1,0:T(8,128)(2,1)S(1)} %choose.24.refs_3_), channel_id=1, source_target_pairs={{0,4},{1,5},{2,6},{3,7},{4,0},{5,1},{6,2},{7,3},{8,12},{9,13},{10,... | collective-permute-start | bytes 1179656 | tf_op jit(solution)/shard_map/ppermute | solution.py:339
  73.5 3.2 %weight_grads.5 = (f32[1024,2048]{1,0:T(8,128)}, f32[1024,2048]{1,0:T(8,128)}, f32[2048,1024]{1,0:T(8,128)}, f32[8,128]{1,0:T(8,128)S(1)}) custom-call(bf16[1024,256]{1,0:T(8,128)(2,1)S(1)} %get-tuple-element.103.refs_0_, bf16[256,1024]{1,0:T(8,128)(2,1)S(1)} %get-tuple-element.72.refs_1_, ...), custom_call_target="tpu_custom_call", output_to_operand_aliasing={{0}: (4, {}), {1}: (5, {}), {2}: (6, {})} | custom-call | flops 805306368 | bytes 6291456 | tf_op jit(solution)/shard_map/weight_grads/pallas_call | solution.py:90
  77.1 3.2 %collective-permute-start.22 = (bf16[3,128,512]{2,1,0:T(8,128)(2,1)S(1)}, bf16[3,128,512]{2,1,0:T(8,128)(2,1)S(1)}, u32[]{:S(2)}, u32[]{:S(2)}) collective-permute-start(bf16[3,128,512]{2,1,0:T(8,128)(2,1)S(1)} %choose.26.refs_3_), channel_id=1, source_target_pairs={{0,4},{1,5},{2,6},{3,7},{4,0},{5,1},{6,2},{7,3},{8,12},{9,13},{10,... | collective-permute-start | bytes 1179656 | tf_op jit(solution)/shard_map/ppermute | solution.py:339
  81.9 6.3 %collective-permute-start.23 = (bf16[3,128,512]{2,1,0:T(8,128)(2,1)S(1)}, bf16[3,128,512]{2,1,0:T(8,128)(2,1)S(1)}, u32[]{:S(2)}, u32[]{:S(2)}) collective-permute-start(bf16[3,128,512]{2,1,0:T(8,128)(2,1)S(1)} %choose.28.refs_3_), channel_id=1, source_target_pairs={{0,4},{1,5},{2,6},{3,7},{4,0},{5,1},{6,2},{7,3},{8,12},{9,13},{10,... | collective-permute-start | bytes 1179656 | tf_op jit(solution)/shard_map/ppermute | solution.py:339
  89.1 1.6 %collective-permute-start.21 = (bf16[128,1024]{1,0:T(8,128)(2,1)S(1)}, bf16[128,1024]{1,0:T(8,128)(2,1)S(1)}, u32[]{:S(2)}, u32[]{:S(2)}) collective-permute-start(bf16[128,1024]{1,0:T(8,128)(2,1)S(1)} %get-tuple-element.129), channel_id=1, source_target_pairs={{0,2},{1,3},{2,0},{3,1},{4,6},{5,7},{6,4},{7,5},{8,10},{9,11},{10,... | collective-permute-start | bytes 786440 | tf_op jit(solution)/shard_map/ppermute | solution.py:333
  94.4 3.2 %weight_grads.6 = (f32[1024,2048]{1,0:T(8,128)}, f32[1024,2048]{1,0:T(8,128)}, f32[2048,1024]{1,0:T(8,128)}, f32[8,128]{1,0:T(8,128)S(1)}) custom-call(bf16[1024,256]{1,0:T(8,128)(2,1)S(1)} %get-tuple-element.103.refs_0_, bf16[256,1024]{1,0:T(8,128)(2,1)S(1)} %get-tuple-element.72.refs_1_, ...), custom_call_target="tpu_custom_call", output_to_operand_aliasing={{0}: (4, {}), {1}: (5, {}), {2}: (6, {})} | custom-call | flops 805306368 | bytes 6291456 | tf_op jit(solution)/shard_map/weight_grads/pallas_call | solution.py:90
  97.6 3.3 %collective-permute-done.23.refs_1_ = bf16[3,128,512]{2,1,0:T(8,128)(2,1)S(1)} collective-permute-done((bf16[3,128,512]{2,1,0:T(8,128)(2,1)S(1)}, bf16[3,128,512]{2,1,0:T(8,128)(2,1)S(1)}, u32[]{:S(2)}, u32[]{:S(2)}) %collective-permute-start.23) | collective-permute-done | bytes 393248 | tf_op jit(solution)/shard_map/ppermute | solution.py:339
  103.0 3.2 %weight_grads.7 = (f32[1024,2048]{1,0:T(8,128)}, f32[1024,2048]{1,0:T(8,128)}, f32[2048,1024]{1,0:T(8,128)}, f32[8,128]{1,0:T(8,128)}) custom-call(bf16[1024,256]{1,0:T(8,128)(2,1)S(1)} %get-tuple-element.103.refs_0_, bf16[256,1024]{1,0:T(8,128)(2,1)S(1)} %get-tuple-element.72.refs_1_, ...), custom_call_target="tpu_custom_call", output_to_operand_aliasing={{0}: (4, {}), {1}: (5, {}), {2}: (6, {})} | custom-call | flops 805306368 | bytes 6291456 | tf_op jit(solution)/shard_map/weight_grads/pallas_call | solution.py:90
  (103 shorter events, 25.6 us)
Async XLA Ops:
  4.2 13.0 %collective-permute-start.4 = (bf16[3,128,512]{2,1,0:T(8,128)(2,1)S(1)}, bf16[3,128,512]{2,1,0:T(8,128)(2,1)S(1)}, u32[]{:S(2)}, u32[]{:S(2)}) collective-permute-start(bf16[3,128,512]{2,1,0:T(8,128)(2,1)S(1)} %get-tuple-element.76.refs_5_), channel_id=1, source_target_pairs={{0,4},{1,5},{2,6},{3,7},{4,0},{5,1},{6,2},{7,3},{8,12},{9,13},{10,... | collective-permute-start | bytes 1179656 | tf_op jit(solution)/shard_map/ppermute | solution.py:339
  7.3 10.1 %collective-permute-start.2 = (bf16[128,1024]{1,0:T(8,128)(2,1)S(1)}, bf16[128,1024]{1,0:T(8,128)(2,1)S(1)}, u32[]{:S(2)}, u32[]{:S(2)}) collective-permute-start(bf16[128,1024]{1,0:T(8,128)(2,1)S(1)} %get-tuple-element.69.refs_0_), channel_id=1, source_target_pairs={{0,2},{1,3},{2,0},{3,1},{4,6},{5,7},{6,4},{7,5},{8,10},{9,11},{10,... | collective-permute-start | bytes 786440 | tf_op jit(solution)/shard_map/ppermute | solution.py:333
  8.8 12.1 %collective-permute-start.3 = (bf16[128,1024]{1,0:T(8,128)(2,1)S(1)}, bf16[128,1024]{1,0:T(8,128)(2,1)S(1)}, u32[]{:S(2)}, u32[]{:S(2)}) collective-permute-start(bf16[128,1024]{1,0:T(8,128)(2,1)S(1)} %get-tuple-element.70.refs_2_.refs_1_), channel_id=1, source_target_pairs={{0,2},{1,3},{2,0},{3,1},{4,6},{5,7},{6,4},{7,5},{8,10},{9,11},{10,... | collective-permute-start | bytes 786440 | tf_op jit(solution)/shard_map/ppermute | solution.py:333
  12.0 13.7 %collective-permute-start.6 = (bf16[3,128,512]{2,1,0:T(8,128)(2,1)S(1)}, bf16[3,128,512]{2,1,0:T(8,128)(2,1)S(1)}, u32[]{:S(2)}, u32[]{:S(2)}) collective-permute-start(bf16[3,128,512]{2,1,0:T(8,128)(2,1)S(1)} %get-tuple-element.86), channel_id=1, source_target_pairs={{0,4},{1,5},{2,6},{3,7},{4,0},{5,1},{6,2},{7,3},{8,12},{9,13},{10,... | collective-permute-start | bytes 1179656 | tf_op jit(solution)/shard_map/ppermute | solution.py:339
  17.3 8.5 %collective-permute-start.5 = (bf16[3,128,512]{2,1,0:T(8,128)(2,1)S(1)}, bf16[3,128,512]{2,1,0:T(8,128)(2,1)S(1)}, u32[]{:S(2)}, u32[]{:S(2)}) collective-permute-start(bf16[3,128,512]{2,1,0:T(8,128)(2,1)S(1)} %get-tuple-element.82.refs_5_), channel_id=1, source_target_pairs={{0,1},{1,0},{2,3},{3,2},{4,8},{5,9},{6,10},{7,11},{8,4},{9,5},{10,... | collective-permute-start | bytes 1179656 | tf_op jit(solution)/shard_map/ppermute | solution.py:347
  21.7 12.4 %collective-permute-start.8 = (bf16[3,128,512]{2,1,0:T(8,128)(2,1)S(1)}, bf16[3,128,512]{2,1,0:T(8,128)(2,1)S(1)}, u32[]{:S(2)}, u32[]{:S(2)}) collective-permute-start(bf16[3,128,512]{2,1,0:T(8,128)(2,1)S(1)} %get-tuple-element.91), channel_id=1, source_target_pairs={{0,4},{1,5},{2,6},{3,7},{4,0},{5,1},{6,2},{7,3},{8,12},{9,13},{10,... | collective-permute-start | bytes 1179656 | tf_op jit(solution)/shard_map/ppermute | solution.py:339
  25.7 8.5 %collective-permute-start.7 = (bf16[3,128,512]{2,1,0:T(8,128)(2,1)S(1)}, bf16[3,128,512]{2,1,0:T(8,128)(2,1)S(1)}, u32[]{:S(2)}, u32[]{:S(2)}) collective-permute-start(bf16[3,128,512]{2,1,0:T(8,128)(2,1)S(1)} %get-tuple-element.88.refs_2_), channel_id=1, source_target_pairs={{0,1},{1,0},{2,3},{3,2},{4,8},{5,9},{6,10},{7,11},{8,4},{9,5},{10,... | collective-permute-start | bytes 1179656 | tf_op jit(solution)/shard_map/ppermute | solution.py:347
  26.1 16.4 %collective-permute-start.10 = (bf16[3,128,512]{2,1,0:T(8,128)(2,1)S(1)}, bf16[3,128,512]{2,1,0:T(8,128)(2,1)S(1)}, u32[]{:S(2)}, u32[]{:S(2)}) collective-permute-start(bf16[3,128,512]{2,1,0:T(8,128)(2,1)S(1)} %choose.16.refs_5_), channel_id=1, source_target_pairs={{0,4},{1,5},{2,6},{3,7},{4,0},{5,1},{6,2},{7,3},{8,12},{9,13},{10,... | collective-permute-start | bytes 1179656 | tf_op jit(solution)/shard_map/ppermute | solution.py:339
  34.2 8.5 %collective-permute-start.9 = (bf16[3,128,512]{2,1,0:T(8,128)(2,1)S(1)}, bf16[3,128,512]{2,1,0:T(8,128)(2,1)S(1)}, u32[]{:S(2)}, u32[]{:S(2)}) collective-permute-start(bf16[3,128,512]{2,1,0:T(8,128)(2,1)S(1)} %get-tuple-element.93.refs_2_), channel_id=1, source_target_pairs={{0,1},{1,0},{2,3},{3,2},{4,8},{5,9},{6,10},{7,11},{8,4},{9,5},{10,... | collective-permute-start | bytes 1179656 | tf_op jit(solution)/shard_map/ppermute | solution.py:347
  34.5 16.4 %collective-permute-start.12 = (bf16[3,128,512]{2,1,0:T(8,128)(2,1)S(1)}, bf16[3,128,512]{2,1,0:T(8,128)(2,1)S(1)}, u32[]{:S(2)}, u32[]{:S(2)}) collective-permute-start(bf16[3,128,512]{2,1,0:T(8,128)(2,1)S(1)} %choose.17.refs_5_), channel_id=1, source_target_pairs={{0,4},{1,5},{2,6},{3,7},{4,0},{5,1},{6,2},{7,3},{8,12},{9,13},{10,... | collective-permute-start | bytes 1179656 | tf_op jit(solution)/shard_map/ppermute | solution.py:339
  42.6 8.5 %collective-permute-start.14 = (bf16[3,128,512]{2,1,0:T(8,128)(2,1)S(1)}, bf16[3,128,512]{2,1,0:T(8,128)(2,1)S(1)}, u32[]{:S(2)}, u32[]{:S(2)}) collective-permute-start(bf16[3,128,512]{2,1,0:T(8,128)(2,1)S(1)} %get-tuple-element.97.refs_2_), channel_id=1, source_target_pairs={{0,1},{1,0},{2,3},{3,2},{4,8},{5,9},{6,10},{7,11},{8,4},{9,5},{10,... | collective-permute-start | bytes 1179656 | tf_op jit(solution)/shard_map/ppermute | solution.py:347
  42.9 16.4 %collective-permute-start.11 = (bf16[3,128,512]{2,1,0:T(8,128)(2,1)S(1)}, bf16[3,128,512]{2,1,0:T(8,128)(2,1)S(1)}, u32[]{:S(2)}, u32[]{:S(2)}) collective-permute-start(bf16[3,128,512]{2,1,0:T(8,128)(2,1)S(1)} %choose.18.refs_3_), channel_id=1, source_target_pairs={{0,4},{1,5},{2,6},{3,7},{4,0},{5,1},{6,2},{7,3},{8,12},{9,13},{10,... | collective-permute-start | bytes 1179656 | tf_op jit(solution)/shard_map/ppermute | solution.py:339
  51.0 8.5 %collective-permute-start.13 = (bf16[3,128,512]{2,1,0:T(8,128)(2,1)S(1)}, bf16[3,128,512]{2,1,0:T(8,128)(2,1)S(1)}, u32[]{:S(2)}, u32[]{:S(2)}) collective-permute-start(bf16[3,128,512]{2,1,0:T(8,128)(2,1)S(1)} %get-tuple-element.99.refs_2_), channel_id=1, source_target_pairs={{0,1},{1,0},{2,3},{3,2},{4,8},{5,9},{6,10},{7,11},{8,4},{9,5},{10,... | collective-permute-start | bytes 1179656 | tf_op jit(solution)/shard_map/ppermute | solution.py:347
  51.4 16.6 %collective-permute-start.15 = (bf16[3,128,512]{2,1,0:T(8,128)(2,1)S(1)}, bf16[3,128,512]{2,1,0:T(8,128)(2,1)S(1)}, u32[]{:S(2)}, u32[]{:S(2)}) collective-permute-start(bf16[3,128,512]{2,1,0:T(8,128)(2,1)S(1)} %choose.20.refs_3_), channel_id=1, source_target_pairs={{0,4},{1,5},{2,6},{3,7},{4,0},{5,1},{6,2},{7,3},{8,12},{9,13},{10,... | collective-permute-start | bytes 1179656 | tf_op jit(solution)/shard_map/ppermute | solution.py:339
  59.4 8.8 %collective-permute-start.16 = (bf16[3,128,512]{2,1,0:T(8,128)(2,1)S(1)}, bf16[3,128,512]{2,1,0:T(8,128)(2,1)S(1)}, u32[]{:S(2)}, u32[]{:S(2)}) collective-permute-start(bf16[3,128,512]{2,1,0:T(8,128)(2,1)S(1)} %get-tuple-element.101.refs_2_), channel_id=1, source_target_pairs={{0,1},{1,0},{2,3},{3,2},{4,8},{5,9},{6,10},{7,11},{8,4},{9,5},{10,... | collective-permute-start | bytes 1179656 | tf_op jit(solution)/shard_map/ppermute | solution.py:347
  59.8 16.9 %collective-permute-start.17 = (bf16[3,128,512]{2,1,0:T(8,128)(2,1)S(1)}, bf16[3,128,512]{2,1,0:T(8,128)(2,1)S(1)}, u32[]{:S(2)}, u32[]{:S(2)}) collective-permute-start(bf16[3,128,512]{2,1,0:T(8,128)(2,1)S(1)} %choose.22.refs_3_), channel_id=1, source_target_pairs={{0,4},{1,5},{2,6},{3,7},{4,0},{5,1},{6,2},{7,3},{8,12},{9,13},{10,... | collective-permute-start | bytes 1179656 | tf_op jit(solution)/shard_map/ppermute | solution.py:339
  68.1 8.7 %collective-permute-start.18 = (bf16[3,128,512]{2,1,0:T(8,128)(2,1)S(1)}, bf16[3,128,512]{2,1,0:T(8,128)(2,1)S(1)}, u32[]{:S(2)}, u32[]{:S(2)}) collective-permute-start(bf16[3,128,512]{2,1,0:T(8,128)(2,1)S(1)} %get-tuple-element.105.refs_2_), channel_id=1, source_target_pairs={{0,1},{1,0},{2,3},{3,2},{4,8},{5,9},{6,10},{7,11},{8,4},{9,5},{10,... | collective-permute-start | bytes 1179656 | tf_op jit(solution)/shard_map/ppermute | solution.py:347
  68.5 19.8 %collective-permute-start.19 = (bf16[3,128,512]{2,1,0:T(8,128)(2,1)S(1)}, bf16[3,128,512]{2,1,0:T(8,128)(2,1)S(1)}, u32[]{:S(2)}, u32[]{:S(2)}) collective-permute-start(bf16[3,128,512]{2,1,0:T(8,128)(2,1)S(1)} %choose.24.refs_3_), channel_id=1, source_target_pairs={{0,4},{1,5},{2,6},{3,7},{4,0},{5,1},{6,2},{7,3},{8,12},{9,13},{10,... | collective-permute-start | bytes 1179656 | tf_op jit(solution)/shard_map/ppermute | solution.py:339
  76.8 4.9 %collective-permute-start.20 = (bf16[3,128,512]{2,1,0:T(8,128)(2,1)S(1)}, bf16[3,128,512]{2,1,0:T(8,128)(2,1)S(1)}, u32[]{:S(2)}, u32[]{:S(2)}) collective-permute-start(bf16[3,128,512]{2,1,0:T(8,128)(2,1)S(1)} %get-tuple-element.111.refs_2_), channel_id=1, source_target_pairs={{0,1},{1,0},{2,3},{3,2},{4,8},{5,9},{6,10},{7,11},{8,4},{9,5},{10,... | collective-permute-start | bytes 1179656 | tf_op jit(solution)/shard_map/ppermute | solution.py:347
  77.1 15.9 %collective-permute-start.22 = (bf16[3,128,512]{2,1,0:T(8,128)(2,1)S(1)}, bf16[3,128,512]{2,1,0:T(8,128)(2,1)S(1)}, u32[]{:S(2)}, u32[]{:S(2)}) collective-permute-start(bf16[3,128,512]{2,1,0:T(8,128)(2,1)S(1)} %choose.26.refs_3_), channel_id=1, source_target_pairs={{0,4},{1,5},{2,6},{3,7},{4,0},{5,1},{6,2},{7,3},{8,12},{9,13},{10,... | collective-permute-start | bytes 1179656 | tf_op jit(solution)/shard_map/ppermute | solution.py:339
  81.9 19.0 %collective-permute-start.23 = (bf16[3,128,512]{2,1,0:T(8,128)(2,1)S(1)}, bf16[3,128,512]{2,1,0:T(8,128)(2,1)S(1)}, u32[]{:S(2)}, u32[]{:S(2)}) collective-permute-start(bf16[3,128,512]{2,1,0:T(8,128)(2,1)S(1)} %choose.28.refs_3_), channel_id=1, source_target_pairs={{0,4},{1,5},{2,6},{3,7},{4,0},{5,1},{6,2},{7,3},{8,12},{9,13},{10,... | collective-permute-start | bytes 1179656 | tf_op jit(solution)/shard_map/ppermute | solution.py:339
  89.1 12.9 %collective-permute-start.21 = (bf16[128,1024]{1,0:T(8,128)(2,1)S(1)}, bf16[128,1024]{1,0:T(8,128)(2,1)S(1)}, u32[]{:S(2)}, u32[]{:S(2)}) collective-permute-start(bf16[128,1024]{1,0:T(8,128)(2,1)S(1)} %get-tuple-element.129), channel_id=1, source_target_pairs={{0,2},{1,3},{2,0},{3,1},{4,6},{5,7},{6,4},{7,5},{8,10},{9,11},{10,... | collective-permute-start | bytes 786440 | tf_op jit(solution)/shard_map/ppermute | solution.py:333
  91.2 10.3 %collective-permute-start.24 = (bf16[128,1024]{1,0:T(8,128)(2,1)S(1)}, bf16[128,1024]{1,0:T(8,128)(2,1)S(1)}, u32[]{:S(2)}, u32[]{:S(2)}) collective-permute-start(bf16[128,1024]{1,0:T(8,128)(2,1)S(1)} %get-tuple-element.131), channel_id=1, source_target_pairs={{0,2},{1,3},{2,0},{3,1},{4,6},{5,7},{6,4},{7,5},{8,10},{9,11},{10,... | collective-permute-start | bytes 786440 | tf_op jit(solution)/shard_map/ppermute | solution.py:333
  102.4 3.8 %collective-permute-start.26 = (f32[64,1024]{1,0:T(8,128)S(1)}, f32[64,1024]{1,0:T(8,128)S(1)}, u32[]{:S(2)}, u32[]{:S(2)}) collective-permute-start(f32[64,1024]{1,0:T(8,128)S(1)} %get-tuple-element.120), channel_id=1, source_target_pairs={{0,1},{1,0},{2,3},{3,2},{4,5},{5,4},{6,7},{7,6},{8,9},{9,8},{10,11... | collective-permute-start | bytes 786440 | tf_op jit(solution)/shard_map/ppermute | solution.py:333
  (3 other events, 8.6 us)

commit v5 on v4

--- a/solution.py
+++ b/solution.py
@@ -218,21 +218,20 @@
     )(*[in_hbm(values) for values, _ in pieces], *behind)
 
 
-def close(keeps, cames):
-    n = len(keeps)
-
-    def kernel(*refs):
+def close(keep, came):
+    n, rows, feat = keep.shape
+
+    def kernel(keep_ref, came_ref, *refs):
         for i in range(n):
-            refs[2 * n + i][...] = (refs[i][...] + refs[n + i][...]).astype(BF)
-
-    shape = keeps[0].shape
+            refs[i][...] = (keep_ref[i] + came_ref[i]).astype(BF)
+
     return pl.pallas_call(
         kernel,
-        in_specs=[HERE] * (2 * n),
-        out_shape=[jax.ShapeDtypeStruct(shape, BF)] * n,
+        in_specs=[HERE] * 2,
+        out_shape=[jax.ShapeDtypeStruct((rows, feat), BF)] * n,
         compiler_params=params(4),
         name="close",
-    )(*keeps, *cames)
+    )(keep, came)
 
 
 def gather(pairs):
@@ -277,17 +276,20 @@
 
 
 def split(flags, values):
-    rows, feat = values.shape[0] // 2, values.shape[1]
-
-    def kernel(flag_ref, in_ref, send_ref, keep_ref):
+    n = len(values)
+    rows, feat = values[0].shape[0] // 2, values[0].shape[1]
+
+    def kernel(flag_ref, *refs):
+        send_ref, keep_ref = refs[n:]
         for flag in range(2):
 
             @pl.when(flag_ref[0] % 2 == flag)
             def _():
-                keep_ref[...] = in_ref[flag * rows : (flag + 1) * rows]
-                send_ref[...] = in_ref[(1 - flag) * rows : (2 - flag) * rows]
-
-    return small(kernel, "split", [in_vmem((rows, feat), F32)] * 2, [values], [flags])
+                for i in range(n):
+                    keep_ref[i] = refs[i][flag * rows : (flag + 1) * rows]
+                    send_ref[i] = refs[i][(1 - flag) * rows : (2 - flag) * rows]
+
+    return small(kernel, "split", [in_vmem((n, rows, feat), F32)] * 2, values, [flags])
 
 
 def choose(flags, at_end, start, done, behind):
@@ -512,9 +514,8 @@
         for h in range(WIDE):
             weigh(h, [])
 
-    halves = [split(flags, received[i] + outs[0][i]) for i in range(2)]
-    cames = [swap(send, 1) for send, _ in halves]
-    ends = close([keep for _, keep in halves], cames)
+    send, keep = split(flags, [received[i] + outs[0][i] for i in range(2)])
+    ends = close(keep, swap(send, 1))
     return tuple(end[None] for end in ends) + tuple(g[None] for g in grads)
 
 

time: 107 us -> 107 us (level)
    ppermute x8 -> x7, starting transfers between devices: 5.35 us -> 4.85 us  [swap(): return lax.ppermute(values, 'row', [(i, i ^ bits) for i in range(count)])]
    pallas_call x36 -> x35, Pallas kernels: 3.59 us -> 3.67 us  [small(): pl.pallas_call(lambda *refs: kernel(*refs[:n], *refs[m:]), in_specs=[FLAG...]
    ppermute x8 -> x7, waiting for transfers between devices: 3.53 us -> 3.53 us  [swap(): return lax.ppermute(values, 'row', [(i, i ^ bits) for i in range(count)])]
  transfers between devices with their start and end apart: 27 -> 26, of which waited for: 9 -> 9; matrix products, arithmetic and copies ran while one was open for 9% -> 9% of each run, Pallas kernels for 27% -> 28%
where the time goes in v5:
time: 107 us; the launch traced here: 106 us
  starting transfers between devices  40.4 us (38%)
  Pallas kernels  31 us (29%)
  waiting for transfers between devices  23.4 us (22%)
  matrix products  10.3 us (10%)
  between operations  1.28 us (1%)
    ppermute x11, starting transfers between devices, along(): return lax.ppermute(values, 'row', route)  34.9 us
    ppermute x11, waiting for transfers between devices, along(): return lax.ppermute(values, 'row', route)  19.9 us
    pallas_call x4, Pallas kernels, weight_grads(): pl.pallas_call(lambda *refs: grads_kernel(n, *refs), grid=(nb,), in_specs...  12.9 us
    dot_general x24, matrix products, mm(): lax.dot_general(left, right, (((ldim,), (rdim,)), ((), ())), preferred_el...  10.3 us
    pallas_call x6, Pallas kernels, partials(): pl.pallas_call(kernel, grid=(n,), in_specs=[whole, whole, cols, cols, pl....  6.96 us
    pallas_call x2, Pallas kernels, stage(): pl.pallas_call(kernel, in_specs=[REST] * m, out_specs=[HERE] * n, out_sha...  6.78 us
    ppermute x7, starting transfers between devices, swap(): return lax.ppermute(values, 'row', [(i, i ^ bits) for i in range(count)])  4.85 us
    pallas_call x35, Pallas kernels, small(): pl.pallas_call(lambda *refs: kernel(*refs[:n], *refs[m:]), in_specs=[FLAG...  3.67 us
  transfers between devices with their start and end apart: 26, of which 9 were waited for; matrix products, arithmetic and copies ran while one was open for 9% of the time, Pallas kernels for 28%

profile of v5, /device:TPU:0, one launch (start us, length us, event | category | flops | bytes accessed | tf_op | source)
XLA Modules:
  0.0 106.4 jit_solution(2525182667662534234)
XLA Ops:
  1.2 2.1 %stage.2 = (bf16[64,1024]{1,0:T(8,128)(2,1)S(1)}, bf16[64,1024]{1,0:T(8,128)(2,1)S(1)}, bf16[1024,512]{1,0:T(8,128)(2,1)S(1)}, bf16[1024,512]{1,0:T(8,128)(2,1)S(1)}, bf16[512,1024]{1,0:T(8,128)(2,1)S(1)}) custom-call(bf16[64,1024]{1,0:T(8,128)(2,1)} %bitcast.104, bf16[64,1024]{1,0:T(8,128)(2,1)} %bitcast.106, bf16[1024,2048]{1,0:T(8,128)(2,1)} %bitcast.94, ...), custom_call_target="tpu_custom_call" | custom-call | flops 3407872 | bytes 3407872 | tf_op jit(solution)/shard_map/stage/pallas_call | solution.py:209
  4.2 3.1 %collective-permute-start.4 = (bf16[3,128,512]{2,1,0:T(8,128)(2,1)S(1)}, bf16[3,128,512]{2,1,0:T(8,128)(2,1)S(1)}, u32[]{:S(2)}, u32[]{:S(2)}) collective-permute-start(bf16[3,128,512]{2,1,0:T(8,128)(2,1)S(1)} %get-tuple-element.74.refs_5_), channel_id=1, source_target_pairs={{0,4},{1,5},{2,6},{3,7},{4,0},{5,1},{6,2},{7,3},{8,12},{9,13},{10,... | collective-permute-start | bytes 1179656 | tf_op jit(solution)/shard_map/ppermute | solution.py:341
  9.3 2.7 %partials.7 = (f32[3,128,512]{2,1,0:T(8,128)S(1)}, bf16[3,128,512]{2,1,0:T(8,128)(2,1)S(1)}) custom-call(bf16[128,1024]{1,0:T(8,128)(2,1)S(1)} %get-tuple-element.67.refs_0_, bf16[128,1024]{1,0:T(8,128)(2,1)S(1)} %get-tuple-element.68.refs_2_.refs_1_, bf16[1024,2048]{1,0:T(8,128)(2,1)} %bitcast.95, bf16[1024,2048]{1,0:T(8,128)(2,1)} %bitcast.98, ...), custom_call_target="tpu_custom_call" | custom-call | flops 402653184 | bytes 3145728 | tf_op jit(solution)/shard_map/partials/pallas_call | solution.py:53
  12.1 4.7 %stage.3 = (bf16[1024,2048]{1,0:T(8,128)(2,1)S(1)}, bf16[1024,2048]{1,0:T(8,128)(2,1)S(1)}, bf16[2048,1024]{1,0:T(8,128)(2,1)S(1)}) custom-call(bf16[1024,2048]{1,0:T(8,128)(2,1)} %bitcast.96, bf16[1024,2048]{1,0:T(8,128)(2,1)} %bitcast.99, bf16[2048,1024]{1,0:T(8,128)(2,1)} %bitcast.102, f32[3,128,512]{2,1,0:T(8,128)S(1)} %get-tuple-element.75.refs_3_.refs_1_), custom_call_target="tpu_custom_call" | custom-call | flops 12582912 | bytes 12582912 | tf_op jit(solution)/shard_map/stage/pallas_call | solution.py:209
  17.4 3.5 %collective-permute-done.3.refs_3_.refs_1_ = bf16[128,1024]{1,0:T(8,128)(2,1)S(1)} collective-permute-done((bf16[128,1024]{1,0:T(8,128)(2,1)S(1)}, bf16[128,1024]{1,0:T(8,128)(2,1)S(1)}, u32[]{:S(2)}, u32[]{:S(2)}) %collective-permute-start.3) | collective-permute-done | bytes 262176 | tf_op jit(solution)/shard_map/ppermute | solution.py:335
  23.1 2.5 %collective-permute-done.6.refs_0_ = bf16[3,128,512]{2,1,0:T(8,128)(2,1)S(1)} collective-permute-done((bf16[3,128,512]{2,1,0:T(8,128)(2,1)S(1)}, bf16[3,128,512]{2,1,0:T(8,128)(2,1)S(1)}, u32[]{:S(2)}, u32[]{:S(2)}) %collective-permute-start.6) | collective-permute-done | bytes 393248 | tf_op jit(solution)/shard_map/ppermute | solution.py:341
  26.1 3.7 %collective-permute-start.10 = (bf16[3,128,512]{2,1,0:T(8,128)(2,1)S(1)}, bf16[3,128,512]{2,1,0:T(8,128)(2,1)S(1)}, u32[]{:S(2)}, u32[]{:S(2)}) collective-permute-start(bf16[3,128,512]{2,1,0:T(8,128)(2,1)S(1)} %choose.16.refs_5_), channel_id=1, source_target_pairs={{0,4},{1,5},{2,6},{3,7},{4,0},{5,1},{6,2},{7,3},{8,12},{9,13},{10,... | collective-permute-start | bytes 1179656 | tf_op jit(solution)/shard_map/ppermute | solution.py:341
  30.8 3.3 %collective-permute-done.8.refs_0_ = bf16[3,128,512]{2,1,0:T(8,128)(2,1)S(1)} collective-permute-done((bf16[3,128,512]{2,1,0:T(8,128)(2,1)S(1)}, bf16[3,128,512]{2,1,0:T(8,128)(2,1)S(1)}, u32[]{:S(2)}, u32[]{:S(2)}) %collective-permute-start.8) | collective-permute-done | bytes 393248 | tf_op jit(solution)/shard_map/ppermute | solution.py:341
  34.5 3.7 %collective-permute-start.12 = (bf16[3,128,512]{2,1,0:T(8,128)(2,1)S(1)}, bf16[3,128,512]{2,1,0:T(8,128)(2,1)S(1)}, u32[]{:S(2)}, u32[]{:S(2)}) collective-permute-start(bf16[3,128,512]{2,1,0:T(8,128)(2,1)S(1)} %choose.17.refs_5_), channel_id=1, source_target_pairs={{0,4},{1,5},{2,6},{3,7},{4,0},{5,1},{6,2},{7,3},{8,12},{9,13},{10,... | collective-permute-start | bytes 1179656 | tf_op jit(solution)/shard_map/ppermute | solution.py:341
  39.2 3.3 %collective-permute-done.10.refs_0_.refs_1_ = bf16[3,128,512]{2,1,0:T(8,128)(2,1)S(1)} collective-permute-done((bf16[3,128,512]{2,1,0:T(8,128)(2,1)S(1)}, bf16[3,128,512]{2,1,0:T(8,128)(2,1)S(1)}, u32[]{:S(2)}, u32[]{:S(2)}) %collective-permute-start.10) | collective-permute-done | bytes 393248 | tf_op jit(solution)/shard_map/ppermute | solution.py:341
  42.9 3.7 %collective-permute-start.11 = (bf16[3,128,512]{2,1,0:T(8,128)(2,1)S(1)}, bf16[3,128,512]{2,1,0:T(8,128)(2,1)S(1)}, u32[]{:S(2)}, u32[]{:S(2)}) collective-permute-start(bf16[3,128,512]{2,1,0:T(8,128)(2,1)S(1)} %choose.18.refs_3_), channel_id=1, source_target_pairs={{0,4},{1,5},{2,6},{3,7},{4,0},{5,1},{6,2},{7,3},{8,12},{9,13},{10,... | collective-permute-start | bytes 1179656 | tf_op jit(solution)/shard_map/ppermute | solution.py:341
  47.9 3.0 %collective-permute-done.12.refs_0_.refs_1_ = bf16[3,128,512]{2,1,0:T(8,128)(2,1)S(1)} collective-permute-done((bf16[3,128,512]{2,1,0:T(8,128)(2,1)S(1)}, bf16[3,128,512]{2,1,0:T(8,128)(2,1)S(1)}, u32[]{:S(2)}, u32[]{:S(2)}) %collective-permute-start.12) | collective-permute-done | bytes 393248 | tf_op jit(solution)/shard_map/ppermute | solution.py:341
  51.4 3.7 %collective-permute-start.15 = (bf16[3,128,512]{2,1,0:T(8,128)(2,1)S(1)}, bf16[3,128,512]{2,1,0:T(8,128)(2,1)S(1)}, u32[]{:S(2)}, u32[]{:S(2)}) collective-permute-start(bf16[3,128,512]{2,1,0:T(8,128)(2,1)S(1)} %choose.20.refs_3_), channel_id=1, source_target_pairs={{0,4},{1,5},{2,6},{3,7},{4,0},{5,1},{6,2},{7,3},{8,12},{9,13},{10,... | collective-permute-start | bytes 1179656 | tf_op jit(solution)/shard_map/ppermute | solution.py:341
  56.4 2.9 %collective-permute-done.11.refs_0_.refs_1_ = bf16[3,128,512]{2,1,0:T(8,128)(2,1)S(1)} collective-permute-done((bf16[3,128,512]{2,1,0:T(8,128)(2,1)S(1)}, bf16[3,128,512]{2,1,0:T(8,128)(2,1)S(1)}, u32[]{:S(2)}, u32[]{:S(2)}) %collective-permute-start.11) | collective-permute-done | bytes 393248 | tf_op jit(solution)/shard_map/ppermute | solution.py:341
  59.8 3.7 %collective-permute-start.17 = (bf16[3,128,512]{2,1,0:T(8,128)(2,1)S(1)}, bf16[3,128,512]{2,1,0:T(8,128)(2,1)S(1)}, u32[]{:S(2)}, u32[]{:S(2)}) collective-permute-start(bf16[3,128,512]{2,1,0:T(8,128)(2,1)S(1)} %choose.22.refs_3_), channel_id=1, source_target_pairs={{0,4},{1,5},{2,6},{3,7},{4,0},{5,1},{6,2},{7,3},{8,12},{9,13},{10,... | collective-permute-start | bytes 1179656 | tf_op jit(solution)/shard_map/ppermute | solution.py:341
  64.8 3.2 %weight_grads.4 = (f32[1024,2048]{1,0:T(8,128)}, f32[1024,2048]{1,0:T(8,128)}, f32[2048,1024]{1,0:T(8,128)}, f32[8,128]{1,0:T(8,128)S(1)}) custom-call(bf16[1024,256]{1,0:T(8,128)(2,1)S(1)} %get-tuple-element.101.refs_0_, bf16[256,1024]{1,0:T(8,128)(2,1)S(1)} %get-tuple-element.70.refs_1_, bf16[3,128,512]{2,1,0:T(8,128)(2,1)S(1)} %choose.19.refs_2_, ...), custom_call_target="tpu_custom_call" | custom-call | flops 805306368 | bytes 6291456 | tf_op jit(solution)/shard_map/weight_grads/pallas_call | solution.py:90
  68.5 3.4 %collective-permute-start.19 = (bf16[3,128,512]{2,1,0:T(8,128)(2,1)S(1)}, bf16[3,128,512]{2,1,0:T(8,128)(2,1)S(1)}, u32[]{:S(2)}, u32[]{:S(2)}) collective-permute-start(bf16[3,128,512]{2,1,0:T(8,128)(2,1)S(1)} %choose.24.refs_3_), channel_id=1, source_target_pairs={{0,4},{1,5},{2,6},{3,7},{4,0},{5,1},{6,2},{7,3},{8,12},{9,13},{10,... | collective-permute-start | bytes 1179656 | tf_op jit(solution)/shard_map/ppermute | solution.py:341
  73.5 3.2 %weight_grads.5 = (f32[1024,2048]{1,0:T(8,128)}, f32[1024,2048]{1,0:T(8,128)}, f32[2048,1024]{1,0:T(8,128)}, f32[8,128]{1,0:T(8,128)S(1)}) custom-call(bf16[1024,256]{1,0:T(8,128)(2,1)S(1)} %get-tuple-element.101.refs_0_, bf16[256,1024]{1,0:T(8,128)(2,1)S(1)} %get-tuple-element.70.refs_1_, ...), custom_call_target="tpu_custom_call", output_to_operand_aliasing={{0}: (4, {}), {1}: (5, {}), {2}: (6, {})} | custom-call | flops 805306368 | bytes 6291456 | tf_op jit(solution)/shard_map/weight_grads/pallas_call | solution.py:90
  77.2 3.2 %collective-permute-start.22 = (bf16[3,128,512]{2,1,0:T(8,128)(2,1)S(1)}, bf16[3,128,512]{2,1,0:T(8,128)(2,1)S(1)}, u32[]{:S(2)}, u32[]{:S(2)}) collective-permute-start(bf16[3,128,512]{2,1,0:T(8,128)(2,1)S(1)} %choose.26.refs_3_), channel_id=1, source_target_pairs={{0,4},{1,5},{2,6},{3,7},{4,0},{5,1},{6,2},{7,3},{8,12},{9,13},{10,... | collective-permute-start | bytes 1179656 | tf_op jit(solution)/shard_map/ppermute | solution.py:341
  82.0 6.3 %collective-permute-start.23 = (bf16[3,128,512]{2,1,0:T(8,128)(2,1)S(1)}, bf16[3,128,512]{2,1,0:T(8,128)(2,1)S(1)}, u32[]{:S(2)}, u32[]{:S(2)}) collective-permute-start(bf16[3,128,512]{2,1,0:T(8,128)(2,1)S(1)} %choose.28.refs_3_), channel_id=1, source_target_pairs={{0,4},{1,5},{2,6},{3,7},{4,0},{5,1},{6,2},{7,3},{8,12},{9,13},{10,... | collective-permute-start | bytes 1179656 | tf_op jit(solution)/shard_map/ppermute | solution.py:341
  89.1 1.6 %collective-permute-start.21 = (bf16[128,1024]{1,0:T(8,128)(2,1)S(1)}, bf16[128,1024]{1,0:T(8,128)(2,1)S(1)}, u32[]{:S(2)}, u32[]{:S(2)}) collective-permute-start(bf16[128,1024]{1,0:T(8,128)(2,1)S(1)} %get-tuple-element.125), channel_id=1, source_target_pairs={{0,2},{1,3},{2,0},{3,1},{4,6},{5,7},{6,4},{7,5},{8,10},{9,11},{10,... | collective-permute-start | bytes 786440 | tf_op jit(solution)/shard_map/ppermute | solution.py:335
  94.4 3.2 %weight_grads.6 = (f32[1024,2048]{1,0:T(8,128)}, f32[1024,2048]{1,0:T(8,128)}, f32[2048,1024]{1,0:T(8,128)}, f32[8,128]{1,0:T(8,128)S(1)}) custom-call(bf16[1024,256]{1,0:T(8,128)(2,1)S(1)} %get-tuple-element.101.refs_0_, bf16[256,1024]{1,0:T(8,128)(2,1)S(1)} %get-tuple-element.70.refs_1_, ...), custom_call_target="tpu_custom_call", output_to_operand_aliasing={{0}: (4, {}), {1}: (5, {}), {2}: (6, {})} | custom-call | flops 805306368 | bytes 6291456 | tf_op jit(solution)/shard_map/weight_grads/pallas_call | solution.py:90
  97.6 3.3 %collective-permute-done.23.refs_1_ = bf16[3,128,512]{2,1,0:T(8,128)(2,1)S(1)} collective-permute-done((bf16[3,128,512]{2,1,0:T(8,128)(2,1)S(1)}, bf16[3,128,512]{2,1,0:T(8,128)(2,1)S(1)}, u32[]{:S(2)}, u32[]{:S(2)}) %collective-permute-start.23) | collective-permute-done | bytes 393248 | tf_op jit(solution)/shard_map/ppermute | solution.py:341
  102.5 3.2 %weight_grads.7 = (f32[1024,2048]{1,0:T(8,128)}, f32[1024,2048]{1,0:T(8,128)}, f32[2048,1024]{1,0:T(8,128)}, f32[8,128]{1,0:T(8,128)}) custom-call(bf16[1024,256]{1,0:T(8,128)(2,1)S(1)} %get-tuple-element.101.refs_0_, bf16[256,1024]{1,0:T(8,128)(2,1)S(1)} %get-tuple-element.70.refs_1_, ...), custom_call_target="tpu_custom_call", output_to_operand_aliasing={{0}: (4, {}), {1}: (5, {}), {2}: (6, {})} | custom-call | flops 805306368 | bytes 6291456 | tf_op jit(solution)/shard_map/weight_grads/pallas_call | solution.py:90
  (100 shorter events, 25.1 us)
Async XLA Ops:
  4.2 13.0 %collective-permute-start.4 = (bf16[3,128,512]{2,1,0:T(8,128)(2,1)S(1)}, bf16[3,128,512]{2,1,0:T(8,128)(2,1)S(1)}, u32[]{:S(2)}, u32[]{:S(2)}) collective-permute-start(bf16[3,128,512]{2,1,0:T(8,128)(2,1)S(1)} %get-tuple-element.74.refs_5_), channel_id=1, source_target_pairs={{0,4},{1,5},{2,6},{3,7},{4,0},{5,1},{6,2},{7,3},{8,12},{9,13},{10,... | collective-permute-start | bytes 1179656 | tf_op jit(solution)/shard_map/ppermute | solution.py:341
  7.3 10.1 %collective-permute-start.2 = (bf16[128,1024]{1,0:T(8,128)(2,1)S(1)}, bf16[128,1024]{1,0:T(8,128)(2,1)S(1)}, u32[]{:S(2)}, u32[]{:S(2)}) collective-permute-start(bf16[128,1024]{1,0:T(8,128)(2,1)S(1)} %get-tuple-element.67.refs_0_), channel_id=1, source_target_pairs={{0,2},{1,3},{2,0},{3,1},{4,6},{5,7},{6,4},{7,5},{8,10},{9,11},{10,... | collective-permute-start | bytes 786440 | tf_op jit(solution)/shard_map/ppermute | solution.py:335
  8.8 12.1 %collective-permute-start.3 = (bf16[128,1024]{1,0:T(8,128)(2,1)S(1)}, bf16[128,1024]{1,0:T(8,128)(2,1)S(1)}, u32[]{:S(2)}, u32[]{:S(2)}) collective-permute-start(bf16[128,1024]{1,0:T(8,128)(2,1)S(1)} %get-tuple-element.68.refs_2_.refs_1_), channel_id=1, source_target_pairs={{0,2},{1,3},{2,0},{3,1},{4,6},{5,7},{6,4},{7,5},{8,10},{9,11},{10,... | collective-permute-start | bytes 786440 | tf_op jit(solution)/shard_map/ppermute | solution.py:335
  12.0 13.6 %collective-permute-start.6 = (bf16[3,128,512]{2,1,0:T(8,128)(2,1)S(1)}, bf16[3,128,512]{2,1,0:T(8,128)(2,1)S(1)}, u32[]{:S(2)}, u32[]{:S(2)}) collective-permute-start(bf16[3,128,512]{2,1,0:T(8,128)(2,1)S(1)} %get-tuple-element.84), channel_id=1, source_target_pairs={{0,4},{1,5},{2,6},{3,7},{4,0},{5,1},{6,2},{7,3},{8,12},{9,13},{10,... | collective-permute-start | bytes 1179656 | tf_op jit(solution)/shard_map/ppermute | solution.py:341
  17.3 8.5 %collective-permute-start.5 = (bf16[3,128,512]{2,1,0:T(8,128)(2,1)S(1)}, bf16[3,128,512]{2,1,0:T(8,128)(2,1)S(1)}, u32[]{:S(2)}, u32[]{:S(2)}) collective-permute-start(bf16[3,128,512]{2,1,0:T(8,128)(2,1)S(1)} %get-tuple-element.80.refs_5_), channel_id=1, source_target_pairs={{0,1},{1,0},{2,3},{3,2},{4,8},{5,9},{6,10},{7,11},{8,4},{9,5},{10,... | collective-permute-start | bytes 1179656 | tf_op jit(solution)/shard_map/ppermute | solution.py:349
  21.7 12.3 %collective-permute-start.8 = (bf16[3,128,512]{2,1,0:T(8,128)(2,1)S(1)}, bf16[3,128,512]{2,1,0:T(8,128)(2,1)S(1)}, u32[]{:S(2)}, u32[]{:S(2)}) collective-permute-start(bf16[3,128,512]{2,1,0:T(8,128)(2,1)S(1)} %get-tuple-element.89), channel_id=1, source_target_pairs={{0,4},{1,5},{2,6},{3,7},{4,0},{5,1},{6,2},{7,3},{8,12},{9,13},{10,... | collective-permute-start | bytes 1179656 | tf_op jit(solution)/shard_map/ppermute | solution.py:341
  25.8 8.5 %collective-permute-start.7 = (bf16[3,128,512]{2,1,0:T(8,128)(2,1)S(1)}, bf16[3,128,512]{2,1,0:T(8,128)(2,1)S(1)}, u32[]{:S(2)}, u32[]{:S(2)}) collective-permute-start(bf16[3,128,512]{2,1,0:T(8,128)(2,1)S(1)} %get-tuple-element.86.refs_2_), channel_id=1, source_target_pairs={{0,1},{1,0},{2,3},{3,2},{4,8},{5,9},{6,10},{7,11},{8,4},{9,5},{10,... | collective-permute-start | bytes 1179656 | tf_op jit(solution)/shard_map/ppermute | solution.py:349
  26.1 16.4 %collective-permute-start.10 = (bf16[3,128,512]{2,1,0:T(8,128)(2,1)S(1)}, bf16[3,128,512]{2,1,0:T(8,128)(2,1)S(1)}, u32[]{:S(2)}, u32[]{:S(2)}) collective-permute-start(bf16[3,128,512]{2,1,0:T(8,128)(2,1)S(1)} %choose.16.refs_5_), channel_id=1, source_target_pairs={{0,4},{1,5},{2,6},{3,7},{4,0},{5,1},{6,2},{7,3},{8,12},{9,13},{10,... | collective-permute-start | bytes 1179656 | tf_op jit(solution)/shard_map/ppermute | solution.py:341
  34.2 8.5 %collective-permute-start.9 = (bf16[3,128,512]{2,1,0:T(8,128)(2,1)S(1)}, bf16[3,128,512]{2,1,0:T(8,128)(2,1)S(1)}, u32[]{:S(2)}, u32[]{:S(2)}) collective-permute-start(bf16[3,128,512]{2,1,0:T(8,128)(2,1)S(1)} %get-tuple-element.91.refs_2_), channel_id=1, source_target_pairs={{0,1},{1,0},{2,3},{3,2},{4,8},{5,9},{6,10},{7,11},{8,4},{9,5},{10,... | collective-permute-start | bytes 1179656 | tf_op jit(solution)/shard_map/ppermute | solution.py:349
  34.5 16.4 %collective-permute-start.12 = (bf16[3,128,512]{2,1,0:T(8,128)(2,1)S(1)}, bf16[3,128,512]{2,1,0:T(8,128)(2,1)S(1)}, u32[]{:S(2)}, u32[]{:S(2)}) collective-permute-start(bf16[3,128,512]{2,1,0:T(8,128)(2,1)S(1)} %choose.17.refs_5_), channel_id=1, source_target_pairs={{0,4},{1,5},{2,6},{3,7},{4,0},{5,1},{6,2},{7,3},{8,12},{9,13},{10,... | collective-permute-start | bytes 1179656 | tf_op jit(solution)/shard_map/ppermute | solution.py:341
  42.6 8.5 %collective-permute-start.14 = (bf16[3,128,512]{2,1,0:T(8,128)(2,1)S(1)}, bf16[3,128,512]{2,1,0:T(8,128)(2,1)S(1)}, u32[]{:S(2)}, u32[]{:S(2)}) collective-permute-start(bf16[3,128,512]{2,1,0:T(8,128)(2,1)S(1)} %get-tuple-element.95.refs_2_), channel_id=1, source_target_pairs={{0,1},{1,0},{2,3},{3,2},{4,8},{5,9},{6,10},{7,11},{8,4},{9,5},{10,... | collective-permute-start | bytes 1179656 | tf_op jit(solution)/shard_map/ppermute | solution.py:349
  42.9 16.4 %collective-permute-start.11 = (bf16[3,128,512]{2,1,0:T(8,128)(2,1)S(1)}, bf16[3,128,512]{2,1,0:T(8,128)(2,1)S(1)}, u32[]{:S(2)}, u32[]{:S(2)}) collective-permute-start(bf16[3,128,512]{2,1,0:T(8,128)(2,1)S(1)} %choose.18.refs_3_), channel_id=1, source_target_pairs={{0,4},{1,5},{2,6},{3,7},{4,0},{5,1},{6,2},{7,3},{8,12},{9,13},{10,... | collective-permute-start | bytes 1179656 | tf_op jit(solution)/shard_map/ppermute | solution.py:341
  51.0 8.5 %collective-permute-start.13 = (bf16[3,128,512]{2,1,0:T(8,128)(2,1)S(1)}, bf16[3,128,512]{2,1,0:T(8,128)(2,1)S(1)}, u32[]{:S(2)}, u32[]{:S(2)}) collective-permute-start(bf16[3,128,512]{2,1,0:T(8,128)(2,1)S(1)} %get-tuple-element.97.refs_2_), channel_id=1, source_target_pairs={{0,1},{1,0},{2,3},{3,2},{4,8},{5,9},{6,10},{7,11},{8,4},{9,5},{10,... | collective-permute-start | bytes 1179656 | tf_op jit(solution)/shard_map/ppermute | solution.py:349
  51.4 16.6 %collective-permute-start.15 = (bf16[3,128,512]{2,1,0:T(8,128)(2,1)S(1)}, bf16[3,128,512]{2,1,0:T(8,128)(2,1)S(1)}, u32[]{:S(2)}, u32[]{:S(2)}) collective-permute-start(bf16[3,128,512]{2,1,0:T(8,128)(2,1)S(1)} %choose.20.refs_3_), channel_id=1, source_target_pairs={{0,4},{1,5},{2,6},{3,7},{4,0},{5,1},{6,2},{7,3},{8,12},{9,13},{10,... | collective-permute-start | bytes 1179656 | tf_op jit(solution)/shard_map/ppermute | solution.py:341
  59.4 8.8 %collective-permute-start.16 = (bf16[3,128,512]{2,1,0:T(8,128)(2,1)S(1)}, bf16[3,128,512]{2,1,0:T(8,128)(2,1)S(1)}, u32[]{:S(2)}, u32[]{:S(2)}) collective-permute-start(bf16[3,128,512]{2,1,0:T(8,128)(2,1)S(1)} %get-tuple-element.99.refs_2_), channel_id=1, source_target_pairs={{0,1},{1,0},{2,3},{3,2},{4,8},{5,9},{6,10},{7,11},{8,4},{9,5},{10,... | collective-permute-start | bytes 1179656 | tf_op jit(solution)/shard_map/ppermute | solution.py:349
  59.8 16.9 %collective-permute-start.17 = (bf16[3,128,512]{2,1,0:T(8,128)(2,1)S(1)}, bf16[3,128,512]{2,1,0:T(8,128)(2,1)S(1)}, u32[]{:S(2)}, u32[]{:S(2)}) collective-permute-start(bf16[3,128,512]{2,1,0:T(8,128)(2,1)S(1)} %choose.22.refs_3_), channel_id=1, source_target_pairs={{0,4},{1,5},{2,6},{3,7},{4,0},{5,1},{6,2},{7,3},{8,12},{9,13},{10,... | collective-permute-start | bytes 1179656 | tf_op jit(solution)/shard_map/ppermute | solution.py:341
  68.2 8.7 %collective-permute-start.18 = (bf16[3,128,512]{2,1,0:T(8,128)(2,1)S(1)}, bf16[3,128,512]{2,1,0:T(8,128)(2,1)S(1)}, u32[]{:S(2)}, u32[]{:S(2)}) collective-permute-start(bf16[3,128,512]{2,1,0:T(8,128)(2,1)S(1)} %get-tuple-element.103.refs_2_), channel_id=1, source_target_pairs={{0,1},{1,0},{2,3},{3,2},{4,8},{5,9},{6,10},{7,11},{8,4},{9,5},{10,... | collective-permute-start | bytes 1179656 | tf_op jit(solution)/shard_map/ppermute | solution.py:349
  68.5 19.8 %collective-permute-start.19 = (bf16[3,128,512]{2,1,0:T(8,128)(2,1)S(1)}, bf16[3,128,512]{2,1,0:T(8,128)(2,1)S(1)}, u32[]{:S(2)}, u32[]{:S(2)}) collective-permute-start(bf16[3,128,512]{2,1,0:T(8,128)(2,1)S(1)} %choose.24.refs_3_), channel_id=1, source_target_pairs={{0,4},{1,5},{2,6},{3,7},{4,0},{5,1},{6,2},{7,3},{8,12},{9,13},{10,... | collective-permute-start | bytes 1179656 | tf_op jit(solution)/shard_map/ppermute | solution.py:341
  76.8 4.9 %collective-permute-start.20 = (bf16[3,128,512]{2,1,0:T(8,128)(2,1)S(1)}, bf16[3,128,512]{2,1,0:T(8,128)(2,1)S(1)}, u32[]{:S(2)}, u32[]{:S(2)}) collective-permute-start(bf16[3,128,512]{2,1,0:T(8,128)(2,1)S(1)} %get-tuple-element.109.refs_2_), channel_id=1, source_target_pairs={{0,1},{1,0},{2,3},{3,2},{4,8},{5,9},{6,10},{7,11},{8,4},{9,5},{10,... | collective-permute-start | bytes 1179656 | tf_op jit(solution)/shard_map/ppermute | solution.py:349
  77.2 15.9 %collective-permute-start.22 = (bf16[3,128,512]{2,1,0:T(8,128)(2,1)S(1)}, bf16[3,128,512]{2,1,0:T(8,128)(2,1)S(1)}, u32[]{:S(2)}, u32[]{:S(2)}) collective-permute-start(bf16[3,128,512]{2,1,0:T(8,128)(2,1)S(1)} %choose.26.refs_3_), channel_id=1, source_target_pairs={{0,4},{1,5},{2,6},{3,7},{4,0},{5,1},{6,2},{7,3},{8,12},{9,13},{10,... | collective-permute-start | bytes 1179656 | tf_op jit(solution)/shard_map/ppermute | solution.py:341
  82.0 18.9 %collective-permute-start.23 = (bf16[3,128,512]{2,1,0:T(8,128)(2,1)S(1)}, bf16[3,128,512]{2,1,0:T(8,128)(2,1)S(1)}, u32[]{:S(2)}, u32[]{:S(2)}) collective-permute-start(bf16[3,128,512]{2,1,0:T(8,128)(2,1)S(1)} %choose.28.refs_3_), channel_id=1, source_target_pairs={{0,4},{1,5},{2,6},{3,7},{4,0},{5,1},{6,2},{7,3},{8,12},{9,13},{10,... | collective-permute-start | bytes 1179656 | tf_op jit(solution)/shard_map/ppermute | solution.py:341
  89.1 11.8 %collective-permute-start.21 = (bf16[128,1024]{1,0:T(8,128)(2,1)S(1)}, bf16[128,1024]{1,0:T(8,128)(2,1)S(1)}, u32[]{:S(2)}, u32[]{:S(2)}) collective-permute-start(bf16[128,1024]{1,0:T(8,128)(2,1)S(1)} %get-tuple-element.125), channel_id=1, source_target_pairs={{0,2},{1,3},{2,0},{3,1},{4,6},{5,7},{6,4},{7,5},{8,10},{9,11},{10,... | collective-permute-start | bytes 786440 | tf_op jit(solution)/shard_map/ppermute | solution.py:335
  91.2 10.6 %collective-permute-start.24 = (bf16[128,1024]{1,0:T(8,128)(2,1)S(1)}, bf16[128,1024]{1,0:T(8,128)(2,1)S(1)}, u32[]{:S(2)}, u32[]{:S(2)}) collective-permute-start(bf16[128,1024]{1,0:T(8,128)(2,1)S(1)} %get-tuple-element.127), channel_id=1, source_target_pairs={{0,2},{1,3},{2,0},{3,1},{4,6},{5,7},{6,4},{7,5},{8,10},{9,11},{10,... | collective-permute-start | bytes 786440 | tf_op jit(solution)/shard_map/ppermute | solution.py:335
  102.4 3.3 %collective-permute-start.25 = (f32[2,64,1024]{2,1,0:T(8,128)S(1)}, f32[2,64,1024]{2,1,0:T(8,128)S(1)}, u32[]{:S(2)}, u32[]{:S(2)}) collective-permute-start(f32[2,64,1024]{2,1,0:T(8,128)S(1)} %get-tuple-element.116), channel_id=1, source_target_pairs={{0,1},{1,0},{2,3},{3,2},{4,5},{5,4},{6,7},{7,6},{8,9},{9,8},{10,11... | collective-permute-start | bytes 1572872 | tf_op jit(solution)/shard_map/ppermute | solution.py:335
  (2 other events, 4.9 us)
